TPU v7x, 32 devices: a whole 2x2x4 slice. The times are simulated.
32 devices in a mesh: replica: 8 (over z, core), fsdp: 4 (over y, x).
Axes of the slice: x: 2, y: 2, z: 4, core: 2. Of those that a mesh axis runs over, the one named last changes fastest.
Arguments:
- tokens: bfloat16 [50432, 512], P(('replica', 'fsdp')), may hold values from -8 to 8
- cotangent: bfloat16 [50432, 512], P(('replica', 'fsdp')), may hold values from -6 to 6
- routes: int32 [50432, 2], P(('replica', 'fsdp')), may hold values from 0 to 31, all different within a row
- attn_norm: bfloat16 [2, 512], P(None, 'fsdp'), may hold values from 0.5 to 1.5
- query_w: bfloat16 [2, 512, 512], P(None, 'fsdp'), may hold values from -0.375 to 0.375
- key_w: bfloat16 [2, 512, 512], P(None, 'fsdp'), may hold values from -0.375 to 0.375
- value_w: bfloat16 [2, 512, 512], P(None, 'fsdp'), may hold values from -0.25 to 0.25
- output_w: bfloat16 [2, 512, 512], P(None, 'fsdp'), may hold values from -0.75 to 0.75
- ffn_norm: bfloat16 [2, 512], P(None, 'fsdp'), may hold values from 0.5 to 1.5
- mlp_in: bfloat16 [512, 2048], P('fsdp'), may hold values from -0.25 to 0.25
- mlp_out: bfloat16 [2048, 512], P('fsdp'), may hold values from -0.1875 to 0.1875
- router_w: bfloat16 [512, 32], P('fsdp'), may hold values from -0.1875 to 0.1875
- expert_in: bfloat16 [32, 512, 2048], P('fsdp'), may hold values from -0.25 to 0.25
- expert_out: bfloat16 [32, 2048, 512], P('fsdp'), may hold values from -3 to 3
- updated_query: float32 [2, 512, 512], P(None, 'fsdp'), may hold values from -0.25 to 0.25
- updated_key: float32 [2, 512, 512], P(None, 'fsdp'), may hold values from -0.25 to 0.25
- clip_threshold: float32 [2, 8], replicated, may hold values from 1.5 to 4
Outputs:
- block_output: float32 [50432, 512], P(('replica', 'fsdp'))
- tokens_grad: float32 [50432, 512], P(('replica', 'fsdp'))
- attn_norm_grad: float32 [2, 512], P(None, 'fsdp')
- query_grad: float32 [2, 512, 512], P(None, 'fsdp')
- key_grad: float32 [2, 512, 512], P(None, 'fsdp')
- value_grad: float32 [2, 512, 512], P(None, 'fsdp')
- output_grad: float32 [2, 512, 512], P(None, 'fsdp')
- ffn_norm_grad: float32 [2, 512], P(None, 'fsdp')
- mlp_in_grad: float32 [512, 2048], P('fsdp')
- mlp_out_grad: float32 [2048, 512], P('fsdp')
- router_grad: float32 [512, 32], P('fsdp')
- expert_in_grad: float32 [32, 512, 2048], P('fsdp')
- expert_out_grad: float32 [32, 2048, 512], P('fsdp')
- clipped_query: float32 [2, 512, 512], P(None, 'fsdp')
- clipped_key: float32 [2, 512, 512], P(None, 'fsdp')
Inputs may be any that keep to these rules, and one draw needn't show every extreme that they name: `routes`: each token names 2 different experts.
All inputs are finite; a program needn't handle non-finite values.
Results may differ from a plain program's by a relative error of at most 0.025.
Values may be sent and summed in bfloat16 or wider, within the bound.
A program may use at most 448 MiB of HBM per device.

v0:
```python
from functools import partial

import jax
import jax.numpy as jnp
from jax import lax
from jax.sharding import PartitionSpec as P

D = 512
HEADS = 8
SEQ = 197
CAP = 128


EPSILON = 1e-06
NARROW = jnp.bfloat16
WIDE = jnp.float32


def matmul(former, latter):
    return jnp.dot(former, latter, preferred_element_type=WIDE)


def contract_rows(former, latter):
    return lax.dot_general(former, latter, (((0,), (0,)), ((), ())), preferred_element_type=WIDE)


def contract_cols(former, latter):
    return lax.dot_general(former, latter, (((1,), (1,)), ((), ())), preferred_element_type=WIDE)


def split_heads(matrix, images):
    return matrix.reshape(images, -1, HEADS, matrix.shape[-1] // HEADS)


def norm_forward(values, gain_row):
    centred = values - jnp.mean(values, -1, keepdims=True)
    inverse = lax.rsqrt(jnp.mean(centred * centred, -1, keepdims=True) + EPSILON)
    unit_rows = centred * inverse
    return (unit_rows * gain_row, unit_rows, inverse)


def norm_backward(incoming, unit_rows, inverse, gain_row):
    gain_grad = jnp.sum(incoming * unit_rows, 0)
    scaled = incoming * gain_row
    centred = (
        scaled
        - jnp.mean(scaled, -1, keepdims=True)
        - unit_rows * jnp.mean(scaled * unit_rows, -1, keepdims=True)
    )
    return (inverse * centred, gain_grad)


def gelu_grad(pre_act, incoming):
    ignored, pullback = jax.vjp(partial(jax.nn.gelu, approximate=False), pre_act)
    return pullback(incoming)[0]


def attend_forward(residual, gain_row, query_rows, key_rows, value_rows, output_rows, images):
    normed_wide, unit_rows, inverse = norm_forward(residual, gain_row.astype(WIDE))
    normed = normed_wide.astype(NARROW)
    queries = matmul(normed, query_rows).astype(NARROW)
    keys_low = matmul(normed, key_rows).astype(NARROW)
    values_low = matmul(normed, value_rows).astype(NARROW)
    score_scale = (queries.shape[-1] // HEADS) ** (-0.5)
    scores = (
        jnp.einsum(
            "iqhd,ikhd->ihqk",
            split_heads(queries, images),
            split_heads(keys_low, images),
            preferred_element_type=WIDE,
        )
        * score_scale
    )
    highest = jnp.max(scores, -1, keepdims=True)
    powered = jnp.exp(scores - highest)
    totals = jnp.sum(powered, -1, keepdims=True)
    attn_probs = (powered / totals).astype(NARROW)
    mixed_heads = jnp.einsum(
        "ihqk,ikhd->iqhd", attn_probs, split_heads(values_low, images), preferred_element_type=WIDE
    )
    mixed_heads = mixed_heads.astype(NARROW).reshape(residual.shape)
    attn_out = matmul(mixed_heads, output_rows)
    head_max = jnp.max(highest, axis=(0, 2, 3))
    saved_state = (
        normed,
        unit_rows,
        inverse,
        queries,
        keys_low,
        values_low,
        highest + jnp.log(totals),
        mixed_heads,
    )
    return (residual + attn_out, head_max, saved_state)


def attend_backward(
    incoming, saved_state, gain_row, query_rows, key_rows, value_rows, output_rows, images
):
    normed, unit_rows, inverse, queries, keys_low, values_low, log_totals, mixed_heads = saved_state
    out_grad = incoming.astype(NARROW)
    output_grad = contract_rows(mixed_heads, out_grad)
    mixed_grad = split_heads(contract_cols(out_grad, output_rows).astype(NARROW), images)
    score_scale = (queries.shape[-1] // HEADS) ** (-0.5)
    query_heads = split_heads(queries, images)
    key_heads = split_heads(keys_low, images)
    value_heads = split_heads(values_low, images)
    scores = (
        jnp.einsum("iqhd,ikhd->ihqk", query_heads, key_heads, preferred_element_type=WIDE)
        * score_scale
    )
    softened = jnp.exp(scores - log_totals)
    prob_grad = jnp.einsum("iqhd,ikhd->ihqk", mixed_grad, value_heads, preferred_element_type=WIDE)
    values_grad = jnp.einsum(
        "ihqk,iqhd->ikhd", softened.astype(NARROW), mixed_grad, preferred_element_type=WIDE
    )
    values_grad = values_grad.astype(NARROW).reshape(incoming.shape)
    score_grad = (softened * (prob_grad - jnp.sum(softened * prob_grad, -1, keepdims=True))).astype(
        NARROW
    )
    queries_grad = (
        jnp.einsum("ihqk,ikhd->iqhd", score_grad, key_heads, preferred_element_type=WIDE)
        * score_scale
    )
    queries_grad = queries_grad.astype(NARROW).reshape(incoming.shape)
    keys_grad = (
        jnp.einsum("ihqk,iqhd->ikhd", score_grad, query_heads, preferred_element_type=WIDE)
        * score_scale
    )
    keys_grad = keys_grad.astype(NARROW).reshape(incoming.shape)
    normed_grad = (
        contract_cols(queries_grad, query_rows)
        + contract_cols(keys_grad, key_rows)
        + contract_cols(values_grad, value_rows)
    )
    input_grad, gain_grad = norm_backward(normed_grad, unit_rows, inverse, gain_row.astype(WIDE))
    weight_grads = (
        gain_grad,
        contract_rows(normed, queries_grad),
        contract_rows(normed, keys_grad),
        contract_rows(normed, values_grad),
        output_grad,
    )
    return (incoming + input_grad, weight_grads)


def feed_forward(residual, gain_row, inner_w, outer_w):
    normed_wide, unit_rows, inverse = norm_forward(residual, gain_row.astype(WIDE))
    normed = normed_wide.astype(NARROW)
    pre_act = matmul(normed, inner_w)
    hidden = jax.nn.gelu(pre_act, approximate=False).astype(NARROW)
    return (residual + matmul(hidden, outer_w), (normed, unit_rows, inverse, pre_act, hidden))


def feed_backward(incoming, saved_state, gain_row, inner_w, outer_w):
    normed, unit_rows, inverse, pre_act, hidden = saved_state
    out_grad = incoming.astype(NARROW)
    outer_grad = contract_rows(hidden, out_grad)
    pre_grad = gelu_grad(pre_act, contract_cols(out_grad, outer_w)).astype(NARROW)
    inner_grad = contract_rows(normed, pre_grad)
    input_grad, gain_grad = norm_backward(
        contract_cols(pre_grad, inner_w), unit_rows, inverse, gain_row.astype(WIDE)
    )
    return (incoming + input_grad, gain_grad, inner_grad, outer_grad)


def dense_weights(attn_norm, query_w, key_w, value_w, output_w, ffn_norm, mlp_in, mlp_out):
    return (
        lax.all_gather(attn_norm[0], "fsdp", axis=0, tiled=True),
        lax.all_gather(query_w[0], "fsdp", axis=0, tiled=True),
        lax.all_gather(key_w[0], "fsdp", axis=0, tiled=True),
        lax.all_gather(value_w[0], "fsdp", axis=0, tiled=True),
        lax.all_gather(output_w[0], "fsdp", axis=0, tiled=True),
        lax.all_gather(ffn_norm[0], "fsdp", axis=0, tiled=True),
        lax.all_gather(mlp_in, "fsdp", axis=0, tiled=True),
        lax.all_gather(mlp_out, "fsdp", axis=0, tiled=True),
    )


def expert_block_weights(attn_norm, query_w, key_w, value_w, output_w, ffn_norm, router_w):
    return (
        lax.all_gather(attn_norm[1], "fsdp", axis=0, tiled=True),
        lax.all_gather(query_w[1], "fsdp", axis=0, tiled=True),
        lax.all_gather(key_w[1], "fsdp", axis=0, tiled=True),
        lax.all_gather(value_w[1], "fsdp", axis=0, tiled=True),
        lax.all_gather(output_w[1], "fsdp", axis=0, tiled=True),
        lax.all_gather(ffn_norm[1], "fsdp", axis=0, tiled=True),
        lax.all_gather(router_w, "fsdp", axis=0, tiled=True),
    )


def global_maximum(head_max):
    return lax.pmax(head_max, ("replica", "fsdp"))


def slot_targets(routes, experts_local, groups, capacity):
    experts_total = experts_local * groups
    order = jnp.transpose(routes).reshape(-1)
    expert_ids = jnp.arange(experts_total, dtype=jnp.int32)
    hits = (order[:, None] == expert_ids[None, :]).astype(jnp.int32)
    place = jnp.sum(
        (jnp.cumsum(hits, axis=0, dtype=jnp.int32) - hits) * hits, axis=1, dtype=jnp.int32
    )
    target = (order % experts_local * groups + order // experts_local) * capacity + place
    return jnp.where(place < capacity, target, experts_total * capacity)


def local(
    tokens,
    cotangent,
    routes,
    attn_norm,
    query_w,
    key_w,
    value_w,
    output_w,
    ffn_norm,
    mlp_in,
    mlp_out,
    router_w,
    expert_in,
    expert_out,
    updated_query,
    updated_key,
    clip_threshold,
):
    images = tokens.shape[0] // SEQ
    tokens_here = tokens.shape[0]
    groups = lax.axis_size("fsdp")
    experts_local = expert_in.shape[0]
    experts_total = experts_local * groups
    start_state = tokens.astype(WIDE)
    dense_set = dense_weights(
        attn_norm, query_w, key_w, value_w, output_w, ffn_norm, mlp_in, mlp_out
    )
    after_first_attn, max_zero, saved_zero = attend_forward(
        start_state, dense_set[0], dense_set[1], dense_set[2], dense_set[3], dense_set[4], images
    )
    max_zero = global_maximum(max_zero)
    mid_state, saved_ffn = feed_forward(after_first_attn, dense_set[5], dense_set[6], dense_set[7])
    moe_set = expert_block_weights(attn_norm, query_w, key_w, value_w, output_w, ffn_norm, router_w)
    after_second_attn, max_one, saved_one = attend_forward(
        mid_state, moe_set[0], moe_set[1], moe_set[2], moe_set[3], moe_set[4], images
    )
    max_one = global_maximum(max_one)
    moe_wide, unit_moe, inverse_moe = norm_forward(after_second_attn, moe_set[5].astype(WIDE))
    moe_normed = moe_wide.astype(NARROW)
    logits = matmul(moe_normed, moe_set[6])
    shifted = jnp.exp(logits - jnp.max(logits, -1, keepdims=True))
    router_probs = shifted / jnp.sum(shifted, -1, keepdims=True)
    expert_ids = jnp.arange(experts_total, dtype=jnp.int32)
    first_hit = (routes[:, 0:1] == expert_ids[None, :]).astype(WIDE)
    second_hit = (routes[:, 1:2] == expert_ids[None, :]).astype(WIDE)
    gates_first = jnp.sum(router_probs * first_hit, -1)
    gates_second = jnp.sum(router_probs * second_hit, -1)
    target = slot_targets(routes, experts_local, groups, CAP)
    assign_count = target.shape[0]
    source = jnp.full((experts_total * CAP,), assign_count, jnp.int32)
    source = source.at[target].set(jnp.arange(assign_count, dtype=jnp.int32), mode="drop")
    token_pick = jnp.where(source < assign_count, source % tokens_here, tokens_here)
    pad_row = jnp.zeros((1, D), NARROW)
    sent_rows = jnp.concatenate([moe_normed, pad_row], 0)[token_pick].reshape(
        experts_local, groups, CAP, D
    )
    received = lax.all_to_all(sent_rows, "fsdp", split_axis=1, concat_axis=1, tiled=True)
    slot_rows = received.reshape(experts_local, groups * CAP, D)
    expert_pre = jnp.einsum("erd,edf->erf", slot_rows, expert_in, preferred_element_type=WIDE)
    expert_hidden = jax.nn.gelu(expert_pre, approximate=False).astype(NARROW)
    expert_result = jnp.einsum(
        "erf,efd->erd", expert_hidden, expert_out, preferred_element_type=WIDE
    ).astype(NARROW)
    returned = lax.all_to_all(
        expert_result.reshape(experts_local, groups, CAP, D),
        "fsdp",
        split_axis=1,
        concat_axis=1,
        tiled=True,
    )
    result_table = jnp.concatenate([returned.reshape(experts_total * CAP, D), pad_row], 0)
    picks = target.reshape(2, tokens_here)
    first_pick = result_table[picks[0]].astype(WIDE)
    second_pick = result_table[picks[1]].astype(WIDE)
    block_output = after_second_attn + (
        gates_first[:, None] * first_pick + gates_second[:, None] * second_pick
    )
    maxima = jnp.stack([max_zero, max_one])
    factor = clip_threshold / jnp.maximum(maxima, clip_threshold)
    column_scale = jnp.repeat(jnp.sqrt(factor), updated_query.shape[-1] // HEADS, axis=1)
    clipped_query = updated_query * column_scale[:, None, :]
    clipped_key = updated_key * column_scale[:, None, :]
    moe_back = expert_block_weights(
        attn_norm, query_w, key_w, value_w, output_w, ffn_norm, router_w
    )
    upstream = cotangent.astype(WIDE)
    gate_table = jnp.concatenate([gates_first, gates_second, jnp.zeros((1,), WIDE)])
    grad_table = jnp.concatenate([upstream, jnp.zeros((1, D), WIDE)], 0)
    result_grad = (gate_table[source][:, None] * grad_table[token_pick]).astype(NARROW)
    grad_rows = lax.all_to_all(
        result_grad.reshape(experts_local, groups, CAP, D),
        "fsdp",
        split_axis=1,
        concat_axis=1,
        tiled=True,
    )
    grad_rows = grad_rows.reshape(experts_local, groups * CAP, D)
    expert_out_grad = jnp.einsum(
        "erf,erd->efd", expert_hidden, grad_rows, preferred_element_type=WIDE
    )
    hidden_grad = jnp.einsum("erd,efd->erf", grad_rows, expert_out, preferred_element_type=WIDE)
    pre_grad = gelu_grad(expert_pre, hidden_grad).astype(NARROW)
    expert_in_grad = jnp.einsum("erd,erf->edf", slot_rows, pre_grad, preferred_element_type=WIDE)
    input_slots = jnp.einsum(
        "erf,edf->erd", pre_grad, expert_in, preferred_element_type=WIDE
    ).astype(NARROW)
    back_rows = lax.all_to_all(
        input_slots.reshape(experts_local, groups, CAP, D),
        "fsdp",
        split_axis=1,
        concat_axis=1,
        tiled=True,
    )
    back_table = jnp.concatenate([back_rows.reshape(experts_total * CAP, D), pad_row], 0)
    gate_first_grad = jnp.sum(upstream * first_pick, -1)
    gate_second_grad = jnp.sum(upstream * second_pick, -1)
    prob_grad = gate_first_grad[:, None] * first_hit + gate_second_grad[:, None] * second_hit
    logit_grad = (
        router_probs * (prob_grad - jnp.sum(router_probs * prob_grad, -1, keepdims=True))
    ).astype(NARROW)
    router_grad = contract_rows(moe_normed, logit_grad)
    normed_grad = (
        back_table[picks[0]].astype(WIDE)
        + back_table[picks[1]].astype(WIDE)
        + contract_cols(logit_grad, moe_back[6])
    )
    moe_input_grad, ffn_gain_one = norm_backward(
        normed_grad, unit_moe, inverse_moe, moe_back[5].astype(WIDE)
    )
    second_grad = upstream + moe_input_grad
    mid_grad, attn_one = attend_backward(
        second_grad,
        saved_one,
        moe_back[0],
        moe_back[1],
        moe_back[2],
        moe_back[3],
        moe_back[4],
        images,
    )
    moe_sums = (
        lax.psum_scatter(
            attn_one[0].astype(jnp.bfloat16), "fsdp", scatter_dimension=0, tiled=True
        ).astype(jnp.float32),
        lax.psum_scatter(
            attn_one[1].astype(jnp.bfloat16), "fsdp", scatter_dimension=0, tiled=True
        ).astype(jnp.float32),
        lax.psum_scatter(
            attn_one[2].astype(jnp.bfloat16), "fsdp", scatter_dimension=0, tiled=True
        ).astype(jnp.float32),
        lax.psum_scatter(
            attn_one[3].astype(jnp.bfloat16), "fsdp", scatter_dimension=0, tiled=True
        ).astype(jnp.float32),
        lax.psum_scatter(
            attn_one[4].astype(jnp.bfloat16), "fsdp", scatter_dimension=0, tiled=True
        ).astype(jnp.float32),
        lax.psum_scatter(
            ffn_gain_one.astype(jnp.bfloat16), "fsdp", scatter_dimension=0, tiled=True
        ).astype(jnp.float32),
        lax.psum_scatter(
            router_grad.astype(jnp.bfloat16), "fsdp", scatter_dimension=0, tiled=True
        ).astype(jnp.float32),
    )
    dense_back = dense_weights(
        attn_norm, query_w, key_w, value_w, output_w, ffn_norm, mlp_in, mlp_out
    )
    first_grad, ffn_gain_zero, inner_grad, outer_grad = feed_backward(
        mid_grad, saved_ffn, dense_back[5], dense_back[6], dense_back[7]
    )
    tokens_grad, attn_zero = attend_backward(
        first_grad,
        saved_zero,
        dense_back[0],
        dense_back[1],
        dense_back[2],
        dense_back[3],
        dense_back[4],
        images,
    )
    dense_sums = (
        lax.psum_scatter(
            attn_zero[0].astype(jnp.bfloat16), "fsdp", scatter_dimension=0, tiled=True
        ).astype(jnp.float32),
        lax.psum_scatter(
            attn_zero[1].astype(jnp.bfloat16), "fsdp", scatter_dimension=0, tiled=True
        ).astype(jnp.float32),
        lax.psum_scatter(
            attn_zero[2].astype(jnp.bfloat16), "fsdp", scatter_dimension=0, tiled=True
        ).astype(jnp.float32),
        lax.psum_scatter(
            attn_zero[3].astype(jnp.bfloat16), "fsdp", scatter_dimension=0, tiled=True
        ).astype(jnp.float32),
        lax.psum_scatter(
            attn_zero[4].astype(jnp.bfloat16), "fsdp", scatter_dimension=0, tiled=True
        ).astype(jnp.float32),
        lax.psum_scatter(
            ffn_gain_zero.astype(jnp.bfloat16), "fsdp", scatter_dimension=0, tiled=True
        ).astype(jnp.float32),
        lax.psum_scatter(
            inner_grad.astype(jnp.bfloat16), "fsdp", scatter_dimension=0, tiled=True
        ).astype(jnp.float32),
        lax.psum_scatter(
            outer_grad.astype(jnp.bfloat16), "fsdp", scatter_dimension=0, tiled=True
        ).astype(jnp.float32),
    )
    summed = (
        lax.psum(dense_sums[0].astype(jnp.bfloat16), "replica").astype(jnp.float32),
        lax.psum(dense_sums[1].astype(jnp.bfloat16), "replica").astype(jnp.float32),
        lax.psum(dense_sums[2].astype(jnp.bfloat16), "replica").astype(jnp.float32),
        lax.psum(dense_sums[3].astype(jnp.bfloat16), "replica").astype(jnp.float32),
        lax.psum(dense_sums[4].astype(jnp.bfloat16), "replica").astype(jnp.float32),
        lax.psum(dense_sums[5].astype(jnp.bfloat16), "replica").astype(jnp.float32),
        lax.psum(dense_sums[6].astype(jnp.bfloat16), "replica").astype(jnp.float32),
        lax.psum(dense_sums[7].astype(jnp.bfloat16), "replica").astype(jnp.float32),
        lax.psum(moe_sums[0].astype(jnp.bfloat16), "replica").astype(jnp.float32),
        lax.psum(moe_sums[1].astype(jnp.bfloat16), "replica").astype(jnp.float32),
        lax.psum(moe_sums[2].astype(jnp.bfloat16), "replica").astype(jnp.float32),
        lax.psum(moe_sums[3].astype(jnp.bfloat16), "replica").astype(jnp.float32),
        lax.psum(moe_sums[4].astype(jnp.bfloat16), "replica").astype(jnp.float32),
        lax.psum(moe_sums[5].astype(jnp.bfloat16), "replica").astype(jnp.float32),
        lax.psum(moe_sums[6].astype(jnp.bfloat16), "replica").astype(jnp.float32),
        lax.psum(expert_in_grad.astype(jnp.bfloat16), "replica").astype(jnp.float32),
        lax.psum(expert_out_grad.astype(jnp.bfloat16), "replica").astype(jnp.float32),
    )
    dense_sums = summed[0:8]
    moe_sums = summed[8:15]
    expert_in_total = summed[15]
    expert_out_total = summed[16]
    attn_norm_grad = jnp.stack([dense_sums[0], moe_sums[0]])
    query_grad = jnp.stack([dense_sums[1], moe_sums[1]])
    key_grad = jnp.stack([dense_sums[2], moe_sums[2]])
    value_grad = jnp.stack([dense_sums[3], moe_sums[3]])
    output_grad = jnp.stack([dense_sums[4], moe_sums[4]])
    ffn_norm_grad = jnp.stack([dense_sums[5], moe_sums[5]])
    return (
        block_output,
        tokens_grad,
        attn_norm_grad,
        query_grad,
        key_grad,
        value_grad,
        output_grad,
        ffn_norm_grad,
        dense_sums[6],
        dense_sums[7],
        moe_sums[6],
        expert_in_total,
        expert_out_total,
        clipped_query,
        clipped_key,
    )


def solution(mesh):
    in_specs = (
        P(("replica", "fsdp"), None),
        P(("replica", "fsdp"), None),
        P(("replica", "fsdp"), None),
        P(None, "fsdp"),
        P(None, "fsdp", None),
        P(None, "fsdp", None),
        P(None, "fsdp", None),
        P(None, "fsdp", None),
        P(None, "fsdp"),
        P("fsdp", None),
        P("fsdp", None),
        P("fsdp", None),
        P("fsdp", None, None),
        P("fsdp", None, None),
        P(None, "fsdp", None),
        P(None, "fsdp", None),
        P(),
    )
    out_specs = (
        P(("replica", "fsdp"), None),
        P(("replica", "fsdp"), None),
        P(None, "fsdp"),
        P(None, "fsdp", None),
        P(None, "fsdp", None),
        P(None, "fsdp", None),
        P(None, "fsdp", None),
        P(None, "fsdp"),
        P("fsdp", None),
        P("fsdp", None),
        P("fsdp", None),
        P("fsdp", None, None),
        P("fsdp", None, None),
        P(None, "fsdp", None),
        P(None, "fsdp", None),
    )
    return jax.shard_map(local, mesh=mesh, in_specs=in_specs, out_specs=out_specs, check_vma=False)
```

profile of v0, /device:TPU:0, one launch (start us, length us, event | category | flops | bytes accessed | tf_op | source)
XLA Modules:
  0.0 1930.7 jit_solution(9248122434857054436)
XLA Ops:
  61.0 15.8 scatter_custom_fusion
  232.1 35.2 %multiply_convert_fusion.3 = (bf16[1576,2048]{1,0:T(8,128)(2,1)}, f32[1576,2048]{1,0:T(8,128)}, f32[1576,2048]{1,0:T(8,128)}) fusion(bf16[512,2048]{1,0:T(8,128)(2,1)} %all-gather.15.cloned.1.call-done, f32[1576,512]{1,0:T(8,128)} %copy-done.11, f32[512]{0:T(512)S(1)} %bitcast.248, f32[1576]{0:T(1024)S(1)} %add_rsqrt_fusion.2, ...), kind=kOutput, calls=%fused_computation.44 | convolution fusion | flops 3518136320 | bytes 37615936 | tf_op jit(solution)/shard_map/dot_general | solution.py:20
  338.8 17.3 gather_fusion
  358.8 32.6 %all_to_all.20 = bf16[8,4,128,512]{3,2,0,1:T(8,128)(2,1)S(1)} all-to-all(bf16[8,4,128,512]{3,2,0,1:T(8,128)(2,1)S(1)} %copy.166), channel_id=1, replica_groups=mesh['replica'=8,'fsdp'=4] {'fsdp'}, dimensions={1} | all-to-all | bytes 8388608 | tf_op jit(solution)/shard_map/all_to_all | solution.py:265
  393.9 33.7 %fusion.18 = (u8[512,2048]{1,0:T(8,128)(4,1)S(1)}, u8[512,2048]{1,0:T(8,128)(4,1)S(1)}, f32[8,512,2048]{2,1,0:T(8,128)}) fusion(bf16[8,512,512]{2,1,0:T(8,128)(2,1)} %bitcast.219, bf16[8,512,2048]{2,1,0:T(8,128)(2,1)} %param.29), kind=kOutput, calls=%fused_computation.67 | convolution fusion | flops 8696889344 | bytes 56623104 | tf_op jit(solution)/shard_map/erd,edf->erf/dot_general | solution.py:267
  427.7 77.3 %multiply_convert_fusion = (bf16[8,512,2048]{2,1,0:T(8,128)(2,1)}, f32[8,512,2048]{2,1,0:T(8,128)}) fusion(f32[8,512,2048]{2,1,0:T(8,128)} %get-tuple-element.98, u8[512,2048]{1,0:T(8,128)(4,1)S(1)} %get-tuple-element.16, u8[512,2048]{1,0:T(8,128)(4,1)S(1)} %get-tuple-element.15), kind=kLoop, calls=%fused_computation.16 | loop fusion | flops 587202560 | bytes 85983232 | tf_op jit(solution)/shard_map/convert_element_type | solution.py:268
  505.0 17.4 convolution_convert_fusion.13
  531.5 16.8 gather_fusion.4
  548.3 12.5 all_gather.74
  590.1 23.0 %gather_fusion.3 = f32[4096]{0:T(1024)S(1)} fusion(f32[3153]{0:T(1024)S(1)} %concatenate.17, s32[4096]{0:T(1024)S(1)} %copy-done.113), kind=kCustom, calls=%fused_computation.3 | custom fusion | bytes 49152 | tf_op jit(solution)/shard_map/gather | solution.py:297
  617.0 40.1 %all_to_all.21 = bf16[8,4,128,512]{3,2,0,1:T(8,128)(2,1)S(1)} all-to-all(bf16[8,4,128,512]{3,2,0,1:T(8,128)(2,1)S(1)} %fusion.16), channel_id=1, replica_groups=mesh['replica'=8,'fsdp'=4] {'fsdp'}, dimensions={1} | all-to-all | bytes 8388608 | tf_op jit(solution)/shard_map/all_to_all | solution.py:298
  659.6 35.7 %add_convert_fusion = bf16[8,512,2048]{2,1,0:T(8,128)(2,1)} fusion(f32[8,512,2048]{2,1,0:T(8,128)} %get-tuple-element.64, f32[8,512,2048]{2,1,0:T(8,128)} %get-tuple-element.98, bf16[8,512,512]{2,1,0:T(8,128)(2,1)S(1)} %bitcast.221, bf16[8,2048,512]{2,1,0:T(8,128)(2,1)} %param.30), kind=kOutput, calls=%fused_computation.15 | convolution fusion | flops 8707375104 | bytes 104857600 | tf_op jit(solution)/shard_map/erd,efd->erf/dot_general | solution.py:309
  695.3 16.4 convolution_convert_fusion.12
  722.2 34.9 %all-to-all-done.3 = bf16[8,4,128,512]{3,2,0,1:T(8,128)(2,1)} async-done(((bf16[8,4,128,512]{3,2,0,1:T(8,128)(2,1)}), bf16[8,4,128,512]{3,2,0,1:T(8,128)(2,1)}, u32[]{:S(2)}, u32[]{:S(2)}) %all-to-all-start.3) | async-done | bytes 4194336 | tf_op jit(solution)/shard_map/all_to_all | solution.py:315
  878.1 16.6 add_convert_fusion.1
  1024.9 17.6 convolution_convert_fusion
  1042.5 18.9 convolution_convert_fusion.1
  1071.3 38.2 %reduce-scatter.32.cloned.1.call-done = bf16[512,512]{1,0:T(8,128)(2,1)} async-done(((bf16[2048,512]{1,0:T(8,128)(2,1)}), bf16[512,512]{1,0:T(8,128)(2,1)}) %reduce-scatter.32.cloned.1.call-update) | async-done | bytes 524304 | tf_op jit(solution)/shard_map/reduce_scatter | solution.py:410
  1109.5 38.4 %reduce-scatter.30.cloned.1.call-done = bf16[128,2048]{1,0:T(8,128)(2,1)} async-done(((bf16[512,2048]{1,0:T(8,128)(2,1)}), bf16[128,2048]{1,0:T(8,128)(2,1)}) %reduce-scatter.30.cloned.1.call-update) | async-done | bytes 524304 | tf_op jit(solution)/shard_map/reduce_scatter | solution.py:407
  1149.7 24.7 %reduce-scatter.34.cloned.1.call-done = bf16[128,32]{1,0:T(8,128)(2,1)} async-done(((bf16[512,32]{1,0:T(8,128)(2,1)}), bf16[128,32]{1,0:T(8,128)(2,1)}) %reduce-scatter.34.cloned.1.call-update) | async-done | bytes 8208
  1175.2 40.6 %all-reduce.9 = (f32[1,8]{1,0:T(1,128)S(1)}, f32[1,8]{1,0:T(1,128)S(1)}) all-reduce(f32[1,8]{1,0:T(1,128)S(1)} %bitcast.252, f32[1,8]{1,0:T(1,128)S(1)} %bitcast.253), channel_id=1, replica_groups=mesh['replica'=8,'fsdp'=4] {'replica','fsdp'}, use_global_device_ids=true, to_apply=%region_72.73 | all-reduce | flops 16 | bytes 128 | tf_op jit(solution)/shard_map/pmax | solution.py:193
  1234.7 28.0 %all-reduce.10 = (bf16[1,128]{1,0:T(2,128)(2,1)S(1)}, bf16[1,128]{1,0:T(2,128)(2,1)S(1)}, bf16[1,128]{1,0:T(2,128)(2,1)S(1)}, bf16[1,128]{1,0:T(2,128)(2,1)S(1)}, bf16[128,32]{0,1:T(8,128)(2,1)S(1)}) all-reduce(bf16[1,128]{1,0:T(2,128)(2,1)S(1)} %dynamic-slice_bitcast_fusion.2, ...), channel_id=1, replica_groups=mesh['replica'=8,'fsdp'=4] {'replica'}, use_global_device_ids=true, to_apply=%region_38.39 | all-reduce | flops 4608 | bytes 18432 | tf_op jit(solution)/shard_map/psum | solution.py:423
  1270.3 611.6 %all-reduce.15.cloned.1.call-done = (bf16[1,128,512]{2,1,0:T(8,128)(2,1)}, bf16[1,128,512]{2,1,0:T(8,128)(2,1)}, bf16[1,128,512]{2,1,0:T(8,128)(2,1)}, bf16[1,12...) async-done(((bf16[1,128,512]{2,1,0:T(8,128)(2,1)}, ...) | async-done | bytes 35651600 | tf_op jit(solution)/shard_map/psum | solution.py:424
  1886.3 21.8 %convert_element_type.359 = f32[8,512,2048]{2,1,0:T(8,128)} convert(bf16[8,512,2048]{2,1,0:T(8,128)(2,1)} %get-tuple-element.57) | non-fusion elementwise | flops 8388608 | bytes 50331648 | tf_op jit(solution)/shard_map/convert_element_type | solution.py:430
  (533 shorter events, 648.4 us)
Async XLA Ops:
  7.2 224.8 %all-gather.15.cloned.1.call-start = ((), (), s32[]{:S(2)}) async-start(), calls=%async_computation.15 | async-start | bytes 2621440 | tf_op jit(solution)/shard_map/all_gather | solution.py:175
  8.0 259.4 %all-gather.17.cloned.1.call-start = ((), (), s32[]{:S(2)}) async-start(), calls=%async_computation.16 | async-start | bytes 2621440 | tf_op jit(solution)/shard_map/all_gather | solution.py:176
  37.2 194.9 %copy-start.134 = (f32[1,512]{1,0:T(1,128)}, f32[1,512]{1,0:T(1,128)S(1)}, u32[]{:S(2)}) copy-start(f32[1,512]{1,0:T(1,128)S(1)} %convert_element_type.363) | copy-start | bytes 6148
  45.1 118.5 %copy-start.130 = (f32[1,512]{1,0:T(1,128)}, f32[1,512]{1,0:T(1,128)S(1)}, u32[]{:S(2)}) copy-start(f32[1,512]{1,0:T(1,128)S(1)} %convert_element_type.362) | copy-start | bytes 6148
  46.8 116.8 %copy-start.95 = (f32[1576]{0:T(1024)}, f32[1576]{0:T(1024)S(1)}, u32[]{:S(2)}) copy-start(f32[1576]{0:T(1024)S(1)} %broadcast_multiply_fusion.13) | copy-start | bytes 18916
  47.7 115.9 %copy-start.109 = (f32[1576]{0:T(1024)}, f32[1576]{0:T(1024)S(1)}, u32[]{:S(2)}) copy-start(f32[1576]{0:T(1024)S(1)} %add_rsqrt_fusion.3) | copy-start | bytes 18916
  59.3 74.0 %copy-start.64 = (bf16[1,128,512]{2,1,0:T(8,128)(2,1)S(1)}, bf16[1,128,512]{2,1,0:T(8,128)(2,1)}, u32[]{:S(2)}) copy-start(bf16[1,128,512]{2,1,0:T(8,128)(2,1)} %get-tuple-element.76) | copy-start | bytes 393220
  60.8 103.4 %copy-start.83 = (s32[3152]{0:T(1024)}, s32[3152]{0:T(1024)S(1)}, u32[]{:S(2)}) copy-start(s32[3152]{0:T(1024)S(1)} %fusion.77) | copy-start | bytes 37828
  133.3 93.7 %copy-start.36 = (bf16[1,512,512]{2,1,0:T(8,128)(2,1)}, bf16[1,512,512]{2,1,0:T(8,128)(2,1)S(1)}, u32[]{:S(2)}) copy-start(bf16[1,512,512]{2,1,0:T(8,128)(2,1)S(1)} %all-gather.4) | copy-start | bytes 1572868
  524.7 39.0 %all-to-all-start.1 = ((bf16[8,4,128,512]{3,2,0,1:T(8,128)(2,1)}), bf16[8,4,128,512]{3,2,0,1:T(8,128)(2,1)}, u32[]{:S(2)}, u32[]{:S(2)}) async-start(bf16[8,4,128,512]{3,2,0,1:T(8,128)(2,1)} %copy.168), calls=%async_computation.1 | async-start | bytes 8388608 | tf_op jit(solution)/shard_map/all_to_all | solution.py:272
  563.6 216.6 %copy-start.50 = (f32[1576,32]{0,1:T(8,128)}, f32[1576,32]{0,1:T(8,128)S(1)}, u32[]{:S(2)}) copy-start(f32[1576,32]{0,1:T(8,128)S(1)} %get-tuple-element.100) | copy-start | bytes 605188
  716.4 40.7 %all-to-all-start.3 = ((bf16[8,4,128,512]{3,2,0,1:T(8,128)(2,1)}), bf16[8,4,128,512]{3,2,0,1:T(8,128)(2,1)}, u32[]{:S(2)}, u32[]{:S(2)}) async-start(bf16[8,4,128,512]{3,2,0,1:T(8,128)(2,1)} %copy.173), calls=%async_computation.3 | async-start | bytes 8388608 | tf_op jit(solution)/shard_map/all_to_all | solution.py:315
  721.4 340.0 %reduce-scatter.28.cloned.1.call-start = ((), (), s32[]{:S(2)}) async-start(), calls=%async_computation.24 | async-start | bytes 655360 | tf_op jit(solution)/shard_map/reduce_scatter | solution.py:362
  838.9 222.5 %reduce-scatter.24.cloned.1.call-start = ((), (), s32[]{:S(2)}) async-start(), calls=%async_computation.22 | async-start | bytes 655360 | tf_op jit(solution)/shard_map/reduce_scatter | solution.py:359
  874.1 187.3 %reduce-scatter.16.cloned.1.call-start = ((), (), s32[]{:S(2)}) async-start(), calls=%async_computation.18 | async-start | bytes 655360 | tf_op jit(solution)/shard_map/reduce_scatter | solution.py:353
  906.3 155.2 %reduce-scatter.20.cloned.1.call-start = ((), (), s32[]{:S(2)}) async-start(), calls=%async_computation.20 | async-start | bytes 655360 | tf_op jit(solution)/shard_map/reduce_scatter | solution.py:356
  928.5 133.0 %reduce-scatter.26.cloned.1.call-start = ((), (), s32[]{:S(2)}) async-start(), calls=%async_computation.23 | async-start | bytes 655360 | tf_op jit(solution)/shard_map/reduce_scatter | solution.py:401
  947.8 113.7 %reduce-scatter.22.cloned.1.call-start = ((), (), s32[]{:S(2)}) async-start(), calls=%async_computation.21 | async-start | bytes 655360 | tf_op jit(solution)/shard_map/reduce_scatter | solution.py:398
  963.5 98.0 %reduce-scatter.14.cloned.1.call-start = ((), (), s32[]{:S(2)}) async-start(), calls=%async_computation.17 | async-start | bytes 655360 | tf_op jit(solution)/shard_map/reduce_scatter | solution.py:392
  987.2 84.1 %reduce-scatter.18.cloned.1.call-start = ((), (), s32[]{:S(2)}) async-start(), calls=%async_computation.19 | async-start | bytes 655360 | tf_op jit(solution)/shard_map/reduce_scatter | solution.py:395
  1004.3 105.2 %reduce-scatter.32.cloned.1.call-start = ((), (), s32[]{:S(2)}) async-start(), calls=%async_computation.26 | async-start | bytes 2621440 | tf_op jit(solution)/shard_map/reduce_scatter | solution.py:410
  1013.6 134.2 %reduce-scatter.30.cloned.1.call-start = ((), (), s32[]{:S(2)}) async-start(), calls=%async_computation.25 | async-start | bytes 2621440 | tf_op jit(solution)/shard_map/reduce_scatter | solution.py:407
  1022.1 152.3 %reduce-scatter.34.cloned.1.call-start = ((), (), s32[]{:S(2)}) async-start(), calls=%async_computation.27 | async-start | bytes 163840
  1024.9 857.1 %all-reduce.15.cloned.1.call-start = ((), (), s32[]{:S(2)}) async-start(), calls=%async_computation.28 | async-start | bytes 71303168 | tf_op jit(solution)/shard_map/psum | solution.py:424
  (141 other events, 1860.4 us)
Sparse Core Ops, SparseCore 0:
  9.9 38.0 all-gather.14
  49.8 38.2 all-gather.16
  839.1 23.8 reduce-scatter.27
  874.3 23.9 reduce-scatter.23
  906.4 23.9 reduce-scatter.15
  933.9 24.7 reduce-scatter.19
  961.5 24.7 reduce-scatter.25
  990.0 24.7 reduce-scatter.21
  1018.2 24.7 reduce-scatter.13
  1046.5 24.7 reduce-scatter.17
  1074.3 35.1 reduce-scatter.31
  1112.6 35.2 reduce-scatter.29
  1150.6 23.8 reduce-scatter.33
  1179.8 702.1 all-reduce.14
where the time goes:
time: 1940 us; the launch traced here: 1930 us
  waiting for transfers between devices  759 us (39%)
  matrix products  372 us (19%)
  local copies, waits for them, and re-layouts  301 us (16%)
  blocking collectives  283 us (15%)
  other arithmetic  189 us (10%)
    psum x1, waiting for transfers between devices, local(): lax.psum(moe_sums[1].astype(jnp.bfloat16), 'replica').astype(jnp.float32)  612 us
    convert_element_type x1, other arithmetic, local(): expert_hidden = jax.nn.gelu(expert_pre, approximate=False).astype(NARROW)  77.3 us
    reshape x16, local copies, waits for them, and re-layouts, split_heads(): return matrix.reshape(images, -1, HEADS, matrix.shape[-1] // HEADS)  75.2 us
    dot_general x11, matrix products, matmul(): return jnp.dot(former, latter, preferred_element_type=WIDE)  67.9 us
    dot_general x11, matrix products, contract_cols(): lax.dot_general(former, latter, (((1,), (1,)), ((), ())), preferred_eleme...  49.2 us
    dot_general x11, matrix products, contract_rows(): lax.dot_general(former, latter, (((0,), (0,)), ((), ())), preferred_eleme...  45.5 us
    pmax x1, blocking collectives, global_maximum(): return lax.pmax(head_max, ('replica', 'fsdp'))  40.6 us
    all_to_all x1, blocking collectives, local(): lax.all_to_all(result_grad.reshape(experts_local, groups, CAP, D), 'fsdp'...  40.1 us
  transfers between devices with their start and end apart: 16, of which 6 were waited for; matrix products, arithmetic and copies ran while one was open for 20% of the time, Pallas kernels for 0%

commit v1 on v0

v1 whole, which is shorter than its diff:
```python
from functools import partial

import jax
import jax.numpy as jnp
from jax import lax
from jax.experimental import pallas as pl
from jax.experimental.pallas import tpu as pltpu
from jax.sharding import Mesh
from jax.sharding import PartitionSpec as P

D = 512
HEADS = 8
HEAD = 64
FF = 2048
SEQ = 197
SP = 208
CAP = 128
EXPERTS = 32
EPSILON = 1e-06
SCALE = HEAD ** (-0.5)
LOWEST = -1e30
NARROW = jnp.bfloat16
WIDE = jnp.float32
CORES = 2
MIB = 1 << 20


def nn(a, b):
    return lax.dot_general(a, b, (((1,), (0,)), ((), ())), preferred_element_type=WIDE)


def nt(a, b):
    return lax.dot_general(a, b, (((1,), (1,)), ((), ())), preferred_element_type=WIDE)


def tn(a, b):
    return lax.dot_general(a, b, (((0,), (0,)), ((), ())), preferred_element_type=WIDE)


def norm_parts(values):
    centred = values - jnp.mean(values, -1, keepdims=True)
    inverse = lax.rsqrt(jnp.mean(centred * centred, -1, keepdims=True) + EPSILON)
    return centred * inverse, inverse


def norm_backward(incoming, unit, inverse, gain):
    gain_grad = jnp.sum(incoming * unit, 0, keepdims=True)
    scaled = incoming * gain
    centred = (
        scaled
        - jnp.mean(scaled, -1, keepdims=True)
        - unit * jnp.mean(scaled * unit, -1, keepdims=True)
    )
    return inverse * centred, gain_grad


def normal_parts(x):
    z = jnp.abs(x)
    t = 1.0 / (1.0 + (0.3275911 * 0.7071067811865476) * z)
    bell = jnp.exp(-0.5 * (x * x))
    poly = t * (
        0.5 * 0.254829592
        + t
        * (
            0.5 * -0.284496736
            + t * (0.5 * 1.421413741 + t * (0.5 * -1.453152027 + t * (0.5 * 1.061405429)))
        )
    )
    tail = poly * bell
    return jnp.where(x >= 0, 1.0 - tail, tail), bell


INV_ROOT = 0.3989422804014327


def head_masks(dtype):
    lane = lax.broadcasted_iota(jnp.int32, (1, 2 * HEAD), 1)
    low = (lane < HEAD).astype(dtype)
    return (low, (1 - low.astype(WIDE)).astype(dtype))


def attn_fwd_body(x, gain, w_ref, qkv_ref, mixed_ref, peak_ref, ib):
    unit, _ = norm_parts(x)
    normed = (unit * gain).astype(NARROW)
    q = (nn(normed, w_ref[:, 0:D]).astype(NARROW).astype(WIDE) * SCALE).astype(NARROW)
    k = nn(normed, w_ref[:, D : 2 * D]).astype(NARROW)
    v = nn(normed, w_ref[:, 2 * D : 3 * D]).astype(NARROW)
    masks = head_masks(NARROW)
    cols = lax.broadcasted_iota(jnp.int32, (SP, SP), 1)
    rows = lax.broadcasted_iota(jnp.int32, (SP, 1), 0)
    head_row = lax.broadcasted_iota(jnp.int32, (HEADS, 128), 0)
    mixed_all = []
    for i in range(ib):
        peaks = jnp.full((HEADS, 128), LOWEST, WIDE)
        r = slice(i * SP, (i + 1) * SP)
        pairs = []
        for pair in range(HEADS // 2):
            c = slice(pair * 2 * HEAD, (pair + 1) * 2 * HEAD)
            qp, kp, vp = q[r, c], k[r, c], v[r, c]
            acc = None
            for half in range(2):
                s = nt(qp * masks[half], kp)
                s = jnp.where(cols < SEQ, s, LOWEST)
                top = jnp.max(s, -1, keepdims=True)
                e = jnp.exp(s - top)
                p = (e * (1.0 / jnp.sum(e, -1, keepdims=True))).astype(NARROW)
                part = nn(p, vp * masks[half])
                acc = part if acc is None else acc + part
                peak = jnp.max(jnp.where(rows < SEQ, top, LOWEST), 0, keepdims=True)
                peaks = jnp.where(head_row == pair * 2 + half, peak, peaks)
            pairs.append(acc.astype(NARROW))
        mixed_all.append(jnp.concatenate(pairs, 1))
        peak_ref[i] = peaks
    mixed = jnp.concatenate(mixed_all, 0) if ib > 1 else mixed_all[0]
    qkv_ref[...] = jnp.concatenate([q, k, v], 1).reshape(ib, SP, 3 * D)
    mixed_ref[...] = mixed.reshape(ib, SP, D)
    return x + nn(mixed, w_ref[:, 3 * D : 4 * D])


def dense_attn_kernel(ib, x_ref, g_ref, w_ref, y_ref, qkv_ref, mixed_ref, peak_ref):
    x = x_ref[...].astype(WIDE).reshape(ib * SP, D)
    y = attn_fwd_body(x, g_ref[0:1, :], w_ref, qkv_ref, mixed_ref, peak_ref, ib)
    y_ref[...] = y.reshape(ib, SP, D)


def ffn_kernel(ib, x_ref, g_ref, win_ref, wout_ref, y_ref):
    x = x_ref[...].reshape(ib * SP, D)
    unit, _ = norm_parts(x)
    normed = (unit * g_ref[2:3, :]).astype(NARROW)
    acc = x
    for f in range(FF // 512):
        c = slice(f * 512, (f + 1) * 512)
        pre = nn(normed, win_ref[:, c])
        cdf, _ = normal_parts(pre)
        acc = acc + nn((pre * cdf).astype(NARROW), wout_ref[c, :])
    y_ref[...] = acc.reshape(ib, SP, D)


def expert_attn_kernel(
    ib, x_ref, g_ref, w_ref, wr_ref, y_ref, qkv_ref, mixed_ref, peak_ref, moe_ref, prob_ref
):
    x = x_ref[...].reshape(ib * SP, D)
    y = attn_fwd_body(x, g_ref[1:2, :], w_ref, qkv_ref, mixed_ref, peak_ref, ib)
    y_ref[...] = y.reshape(ib, SP, D)
    unit, _ = norm_parts(y)
    moe = (unit * g_ref[3:4, :]).astype(NARROW)
    moe_ref[...] = moe.reshape(ib, SP, D)
    lane = lax.broadcasted_iota(jnp.int32, (1, 128), 1)
    logits = jnp.where(lane < EXPERTS, nn(moe, wr_ref[...]), LOWEST)
    e = jnp.exp(logits - jnp.max(logits, -1, keepdims=True))
    prob_ref[...] = (e / jnp.sum(e, -1, keepdims=True)).reshape(ib, SP, 128)


def whole(shape):
    return pl.BlockSpec(
        shape, lambda *_: (0,) * len(shape), pipeline_mode=pl.Buffered(buffer_count=1)
    )


def per_image(ib, *tail):
    return pl.BlockSpec((ib, *tail), lambda i, *_: (i,) + (0,) * len(tail))


def sds(shape, dtype):
    return jax.ShapeDtypeStruct(shape, dtype)


def cost(flops, moved):
    return pl.CostEstimate(flops=int(flops), bytes_accessed=int(moved), transcendentals=0)


def params(mib):
    return pltpu.CompilerParams(vmem_limit_bytes=mib * MIB)


def dense_attn(x, gains, w0, images, ib):
    return pl.pallas_call(
        partial(dense_attn_kernel, ib),
        grid=(images // ib,),
        in_specs=[per_image(ib, SP, D), whole(gains.shape), whole(w0.shape)],
        out_specs=[
            per_image(ib, SP, D),
            per_image(ib, SP, 3 * D),
            per_image(ib, SP, D),
            per_image(ib, HEADS, 128),
        ],
        out_shape=[
            sds((images, SP, D), WIDE),
            sds((images, SP, 3 * D), NARROW),
            sds((images, SP, D), NARROW),
            sds((images, HEADS, 128), WIDE),
        ],
        compiler_params=params(48),
        name="dense_attention",
    )(x, gains, w0)


def ffn(x, gains, win, wout, images, ib):
    return pl.pallas_call(
        partial(ffn_kernel, ib),
        grid=(images // ib,),
        in_specs=[per_image(ib, SP, D), whole(gains.shape), whole(win.shape), whole(wout.shape)],
        out_specs=per_image(ib, SP, D),
        out_shape=sds((images, SP, D), WIDE),
        compiler_params=params(48),
        name="feed_forward",
    )(x, gains, win, wout)


def expert_attn(x, gains, w1, wr, images, ib):
    return pl.pallas_call(
        partial(expert_attn_kernel, ib),
        grid=(images // ib,),
        in_specs=[per_image(ib, SP, D), whole(gains.shape), whole(w1.shape), whole(wr.shape)],
        out_specs=[
            per_image(ib, SP, D),
            per_image(ib, SP, 3 * D),
            per_image(ib, SP, D),
            per_image(ib, HEADS, 128),
            per_image(ib, SP, D),
            per_image(ib, SP, 128),
        ],
        out_shape=[
            sds((images, SP, D), WIDE),
            sds((images, SP, 3 * D), NARROW),
            sds((images, SP, D), NARROW),
            sds((images, HEADS, 128), WIDE),
            sds((images, SP, D), NARROW),
            sds((images, SP, 128), WIDE),
        ],
        compiler_params=params(48),
        name="expert_attention",
    )(x, gains, w1, wr)


def places_kernel(order_ref, routes_ref, pos_ref, target_ref):
    tokens = routes_ref.shape[1]
    order = order_ref[:, 0:1]
    chunk = 128
    strict = (
        lax.broadcasted_iota(jnp.int32, (chunk, chunk), 0)
        < lax.broadcasted_iota(jnp.int32, (chunk, chunk), 1)
    ).astype(NARROW)
    slot_row = lax.broadcasted_iota(jnp.int32, (EXPERTS, 1), 0).astype(WIDE) * CAP
    base = jnp.zeros((EXPERTS, 1), WIDE)
    for c in range(tokens // chunk):
        pos_ref[:, c * chunk : (c + 1) * chunk] = jnp.full((EXPERTS, chunk), -1.0, WIDE)
    target_ref[...] = jnp.zeros(target_ref.shape, WIDE)
    for k in range(2):
        for c in range(tokens // chunk):
            s = slice(c * chunk, (c + 1) * chunk)
            hit = (order == routes_ref[k : k + 1, s]).astype(WIDE)
            place = base + nn(hit.astype(NARROW), strict)
            base = base + jnp.sum(hit, -1, keepdims=True)
            pos_ref[:, s] = jnp.where(hit > 0, place, pos_ref[:, s])
            slot = jnp.where(place < CAP, slot_row + place, 2.0 * EXPERTS * CAP)
            found = jnp.sum(hit * slot, 0, keepdims=True)
            real = jnp.sum(hit, 0, keepdims=True)
            target_ref[k : k + 1, s] = jnp.where(real > 0, found, 2.0 * EXPERTS * CAP)


def places(order, routes_rows):
    tokens = routes_rows.shape[1]
    return pl.pallas_call(
        places_kernel,
        in_specs=[pl.BlockSpec(memory_space=pltpu.VMEM)] * 2,
        out_specs=[pl.BlockSpec(memory_space=pltpu.VMEM)] * 2,
        out_shape=[sds((EXPERTS, tokens), WIDE), sds((8, tokens), WIDE)],
        name="places",
    )(order, routes_rows)


GROUP = 4


def dispatch_kernel(pos_ref, order_ref, moe_ref, cot_ref, prob_ref, out_ref, parts_ref):
    step = pl.program_id(0)

    @pl.when(step == 0)
    def _():
        prob = prob_ref[...]
        high = prob.astype(NARROW)
        rest = prob - high.astype(WIDE)
        middle = rest.astype(NARROW)
        parts_ref[:, 0:128] = high
        parts_ref[:, 128:256] = middle
        parts_ref[:, 256:384] = (rest - middle.astype(WIDE)).astype(NARROW)

    slot = lax.broadcasted_iota(jnp.int32, (CAP, 1), 0).astype(WIDE)
    lane = lax.broadcasted_iota(jnp.int32, (1, 128), 1)
    hot = jnp.concatenate(
        [(pos_ref[g : g + 1, :] == slot).astype(NARROW) for g in range(GROUP)], 0
    )
    rows = nn(hot, moe_ref[...]).astype(NARROW)
    grads = nn(hot, cot_ref[...])
    parts = nn(hot, parts_ref[...])
    gates = parts[:, 0:128] + parts[:, 128:256] + parts[:, 256:384]
    for g in range(GROUP):
        s = slice(g * CAP, (g + 1) * CAP)
        expert = order_ref[g : g + 1, 0:1]
        gate = jnp.sum(jnp.where(lane == expert, gates[s], 0.0), -1, keepdims=True)
        out_ref[g, 0:CAP, :] = rows[s]
        out_ref[g, CAP : 2 * CAP, :] = (gate * grads[s]).astype(NARROW)


def dispatch(pos, order, moe, cot, prob):
    tokens = moe.shape[0]
    groups = EXPERTS // GROUP
    return pl.pallas_call(
        dispatch_kernel,
        grid=(groups,),
        in_specs=[
            pl.BlockSpec((None, GROUP, tokens), lambda i: (i, 0, 0)),
            pl.BlockSpec((None, GROUP, 128), lambda i: (i, 0, 0)),
            whole(moe.shape),
            whole(cot.shape),
            whole(prob.shape),
        ],
        out_specs=pl.BlockSpec((GROUP, 2 * CAP, D), lambda i: (i, 0, 0)),
        out_shape=sds((EXPERTS, 2 * CAP, D), NARROW),
        scratch_shapes=[pltpu.VMEM((tokens, 384), NARROW)],
        compiler_params=params(48),
        name="dispatch",
    )(pos.reshape(groups, GROUP, tokens), order.reshape(groups, GROUP, 128), moe, cot, prob)


def expert_kernel(pick, rows_ref, win_ref, wout_ref, back_ref, din_ref, dout_ref, res, sgr):
    f = pl.program_id(0)
    senders = rows_ref.shape[0]
    part = min(senders, 8)
    count = part * CAP
    win, wout = win_ref[...], wout_ref[...]
    d_in = d_out = None
    for first in range(0, senders, part):
        slots = rows_ref[first : first + part, 0:CAP, :].reshape(count, D)
        grads = rows_ref[first : first + part, CAP : 2 * CAP, :].reshape(count, D)
        r = slice(first * CAP, (first + part) * CAP)
        pre = nn(slots, win)
        hidden_grad = nt(grads, wout)
        cdf, bell = normal_parts(pre)
        hidden = (pre * cdf).astype(NARROW)
        pre_grad = ((cdf + pre * (bell * INV_ROOT)) * hidden_grad).astype(NARROW)
        result = nn(hidden, wout)
        slot_grad = nt(pre_grad, win)
        in_part, out_part = tn(slots, pre_grad), tn(hidden, grads)
        d_in = in_part if d_in is None else d_in + in_part
        d_out = out_part if d_out is None else d_out + out_part

        @pl.when(f == 0)
        def _(r=r, result=result, slot_grad=slot_grad):
            res[r, :] = result
            sgr[r, :] = slot_grad

        @pl.when(f > 0)
        def _(r=r, result=result, slot_grad=slot_grad):
            res[r, :] += result
            sgr[r, :] += slot_grad

    din_ref[...] = d_in.astype(NARROW)
    dout_ref[...] = d_out.astype(NARROW)

    @pl.when(f == pl.num_programs(0) - 1)
    def _():
        back_ref[:, :, 0:D] = res[...].astype(NARROW).reshape(senders, CAP, D)
        back_ref[:, :, D : 2 * D] = sgr[...].astype(NARROW).reshape(senders, CAP, D)


def expert(pick, rows, win, wout):
    senders = rows.shape[0]
    wide = 512
    return pl.pallas_call(
        expert_kernel,
        grid_spec=pltpu.PrefetchScalarGridSpec(
            num_scalar_prefetch=1,
            grid=(FF // wide,),
            in_specs=[
                whole(rows.shape),
                pl.BlockSpec((None, D, wide), lambda f, p: (p[0], 0, f)),
                pl.BlockSpec((None, wide, D), lambda f, p: (p[0], f, 0)),
            ],
            out_specs=[
                whole((senders, CAP, 2 * D)),
                pl.BlockSpec((None, D, wide), lambda f, p: (f, 0, 0)),
                pl.BlockSpec((None, wide, D), lambda f, p: (f, 0, 0)),
            ],
            scratch_shapes=[
                pltpu.VMEM((senders * CAP, D), WIDE),
                pltpu.VMEM((senders * CAP, D), WIDE),
            ],
        ),
        out_shape=[
            sds((senders, CAP, 2 * D), NARROW),
            sds((FF // wide, D, wide), NARROW),
            sds((FF // wide, wide, D), NARROW),
        ],
        compiler_params=params(56),
        cost_estimate=cost(12 * senders * CAP * D * FF, 8 * D * FF),
        name="one_expert",
    )(pick, rows, win, wout)


def attn_bwd_body(x, incoming, gain, qkv_ref, mixed_ref, w_ref, dw_ref, ib):
    unit, inverse = norm_parts(x)
    normed = (unit * gain).astype(NARROW)
    out_grad = incoming.astype(NARROW)
    mixed = mixed_ref[...].reshape(ib * SP, D)
    dw_ref[:, 3 * D : 4 * D] += tn(mixed, out_grad)
    mixed_grad = nt(out_grad, w_ref[:, 3 * D : 4 * D]).astype(NARROW)
    masks = head_masks(NARROW)
    rows = lax.broadcasted_iota(jnp.int32, (SP, SP), 0)
    dq_all, dk_all, dv_all = [], [], []
    for i in range(ib):
        r = slice(i * SP, (i + 1) * SP)
        dqs, dks, dvs = [], [], []
        for pair in range(HEADS // 2):
            qp = qkv_ref[i, :, pair * 128 : (pair + 1) * 128]
            kp = qkv_ref[i, :, D + pair * 128 : D + (pair + 1) * 128]
            vp = qkv_ref[i, :, 2 * D + pair * 128 : 2 * D + (pair + 1) * 128]
            mp = mixed_grad[r, pair * 128 : (pair + 1) * 128]
            dq = dk = dv = None
            for half in range(2):
                qm, mm, km = qp * masks[half], mp * masks[half], kp * masks[half]
                s = jnp.where(rows < SEQ, nt(kp, qm), LOWEST)
                e = jnp.exp(s - jnp.max(s, 0, keepdims=True))
                soft = e * (1.0 / jnp.sum(e, 0, keepdims=True))
                pg = nt(vp, mm)
                delta = jnp.sum(soft * pg, 0, keepdims=True)
                sg = (soft * (pg - delta)).astype(NARROW)
                v_part = nn(soft.astype(NARROW), mm)
                k_part = nn(sg, qm)
                q_part = tn(sg, km)
                dq = q_part if dq is None else dq + q_part
                dk = k_part if dk is None else dk + k_part
                dv = v_part if dv is None else dv + v_part
            dqs.append((dq * SCALE).astype(NARROW))
            dks.append(dk.astype(NARROW))
            dvs.append(dv.astype(NARROW))
        dq_all.append(jnp.concatenate(dqs, 1))
        dk_all.append(jnp.concatenate(dks, 1))
        dv_all.append(jnp.concatenate(dvs, 1))
    dqkv = jnp.concatenate(
        [
            jnp.concatenate(a, 0) if ib > 1 else a[0]
            for a in (dq_all, dk_all, dv_all)
        ],
        1,
    )
    dw_ref[:, 0 : 3 * D] += tn(normed, dqkv)
    normed_grad = nt(dqkv, w_ref[:, 0 : 3 * D])
    input_grad, gain_grad = norm_backward(normed_grad, unit, inverse, gain)
    return incoming + input_grad, gain_grad


def gain_columns(dg_ref):
    tall = jnp.concatenate(
        [jnp.zeros((EXPERTS, D), WIDE), dg_ref[...], jnp.zeros((128 - EXPERTS - 8, D), WIDE)], 0
    )
    return jnp.transpose(tall)


def put_rows(ref, step, ib, value):
    for image in range(ref.shape[0] // SEQ):

        @pl.when(step == image // ib)
        def _(image=image):
            first = image % ib * SP
            ref[image * SEQ : (image + 1) * SEQ, :] = value[first : first + SEQ]


def moe_bwd_kernel(
    ib,
    tables,
    g_ref,
    w_ref,
    wr_ref,
    mid_ref,
    second_ref,
    cot_ref,
    prob_ref,
    aux_ref,
    qkv_ref,
    mixed_ref,
    *rest,
):
    table_refs = rest[:tables]
    y_ref, grad_ref, dw_out, dr_ref, dg_ref, dw_ref = rest[tables:]
    step = pl.program_id(0)

    @pl.when(step == 0)
    def _():
        dw_ref[...] = jnp.zeros(dw_ref.shape, WIDE)
        dr_ref[...] = jnp.zeros(dr_ref.shape, WIDE)
        dg_ref[...] = jnp.zeros(dg_ref.shape, WIDE)

    second = second_ref[...].reshape(ib * SP, D)
    upstream = cot_ref[...].astype(WIDE).reshape(ib * SP, D)
    prob = prob_ref[...].reshape(ib * SP, 128)
    aux = aux_ref[...].reshape(ib * SP, 128)
    first_pick = second_pick = back = None
    for j, table in enumerate(table_refs):
        owners = table.shape[0]
        count = owners * CAP
        slot = lax.broadcasted_iota(jnp.int32, (1, count), 1) + j * count
        hot_one = (aux[:, 0:1] == slot).astype(NARROW)
        hot_two = (aux[:, 1:2] == slot).astype(NARROW)
        rows = table[...].reshape(count, 2 * D)
        one = nn(hot_one, rows[:, 0:D])
        two = nn(hot_two, rows[:, 0:D])
        both = nn(hot_one + hot_two, rows[:, D : 2 * D])
        first_pick = one if first_pick is None else first_pick + one
        second_pick = two if second_pick is None else second_pick + two
        back = both if back is None else back + both
    lane = lax.broadcasted_iota(jnp.int32, (1, 128), 1)
    first_hit = (aux[:, 2:3] == lane).astype(WIDE)
    second_hit = (aux[:, 3:4] == lane).astype(WIDE)
    gate_one = jnp.sum(prob * first_hit, -1, keepdims=True)
    gate_two = jnp.sum(prob * second_hit, -1, keepdims=True)
    put_rows(y_ref, step, ib, second + (gate_one * first_pick + gate_two * second_pick))
    gate_one_grad = jnp.sum(upstream * first_pick, -1, keepdims=True)
    gate_two_grad = jnp.sum(upstream * second_pick, -1, keepdims=True)
    prob_grad = gate_one_grad * first_hit + gate_two_grad * second_hit
    logit_grad = (prob * (prob_grad - jnp.sum(prob * prob_grad, -1, keepdims=True))).astype(NARROW)
    unit, inverse = norm_parts(second)
    gain = g_ref[3:4, :]
    moe = (unit * gain).astype(NARROW)
    dr_ref[...] += tn(moe, logit_grad)
    normed_grad = back + nt(logit_grad, wr_ref[...])
    moe_grad, gain_grad = norm_backward(normed_grad, unit, inverse, gain)
    dg_ref[3:4, :] += gain_grad
    mid = mid_ref[...].reshape(ib * SP, D)
    grad, gain_grad = attn_bwd_body(
        mid, upstream + moe_grad, g_ref[1:2, :], qkv_ref, mixed_ref, w_ref, dw_ref, ib
    )
    dg_ref[1:2, :] += gain_grad
    grad_ref[...] = grad.reshape(ib, SP, D)

    @pl.when(step == pl.num_programs(0) - 1)
    def _():
        dw_out[:, : 4 * D] = dw_ref[...].astype(NARROW)
        dw_out[:, 4 * D :] = (dr_ref[...] + gain_columns(dg_ref)).astype(NARROW)


def moe_bwd(gains, w1, wr, mid, second, cot, prob, aux, qkv, mixed, tables, images, ib):
    return pl.pallas_call(
        partial(moe_bwd_kernel, ib, len(tables)),
        grid=(images // ib,),
        in_specs=[
            whole(gains.shape),
            whole(w1.shape),
            whole(wr.shape),
            per_image(ib, SP, D),
            per_image(ib, SP, D),
            per_image(ib, SP, D),
            per_image(ib, SP, 128),
            per_image(ib, SP, 128),
            per_image(ib, SP, 3 * D),
            per_image(ib, SP, D),
            *[whole(t.shape) for t in tables],
        ],
        out_specs=[
            whole((images * SEQ, D)),
            per_image(ib, SP, D),
            whole((D, 4 * D + 128)),
        ],
        out_shape=[
            sds((images * SEQ, D), WIDE),
            sds((images, SP, D), WIDE),
            sds((D, 4 * D + 128), NARROW),
        ],
        scratch_shapes=[
            pltpu.VMEM((D, 128), WIDE),
            pltpu.VMEM((8, D), WIDE),
            pltpu.VMEM((D, 4 * D), WIDE),
        ],
        compiler_params=params(56),
        cost_estimate=cost(60e9, 60e6),
        name="expert_block_backward",
    )(gains, w1, wr, mid, second, cot, prob, aux, qkv, mixed, *tables)


def dense_bwd_kernel(
    ib,
    g_ref,
    w_ref,
    win_ref,
    wout_ref,
    x_ref,
    first_ref,
    grad_ref,
    qkv_ref,
    mixed_ref,
    out_ref,
    dw_out,
    dout_out,
    dg_ref,
    dw_ref,
    din_ref,
    dout_ref,
):
    step = pl.program_id(0)

    @pl.when(step == 0)
    def _():
        dw_ref[...] = jnp.zeros(dw_ref.shape, WIDE)
        din_ref[...] = jnp.zeros(din_ref.shape, WIDE)
        dout_ref[...] = jnp.zeros(dout_ref.shape, WIDE)
        dg_ref[...] = jnp.zeros(dg_ref.shape, WIDE)

    incoming = grad_ref[...].reshape(ib * SP, D)
    first = first_ref[...].reshape(ib * SP, D)
    unit, inverse = norm_parts(first)
    gain = g_ref[2:3, :]
    normed = (unit * gain).astype(NARROW)
    out_grad = incoming.astype(NARROW)
    y_grad = None
    for f in range(FF // 512):
        c = slice(f * 512, (f + 1) * 512)
        win, wout = win_ref[:, c], wout_ref[c, :]
        pre = nn(normed, win)
        hidden_grad = nt(out_grad, wout)
        cdf, bell = normal_parts(pre)
        hidden = (pre * cdf).astype(NARROW)
        pre_grad = ((cdf + pre * (bell * INV_ROOT)) * hidden_grad).astype(NARROW)
        dout_ref[c, :] += tn(hidden, out_grad)
        din_ref[:, c] += tn(normed, pre_grad)
        part = nt(pre_grad, win)
        y_grad = part if y_grad is None else y_grad + part
    ffn_grad, gain_grad = norm_backward(y_grad, unit, inverse, gain)
    dg_ref[2:3, :] += gain_grad
    x = x_ref[...].astype(WIDE).reshape(ib * SP, D)
    grad, gain_grad = attn_bwd_body(
        x, incoming + ffn_grad, g_ref[0:1, :], qkv_ref, mixed_ref, w_ref, dw_ref, ib
    )
    dg_ref[0:1, :] += gain_grad
    put_rows(out_ref, step, ib, grad)

    @pl.when(step == pl.num_programs(0) - 1)
    def _():
        dw_out[:, : 4 * D] = dw_ref[...].astype(NARROW)
        dw_out[:, 4 * D : 8 * D] = din_ref[...].astype(NARROW)
        dw_out[:, 8 * D :] = gain_columns(dg_ref).astype(NARROW)
        dout_out[...] = dout_ref[...].astype(NARROW)


def dense_bwd(gains, w0, win, wout, x, first, grad, qkv, mixed, images, ib):
    return pl.pallas_call(
        partial(dense_bwd_kernel, ib),
        grid=(images // ib,),
        in_specs=[
            whole(gains.shape),
            whole(w0.shape),
            whole(win.shape),
            whole(wout.shape),
            per_image(ib, SP, D),
            per_image(ib, SP, D),
            per_image(ib, SP, D),
            per_image(ib, SP, 3 * D),
            per_image(ib, SP, D),
        ],
        out_specs=[
            whole((images * SEQ, D)),
            whole((D, 8 * D + 128)),
            whole((FF, D)),
        ],
        out_shape=[
            sds((images * SEQ, D), WIDE),
            sds((D, 8 * D + 128), NARROW),
            sds((FF, D), NARROW),
        ],
        scratch_shapes=[
            pltpu.VMEM((8, D), WIDE),
            pltpu.VMEM((D, 4 * D), WIDE),
            pltpu.VMEM((D, FF), WIDE),
            pltpu.VMEM((FF, D), WIDE),
        ],
        compiler_params=params(56),
        cost_estimate=cost(60e9, 60e6),
        name="dense_block_backward",
    )(gains, w0, win, wout, x, first, grad, qkv, mixed)


BLOCK = 512
MESH_ID = pl.DeviceIdType.MESH


def add_rows(out, one, two, rows, step):
    @pl.loop(0, rows // step)
    def _(i):
        r = pl.ds(pl.multiple_of(i * step, step), step)
        out[r, :] = (one[r, :].astype(WIDE) + two[r, :].astype(WIDE)).astype(out.dtype)


def sum_kernel(nz, groups, mats, slices, *refs):
    exp_refs, refs = refs[:mats], refs[mats:]
    dense_refs, peak_ref, refs = refs[:3], refs[3], refs[4:]
    exp_out, dense_outs, peak_out, refs = refs[0], refs[1:4], refs[4], refs[5:]
    own, up, down, refs = refs[0], refs[1], refs[2], refs[3:]
    land, refs = refs[:4], refs[4:]
    dense_own, refs = refs[:4], refs[4:]
    dense_up, refs = refs[:4], refs[4:]
    dense_down, refs = refs[:4], refs[4:]
    (own_sem, up_send, up_recv, down_recv, out_send, sib_send, sib_recv, copy_sem, rs_send, rs_recv) = refs

    z, core, f = lax.axis_index("z"), lax.axis_index("core"), lax.axis_index("fsdp")
    half = nz // 2
    left = z < half
    inner = jnp.where(left, z + 1, z - 1)
    outer = jnp.where(left, z - 1, z + 1)
    has_outer = jnp.logical_and(z > 0, z < nz - 1)
    edge = jnp.logical_not(has_outer)
    center = jnp.logical_or(z == half - 1, z == half)
    away = jnp.logical_not(center)
    outer = jnp.where(has_outer, outer, inner)
    sibling = (z, 1 - core, f)
    members = CORES * groups
    me = core * groups + f

    barrier = pltpu.get_barrier_semaphore()
    pl.semaphore_signal(barrier, inc=1, device_id=(inner, core, f), device_id_type=MESH_ID)

    @pl.when(has_outer)
    def _():
        pl.semaphore_signal(barrier, inc=1, device_id=(outer, core, f), device_id_type=MESH_ID)

    for d in range(1, members):
        there = lax.rem(me + d, members)
        pl.semaphore_signal(
            barrier,
            inc=1,
            device_id=(z, there // groups, lax.rem(there, groups)),
            device_id_type=MESH_ID,
        )

    @pl.when(has_outer)
    def _():
        pl.semaphore_wait(barrier, members + 1)

    @pl.when(edge)
    def _():
        pl.semaphore_wait(barrier, members)

    chunks = mats * slices
    items = chunks + 4

    def piece(n, ref, there):
        if n == 3:
            return ref
        rows = ref.shape[0] // members
        place = (lax.rem(there, groups) * CORES + there // groups) * rows
        return ref.at[pl.ds(pl.multiple_of(place, 16), rows), :]

    def scatter(n, d):
        there = lax.rem(me + d, members)
        source = dense_refs[n] if n < 3 else peak_ref
        return pltpu.make_async_remote_copy(
            src_ref=piece(n, source, there),
            dst_ref=land[n].at[d],
            send_sem=rs_send.at[n, d],
            recv_sem=rs_recv.at[n, d],
            device_id=(z, there // groups, lax.rem(there, groups)),
            device_id_type=MESH_ID,
        )

    for n in (3, 1, 0, 2):
        for d in range(1, members):
            scatter(n, d).start()
    keep = [
        pltpu.make_async_copy(
            piece(n, dense_refs[n] if n < 3 else peak_ref, me), land[n].at[0], rs_recv.at[n, 0]
        )
        for n in range(4)
    ]
    for k in keep:
        k.start()

    def load(t):
        return pltpu.make_async_copy(exp_refs[t // slices].at[t % slices], own.at[t], own_sem.at[t])

    @pl.when(has_outer)
    def _():
        for t in range(chunks):
            load(t).start()

    def bufs(t):
        if t < chunks:
            return own.at[t], up.at[t], down.at[t]
        n = t - chunks
        return dense_own[n], dense_up[n], dense_down[n]

    def send_up(t, source, to_center):
        _, u, dn = bufs(t)
        return pltpu.make_async_remote_copy(
            src_ref=source,
            dst_ref=dn if to_center else u,
            send_sem=up_send.at[t],
            recv_sem=(down_recv if to_center else up_recv).at[t],
            device_id=(inner, core, f),
            device_id_type=MESH_ID,
        )

    def source_at_edge(t):
        return exp_refs[t // slices].at[t % slices] if t < chunks else bufs(t)[0]

    def join(t, out, one, two):
        if t == items - 1:
            out[...] = jnp.maximum(one[...], two[...])
        else:
            add_rows(out, one, two, out.shape[0], 16)

    def reduce_own(n):
        for d in range(members):
            if d == 0:
                keep[n].wait()
            else:
                scatter(n, d).wait_recv()
        if n == 3:
            best = land[n][0]
            for d in range(1, members):
                best = jnp.maximum(best, land[n][d])
            dense_own[n][...] = best
            return

        @pl.loop(0, dense_own[n].shape[0] // 16)
        def _(i):
            r = pl.ds(pl.multiple_of(i * 16, 16), 16)
            total = land[n][0, r, :].astype(WIDE)
            for d in range(1, members):
                total = total + land[n][d, r, :].astype(WIDE)
            dense_own[n][r, :] = total.astype(NARROW)

    def up_from_edge(t, before):
        if before is not None:
            send_up(before, source_at_edge(before), half == 1).wait_send()
        if t >= chunks:
            reduce_own(t - chunks)
        send_up(t, source_at_edge(t), half == 1).start()

    def up_from_inside(t):
        o, u, _ = bufs(t)
        if t >= chunks:
            reduce_own(t - chunks)
        else:
            load(t).wait()
        send_up(t, u, False).wait_recv()
        join(t, o, o, u)

        @pl.when(center)
        def _():
            send_up(t, o, True).start()

        if half > 2:

            @pl.when(away)
            def _():
                send_up(t, o, False).start()

    def results(t):
        if t < chunks:
            return exp_out.at[t, core]
        n = t - chunks
        if n == 3:
            return peak_out
        ref = dense_outs[n]
        rows = ref.shape[0] // CORES
        return ref.at[pl.ds(pl.multiple_of(core * rows, 16), rows), :]

    def to_sibling(t):
        return pltpu.make_async_remote_copy(
            src_ref=bufs(t)[2],
            dst_ref=results(t),
            send_sem=sib_send.at[t],
            recv_sem=sib_recv.at[t],
            device_id=sibling,
            device_id_type=MESH_ID,
        )

    def to_outer(t):
        dn = bufs(t)[2]
        return pltpu.make_async_remote_copy(
            src_ref=dn,
            dst_ref=dn,
            send_sem=out_send.at[t],
            recv_sem=down_recv.at[t],
            device_id=(outer, core, f),
            device_id_type=MESH_ID,
        )

    def keep_result(t):
        return pltpu.make_async_copy(bufs(t)[2], results(t), copy_sem.at[t])

    def go_down(t, at_edge):
        o, _, dn = bufs(t)
        to_outer(t).wait_recv()
        if at_edge:
            if half == 1:
                join(t, dn, source_at_edge(t), dn)
        else:

            @pl.when(center)
            def _():
                join(t, dn, o, dn)

            to_outer(t).start()
        keep_result(t).start()
        if t < items - 1:
            to_sibling(t).start()

    early = min(8, chunks)
    sequence = [*range(early), *range(items - 1, chunks - 1, -1), *range(early, chunks)]

    def run(up, at_edge, lag):
        for i in range(items + lag):
            if i < items:
                up(i)
            if i >= lag:
                go_down(sequence[i - lag], at_edge)

    @pl.when(edge)
    def _():
        run(
            lambda i: up_from_edge(sequence[i], sequence[i - 2] if i >= 2 else None),
            True,
            min(7, items),
        )
        for t in sequence[-2:]:
            send_up(t, source_at_edge(t), half == 1).wait_send()

    if half > 1:

        @pl.when(has_outer)
        def _():
            run(lambda i: up_from_inside(sequence[i]), False, 1)
            for t in range(items):
                send_up(t, bufs(t)[0], False).wait_send()
                to_outer(t).wait_send()

    for n in range(4):
        for d in range(1, members):
            scatter(n, d).wait_send()
    for t in range(items):
        keep_result(t).wait()
        if t < items - 1:
            to_sibling(t).wait()


def sum_all(mats, dense, peaks, nz, groups):
    slices = mats[0].shape[0]
    chunks = len(mats) * slices
    members = CORES * groups
    items = chunks + 4
    any_space = pl.BlockSpec(memory_space=pl.ANY)
    vmem = pl.BlockSpec(memory_space=pltpu.VMEM)
    pieces = [(a.shape[0] // members, a.shape[1]) for a in dense]
    block = pltpu.VMEM((chunks, BLOCK, BLOCK), NARROW)

    def four(lead=()):
        return [pltpu.VMEM((*lead, *p), NARROW) for p in pieces] + [
            pltpu.VMEM((*lead, *peaks.shape), WIDE)
        ]

    dma = pltpu.SemaphoreType.DMA
    return pl.pallas_call(
        partial(sum_kernel, nz, groups, len(mats), slices),
        in_specs=[any_space] * (len(mats) + 3) + [vmem],
        out_specs=[any_space] * 4 + [vmem],
        out_shape=[
            sds((chunks, CORES, BLOCK, BLOCK), NARROW),
            *[sds((CORES * r, c), NARROW) for r, c in pieces],
            sds(peaks.shape, WIDE),
        ],
        scratch_shapes=[
            block,
            block,
            block,
            *four((members,)),
            *four(),
            *four(),
            *four(),
            *[dma((items,)) for _ in range(8)],
            dma((4, members)),
            dma((4, members)),
        ],
        compiler_params=pltpu.CompilerParams(
            vmem_limit_bytes=58 * MIB, collective_id=3, has_side_effects=True
        ),
        name="sums",
    )(*mats, *dense, peaks)


def widen_kernel(early, core_ref, *refs):
    own, other, refs = refs[:early], refs[early : 2 * early], refs[2 * early :]
    late, outs = refs[:-2], refs[-2:]
    c, j = pl.program_id(0), pl.program_id(1)

    def put(side, block):
        for f in range(block.shape[0]):
            s = slice(f * BLOCK, (f + 1) * BLOCK)
            if side == 0:
                outs[0][:, s] = block[f].astype(WIDE)
            else:
                outs[1][s, :] = block[f].astype(WIDE)

    for side in range(2):
        for n in range(side, early, 2):
            for source, here in ((own[n], True), (other[n], False)):

                @pl.when(jnp.logical_and(2 * j + side == n, (c == core_ref[0]) == here))
                def _(source=source):
                    put(side, source)

        @pl.when(2 * j + side >= early)
        def _():
            put(side, late[side])


def widen(core, own, other, late, mine, slices):
    early = len(own)
    late = late.reshape(-1, slices, CORES, BLOCK, BLOCK)
    count = late.shape[0]

    def late_spec(side):
        def where_from(c, j, _):
            return (jnp.clip(2 * j + side - early, 0, count - 1), 0, c, 0, 0)

        return pl.BlockSpec((None, slices, None, BLOCK, BLOCK), where_from)

    return pl.pallas_call(
        partial(widen_kernel, early),
        grid_spec=pltpu.PrefetchScalarGridSpec(
            num_scalar_prefetch=1,
            grid=(CORES, mine),
            in_specs=[whole(a.shape) for a in (*own, *other)] + [late_spec(0), late_spec(1)],
            out_specs=[
                pl.BlockSpec((None, D, FF), lambda c, j, _: (c * mine + j, 0, 0)),
                pl.BlockSpec((None, FF, D), lambda c, j, _: (c * mine + j, 0, 0)),
            ],
        ),
        out_shape=[sds((CORES * mine, D, FF), WIDE), sds((CORES * mine, FF, D), WIDE)],
        compiler_params=params(56),
        name="widen",
    )(core, *own, *other, late, late)


def gather(x):
    return lax.all_gather(x, "fsdp", axis=0, tiled=True)


def images_of(x, images):
    return jnp.pad(x.reshape(images, SEQ, x.shape[-1]), ((0, 0), (0, SP - SEQ), (0, 0)))


def local(
    tokens,
    cotangent,
    routes,
    attn_norm,
    query_w,
    key_w,
    value_w,
    output_w,
    ffn_norm,
    mlp_in,
    mlp_out,
    router_w,
    expert_in,
    expert_out,
    updated_query,
    updated_key,
    clip_threshold,
):
    images = tokens.shape[0] // SEQ
    ib = 2
    groups = lax.axis_size("fsdp")
    core = lax.axis_index("core")
    held = expert_in.shape[0]
    mine = held // CORES
    owners = CORES * groups

    small = jnp.concatenate(
        [
            router_w,
            jnp.transpose(attn_norm),
            jnp.transpose(ffn_norm),
            jnp.zeros((router_w.shape[0], 128 - EXPERTS - 4), NARROW),
        ],
        1,
    )
    w0 = gather(jnp.concatenate([query_w[0], key_w[0], value_w[0], output_w[0], small], 1))
    win = gather(mlp_in)
    wout = gather(mlp_out)
    w1 = gather(jnp.concatenate([query_w[1], key_w[1], value_w[1], output_w[1]], 1))
    w_small = w0[:, 4 * D :]
    wr = jnp.where(jnp.arange(128)[None, :] < EXPERTS, w_small, 0)
    gains = jnp.pad(
        jnp.transpose(w_small[:, EXPERTS : EXPERTS + 4]).astype(WIDE), ((0, 4), (0, 0))
    )

    x = images_of(tokens, images)
    cot = images_of(cotangent, images)
    routes_image = jnp.pad(
        routes.reshape(images, SEQ, 2), ((0, 0), (0, SP - SEQ), (0, 0)), constant_values=-1
    )
    routes_rows = jnp.pad(
        jnp.transpose(routes_image.reshape(-1, 2)), ((0, 6), (0, 0)), constant_values=-1
    )
    slot = jnp.arange(EXPERTS, dtype=jnp.int32)
    place_there, owner = slot // owners, slot % owners
    order = (owner % groups) * held + (owner // groups) * mine + place_there
    order = jnp.broadcast_to(order[:, None], (EXPERTS, 128))
    pos, target = places(order, routes_rows)
    aux = jnp.pad(
        jnp.concatenate(
            [
                jnp.transpose(target[0:2]).astype(jnp.int32).reshape(images, SP, 2),
                routes_image,
            ],
            -1,
        ),
        ((0, 0), (0, 0), (0, 124)),
        constant_values=-1,
    )

    first, qkv0, mixed0, peak0 = dense_attn(x, gains, w0, images, ib)
    mid = ffn(first, gains, win, wout, images, ib)
    second, qkv1, mixed1, peak1, moe, prob = expert_attn(mid, gains, w1, wr, images, ib)
    sent = dispatch(
        pos, order, moe.reshape(-1, D), cot.reshape(-1, D), prob.reshape(-1, 128)
    ).reshape(mine, owners, 2 * CAP, D)

    tables, mats, backs = [], [], []
    for j in range(mine):
        chunk = sent[j]
        if j >= 2:
            chunk, _ = lax.optimization_barrier((chunk, backs[j - 2]))
        rows = lax.all_to_all(chunk, ("core", "fsdp"), split_axis=0, concat_axis=0, tiled=True)
        pick = (core * mine + j).astype(jnp.int32).reshape(1)
        back, d_in, d_out = expert(pick, rows, expert_in, expert_out)
        backs.append(back)
        tables.append(
            lax.all_to_all(back, ("core", "fsdp"), split_axis=0, concat_axis=0, tiled=True)
        )
        mats += [d_in, d_out]
    early = len(mats) * 3 // 8
    mats, ready, others = list(mats), [], []
    for n in range(0, early, 2):
        batch = mats[n : min(n + 2, early)]
        if ready:
            batch, _ = lax.optimization_barrier((batch, ready))
        ready += lax.psum(batch, "z")
    others = [lax.ppermute(mat, "core", [(0, 1), (1, 0)]) for mat in ready]

    y, mid_grad, dw1 = moe_bwd(
        gains, w1, wr, mid, second, cot, prob, aux, qkv1, mixed1, tables, images, ib
    )
    x_grad, dw0, d_wout = dense_bwd(
        gains, w0, win, wout, x, first, mid_grad, qkv0, mixed0, images, ib
    )
    lane = jnp.arange(128)[None, :]
    peaks = jnp.where(lane < 64, jnp.max(peak0, 0), jnp.max(peak1, 0))
    late, t1, t0, t_wout, maxima = sum_all(
        mats[early:], [dw1, dw0, d_wout], peaks, lax.axis_size("z"), groups
    )
    expert_in_grad, expert_out_grad = widen(
        core.astype(jnp.int32).reshape(1), ready, others, late, mine, mats[0].shape[0]
    )

    t1, t0 = t1.astype(WIDE), t0.astype(WIDE)
    t_small = t1[:, 4 * D :] + t0[:, 8 * D :]
    norm_rows = jnp.transpose(t_small[:, EXPERTS : EXPERTS + 4])
    maxima = jnp.stack([maxima[:, 0], maxima[:, 64]])
    factor = clip_threshold / jnp.maximum(maxima, clip_threshold)
    column_scale = jnp.repeat(jnp.sqrt(factor), HEAD, axis=1)

    def both(n):
        return jnp.stack([t0[:, n * D : (n + 1) * D], t1[:, n * D : (n + 1) * D]])

    return (
        y,
        x_grad,
        norm_rows[0:2],
        both(0),
        both(1),
        both(2),
        both(3),
        norm_rows[2:4],
        t0[:, 4 * D : 8 * D],
        t_wout.astype(WIDE),
        t_small[:, :EXPERTS],
        expert_in_grad,
        expert_out_grad,
        updated_query * column_scale[:, None, :],
        updated_key * column_scale[:, None, :],
    )


def solution(mesh):
    replicas, groups = mesh.shape["replica"], mesh.shape["fsdp"]
    inner = Mesh(
        mesh.devices.reshape(replicas // CORES, CORES, groups), ("z", "core", "fsdp")
    )
    split = P(("z", "core", "fsdp"), None)
    second = P(None, "fsdp", None)
    in_specs = (
        split,
        split,
        split,
        P(None, "fsdp"),
        second,
        second,
        second,
        second,
        P(None, "fsdp"),
        P("fsdp", None),
        P("fsdp", None),
        P("fsdp", None),
        P("fsdp", None, None),
        P("fsdp", None, None),
        second,
        second,
        P(),
    )
    out_specs = (
        split,
        split,
        P(None, "fsdp"),
        second,
        second,
        second,
        second,
        P(None, "fsdp"),
        P("fsdp", None),
        P("fsdp", None),
        P("fsdp", None),
        P("fsdp", None, None),
        P("fsdp", None, None),
        second,
        second,
    )
    return jax.shard_map(local, mesh=inner, in_specs=in_specs, out_specs=out_specs, check_vma=False)
```

time: 1940 us -> 1020 us (0.53)
  Pallas kernels: 0 us -> 643 us
  waiting for transfers between devices: 759 us -> 193 us
  matrix products: 372 us -> 0 us
  local copies, waits for them, and re-layouts: 301 us -> 37.4 us
  blocking collectives: 283 us -> 88.3 us
  other arithmetic: 189 us -> 13.2 us
  starting transfers between devices: 10.4 us -> 32.6 us
    pallas_call x0 -> x13, Pallas kernels: none -> 643 us  [the longest x1 299 us: sum_all(): pl.pallas_call(partial(sum_kernel, nz, groups, len(mats), slices), in_spe...]
    psum x1 -> x2, waiting for transfers between devices: 612 us -> 68.2 us  [local(): ready += lax.psum(batch, 'z')]
    dot_general x51 -> x0, matrix products: 372 us -> none  [the longest x11 67.9 us: matmul(): return jnp.dot(former, latter, preferred_element_type=WIDE)]
    convert_element_type x16 -> x4, other arithmetic: 142 us -> 5.56 us  [the longest x2 2.6 us: local(): t1, t0 = (t1.astype(WIDE), t0.astype(WIDE))]
    all_gather x13 -> x0, blocking collectives: 131 us -> none  [the longest x1 12.5 us: expert_block_weights(): lax.all_gather(router_w, 'fsdp', axis=0, tiled=True)]
    reshape x28 -> x6, local copies, waits for them, and re-layouts: 122 us -> 5.61 us  [the longest x2 3.67 us: images_of(): x.reshape(images, SEQ, x.shape[-1])]
    all_gather x2 -> x4, waiting for transfers between devices: 0.04 us -> 95.2 us  [gather(): return lax.all_gather(x, 'fsdp', axis=0, tiled=True)]
    gather x7 -> x0, local copies, waits for them, and re-layouts: 93.3 us -> none  [the longest x1 23 us: local(): gate_table[source][:, None] * grad_table[token_pick]]
  transfers between devices with their start and end apart: 16 -> 14, of which waited for: 6 -> 10; matrix products, arithmetic and copies ran while one was open for 20% -> 3% of each run, Pallas kernels for 0% -> 55%
where the time goes in v1:
time: 1020 us
  Pallas kernels  643 us (63%)
  waiting for transfers between devices  193 us (19%)
  blocking collectives  88.3 us (9%)
  local copies, waits for them, and re-layouts  37.4 us (4%)
  starting transfers between devices  32.6 us (3%)
  between operations  14.7 us (1%)
  other arithmetic  13.2 us (1%)
    pallas_call x1, Pallas kernels, sum_all(): pl.pallas_call(partial(sum_kernel, nz, groups, len(mats), slices), in_spe...  299 us
    pallas_call x4, Pallas kernels, expert(): pl.pallas_call(expert_kernel, grid_spec=pltpu.PrefetchScalarGridSpec(num_...  98.7 us
    all_gather x4, waiting for transfers between devices, gather(): return lax.all_gather(x, 'fsdp', axis=0, tiled=True)  95.2 us
    psum x2, waiting for transfers between devices, local(): ready += lax.psum(batch, 'z')  68.2 us
    pallas_call x1, Pallas kernels, dense_bwd(): pl.pallas_call(partial(dense_bwd_kernel, ib), grid=(images // ib,), in_sp...  66.7 us
    pallas_call x1, Pallas kernels, moe_bwd(): pl.pallas_call(partial(moe_bwd_kernel, ib, len(tables)), grid=(images //...  64.6 us
    all_to_all x2, blocking collectives, local(): lax.all_to_all(chunk, ('core', 'fsdp'), split_axis=0, concat_axis=0, tile...  58.9 us
    pallas_call x1, Pallas kernels, widen(): pl.pallas_call(partial(widen_kernel, early), grid_spec=pltpu.PrefetchScal...  34.6 us
  transfers between devices with their start and end apart: 14, of which 10 were waited for; matrix products, arithmetic and copies ran while one was open for 3% of the time, Pallas kernels for 55%

profile of v1, /device:TPU:0, one launch (start us, length us, event | category | flops | bytes accessed | tf_op | source)
XLA Modules:
  0.0 1022.0 jit_solution(14333897547980539083)
XLA Ops:
  26.7 25.5 %all-gather.5.cloned.1.call-done.w_ref = bf16[512,2176]{1,0:T(8,128)(2,1)} async-done(((bf16[128,2176]{1,0:T(8,128)(2,1)}), bf16[512,2176]{1,0:T(8,128)(2,1)}) %all-gather.5.cloned.1.call-update) | async-done | bytes 2228240 | tf_op jit(solution)/shard_map/all_gather | solution.py:1045
  56.6 14.2 %dense_attention.1 = (f32[8,208,512]{2,1,0:T(8,128)}, bf16[8,208,1536]{2,1,0:T(8,128)(2,1)}, bf16[8,208,512]{2,1,0:T(8,128)(2,1)S(1)}, f32[8,8,128]{2,1,0:T(8,128)S(1)}) custom-call(bf16[8,208,512]{2,1,0:T(8,128)(2,1)S(1)} %pad.27.x_ref, f32[8,512]{1,0:T(8,128)S(1)} %copy.79.g_ref, bf16[512,2176]{1,0:T(8,128)(2,1)S(1)} %copy-done.2), custom_call_target="tpu_custom_call" | custom-call | tf_op jit(solution)/shard_map/dense_attention/pallas_call | solution.py:177
  72.0 17.4 %all-gather.11.cloned.1.call-done.wout_ref = bf16[2048,512]{1,0:T(8,128)(2,1)} async-done(((bf16[512,512]{1,0:T(8,128)(2,1)}), bf16[2048,512]{1,0:T(8,128)(2,1)}) %all-gather.11.cloned.1.call-update) | async-done | bytes 2097168 | tf_op jit(solution)/shard_map/all_gather | solution.py:1045
  89.4 37.2 %all-gather.9.cloned.1.call-done.win_ref = bf16[512,2048]{1,0:T(8,128)(2,1)} async-done(((bf16[128,2048]{1,0:T(8,128)(2,1)}), bf16[512,2048]{1,0:T(8,128)(2,1)}) %all-gather.9.cloned.1.call-update) | async-done | bytes 2097168 | tf_op jit(solution)/shard_map/all_gather | solution.py:1045
  129.7 18.4 %feed_forward.1.x_ref.mid_ref = f32[8,208,512]{2,1,0:T(8,128)} custom-call(f32[8,208,512]{2,1,0:T(8,128)} %get-tuple-element.55.x_ref.first_ref, f32[8,512]{1,0:T(8,128)S(1)} %copy.79.g_ref, bf16[512,2048]{1,0:T(8,128)(2,1)S(1)} %copy-done.4, bf16[2048,512]{1,0:T(8,128)(2,1)S(1)} %copy-done.3), custom_call_target="tpu_custom_call" | custom-call | tf_op jit(solution)/shard_map/feed_forward/pallas_call | solution.py:199
  149.0 15.1 %all-gather.7.cloned.1.call-done.w_ref = bf16[512,2048]{1,0:T(8,128)(2,1)} async-done(((bf16[128,2048]{1,0:T(8,128)(2,1)}), bf16[512,2048]{1,0:T(8,128)(2,1)}) %all-gather.7.cloned.1.call-update) | async-done | bytes 2097168 | tf_op jit(solution)/shard_map/all_gather | solution.py:1045
  164.2 18.0 %expert_attention.1 = (f32[8,208,512]{2,1,0:T(8,128)}, bf16[8,208,1536]{2,1,0:T(8,128)(2,1)}, bf16[8,208,512]{2,1,0:T(8,128)(2,1)S(1)}, f32[8,8,128]{2,1,0:T(8,1...) custom-call(f32[8,208,512]{2,1,0:T(8,128)} %feed_forward.1.x_ref.mid_ref, ...), custom_call_target="tpu_custom_call" | custom-call | tf_op jit(solution)/shard_map/expert_attention/pallas_call | solution.py:211
  183.4 26.2 %dispatch.1 = bf16[32,256,512]{2,1,0:T(8,128)(2,1)} custom-call(f32[8,4,1664]{2,1,0:T(4,128)S(1)} %copy-done.6, s32[8,4,128]{2,1,0:T(4,128)S(1)} %broadcast_in_dim.40.order_ref, bf16[1664,512]{1,0:T(8,128)(2,1)S(1)} %bitcast.60, bf16[1664,512]{1,0:T(8,128)(2,1)S(1)} %bitcast.59, f32[1664,128]{1,0:T(8,128)S(1)} %bitcast.61), custom_call_target="tpu_custom_call" | custom-call | tf_op jit(solution)/shard_map/dispatch/pallas_call | solution.py:309
  209.6 5.1 fusion.18
  214.7 29.4 %all_to_all.40.rows_ref = bf16[8,256,512]{2,1,0:T(8,128)(2,1)} all-to-all(bf16[8,256,512]{2,1,0:T(8,128)(2,1)S(1)} %get-tuple-element.161), channel_id=1, replica_groups=mesh['z'=4,'core'=2,'fsdp'=4] {'core','fsdp'}, dimensions={0} | all-to-all | bytes 4194304 | tf_op jit(solution)/shard_map/all_to_all | solution.py:1135
  244.1 4.3 all-to-all-start
  248.5 24.7 %one_expert.5 = (bf16[8,128,1024]{2,1,0:T(8,128)(2,1)}, bf16[4,512,512]{2,1,0:T(8,128)(2,1)}, bf16[4,512,512]{2,1,0:T(8,128)(2,1)}) custom-call(s32[1]{0:T(128)} %bitcast.17.pick, bf16[8,256,512]{2,1,0:T(8,128)(2,1)} %all_to_all.40.rows_ref, bf16[8,512,2048]{2,1,0:T(8,128)(2,1)} %win_ref.7, bf16[8,2048,512]{2,1,0:T(8,128)(2,1)} %wout_ref.7), custom_call_target="tpu_custom_call" | custom-call | flops 12884901888 | bytes 8388608 | tf_op jit(solution)/shard_map/one_expert/pallas_call | solution.py:371
  274.6 15.5 %all-to-all-start.6 = ((bf16[8,256,512]{2,1,0:T(8,128)(2,1)}), bf16[8,256,512]{2,1,0:T(8,128)(2,1)}, u32[]{:S(2)}, u32[]{:S(2)}) async-start(bf16[8,256,512]{2,1,0:T(8,128)(2,1)} %get-tuple-element.67), calls=%async_computation.6 | async-start | bytes 4194304 | tf_op jit(solution)/shard_map/all_to_all | solution.py:1135
  290.1 24.7 %one_expert.4 = (bf16[8,128,1024]{2,1,0:T(8,128)(2,1)}, bf16[4,512,512]{2,1,0:T(8,128)(2,1)}, bf16[4,512,512]{2,1,0:T(8,128)(2,1)}) custom-call(s32[1]{0:T(128)} %bitcast.13.pick, bf16[8,256,512]{2,1,0:T(8,128)(2,1)} %all-to-all-done.rows_ref, bf16[8,512,2048]{2,1,0:T(8,128)(2,1)} %win_ref.7, bf16[8,2048,512]{2,1,0:T(8,128)(2,1)} %wout_ref.7), custom_call_target="tpu_custom_call" | custom-call | flops 12884901888 | bytes 8388608 | tf_op jit(solution)/shard_map/one_expert/pallas_call | solution.py:371
  316.0 29.5 %all_to_all.41.rows_ref = bf16[8,256,512]{2,1,0:T(8,128)(2,1)} all-to-all(bf16[8,256,512]{2,1,0:T(8,128)(2,1)S(1)} %get-tuple-element.65), channel_id=1, replica_groups=mesh['z'=4,'core'=2,'fsdp'=4] {'core','fsdp'}, dimensions={0} | all-to-all | bytes 4194304 | tf_op jit(solution)/shard_map/all_to_all | solution.py:1135
  345.5 29.4 %all_to_all.42.rest_1_ = bf16[8,128,1024]{2,1,0:T(8,128)(2,1)} all-to-all(bf16[8,128,1024]{2,1,0:T(8,128)(2,1)S(1)} %copy-done.14), channel_id=1, replica_groups=mesh['z'=4,'core'=2,'fsdp'=4] {'core','fsdp'}, dimensions={0} | all-to-all | bytes 4194304 | tf_op jit(solution)/shard_map/all_to_all | solution.py:1140
  378.5 24.7 %one_expert.7 = (bf16[8,128,1024]{2,1,0:T(8,128)(2,1)}, bf16[4,512,512]{2,1,0:T(8,128)(2,1)}, bf16[4,512,512]{2,1,0:T(8,128)(2,1)}) custom-call(s32[1]{0:T(128)} %bitcast.19.pick, bf16[8,256,512]{2,1,0:T(8,128)(2,1)} %all-to-all-done.6.rows_ref, bf16[8,512,2048]{2,1,0:T(8,128)(2,1)} %win_ref.7, bf16[8,2048,512]{2,1,0:T(8,128)(2,1)} %wout_ref.7), custom_call_target="tpu_custom_call" | custom-call | flops 12884901888 | bytes 8388608 | tf_op jit(solution)/shard_map/one_expert/pallas_call | solution.py:371
  410.2 24.7 %one_expert.6 = (bf16[8,128,1024]{2,1,0:T(8,128)(2,1)}, bf16[4,512,512]{2,1,0:T(8,128)(2,1)}, bf16[4,512,512]{2,1,0:T(8,128)(2,1)}) custom-call(s32[1]{0:T(128)} %bitcast.18.pick, bf16[8,256,512]{2,1,0:T(8,128)(2,1)} %all_to_all.41.rows_ref, bf16[8,512,2048]{2,1,0:T(8,128)(2,1)} %win_ref.7, bf16[8,2048,512]{2,1,0:T(8,128)(2,1)} %wout_ref.7), custom_call_target="tpu_custom_call" | custom-call | flops 12884901888 | bytes 8388608 | tf_op jit(solution)/shard_map/one_expert/pallas_call | solution.py:371
  442.9 23.1 %all-to-all-done.5.rest_2_ = bf16[8,128,1024]{2,1,0:T(8,128)(2,1)S(1)} async-done(((bf16[8,128,1024]{2,1,0:T(8,128)(2,1)}), bf16[8,128,1024]{2,1,0:T(8,128)(2,1)S(1)}, u32[]{:S(2)}, u32[]{:S(2)}) %all-to-all-start.5) | async-done | bytes 2097184 | tf_op jit(solution)/shard_map/all_to_all | solution.py:1140
  467.4 64.6 %expert_block_backward.1 = (f32[1576,512]{1,0:T(8,128)}, f32[8,208,512]{2,1,0:T(8,128)}, bf16[512,2176]{1,0:T(8,128)(2,1)}) custom-call(f32[8,512]{1,0:T(8,128)} %copy-done.8, bf16[512,2048]{1,0:T(8,128)(2,1)} %all-gather.7.cloned.1.call-done.w_ref, bf16[512,128]{1,0:T(8,128)(2,1)} %copy-done.7, f32[8,208,512]{2,1,0:T(8,128)} %feed_forward.1.x_ref.mid_ref, ...), custom_call_target="tpu_custom_call" | custom-call | flops 60000002048 | bytes 60000000 | tf_op jit(solution)/shard_map/expert_block_backward/pallas_call | solution.py:544
  532.0 68.2 %all-reduce.12.cloned.1.call-done = (bf16[4,512,512]{2,1,0:T(8,128)(2,1)}, bf16[4,512,512]{2,1,0:T(8,128)(2,1)}) async-done(((bf16[4,512,512]{2,1,0:T(8,128)(2,1)}, bf16[4,512,512]{2,1,0:T(8,128)(2,1)}), (bf16[4,512,512]{2,1,0:T(8,128)(2,1)}, bf16[4,512,512]{2,1,0:T(8,128)(2,1)})) %all-reduce.12.cloned.1.call-update) | async-done | bytes 4194320 | tf_op jit(solution)/shard_map/psum | solution.py:1149
  600.2 66.7 %dense_block_backward.1 = (f32[1576,512]{1,0:T(8,128)}, bf16[512,4224]{1,0:T(8,128)(2,1)}, bf16[2048,512]{1,0:T(8,128)(2,1)}) custom-call(f32[8,512]{1,0:T(8,128)} %copy-done.8, bf16[512,2176]{1,0:T(8,128)(2,1)} %all-gather.5.cloned.1.call-done.w_ref, bf16[512,2048]{1,0:T(8,128)(2,1)} %all-gather.9.cloned.1.call-done.win_ref, ...), custom_call_target="tpu_custom_call" | custom-call | flops 60000002048 | bytes 60000000 | tf_op jit(solution)/shard_map/dense_block_backward/pallas_call | solution.py:646
  666.9 299.3 %sums.1 = (bf16[20,2,512,512]{3,2,1,0:T(8,128)(2,1)}, bf16[128,2176]{1,0:T(8,128)(2,1)}, bf16[128,4224]{1,0:T(8,128)(2,1)}, bf16[512,512]{1,0:T(8,128)(2,1)}, f32[8,128]{1,0:T(8,128)}) custom-call(bf16[4,512,512]{2,1,0:T(8,128)(2,1)} %get-tuple-element.74.refs_0_, bf16[4,512,512]{2,1,0:T(8,128)(2,1)} %get-tuple-element.75.refs_1_, ...), custom_call_target="tpu_custom_call" | custom-call | tf_op jit(solution)/shard_map/sums/pallas_call | solution.py:962
  980.3 34.6 %widen.1 = (f32[8,512,2048]{2,1,0:T(8,128)}, f32[8,2048,512]{2,1,0:T(8,128)}) custom-call(s32[1]{0:T(128)} %bitcast.29.core_ref, bf16[4,512,512]{2,1,0:T(8,128)(2,1)} %get-tuple-element.157.refs_0_, bf16[4,512,512]{2,1,0:T(8,128)(2,1)} %get-tuple-element.158.refs_1_, bf16[4,512,512]{2,1,0:T(8,128)(2,1)} %all-reduce.10.cloned.1.call-done.refs_2_, ...), custom_call_target="tpu_custom_call" | custom-call | tf_op jit(solution)/shard_map/widen/pallas_call | solution.py:1027
  (125 shorter events, 66.9 us)
Async XLA Ops:
  7.2 45.0 %all-gather.5.cloned.1.call-start = ((), (), s32[]{:S(2)}) async-start(), calls=%async_computation.8 | async-start | bytes 2785280 | tf_op jit(solution)/shard_map/all_gather | solution.py:1045
  11.9 3.4 copy-start.15
  12.9 76.4 %all-gather.11.cloned.1.call-start = ((), (), s32[]{:S(2)}) async-start(), calls=%async_computation.11 | async-start | bytes 2621440 | tf_op jit(solution)/shard_map/all_gather | solution.py:1045
  13.7 112.9 %all-gather.9.cloned.1.call-start = ((), (), s32[]{:S(2)}) async-start(), calls=%async_computation.10 | async-start | bytes 2621440 | tf_op jit(solution)/shard_map/all_gather | solution.py:1045
  14.4 149.8 %all-gather.7.cloned.1.call-start = ((), (), s32[]{:S(2)}) async-start(), calls=%async_computation.9 | async-start | bytes 2621440 | tf_op jit(solution)/shard_map/all_gather | solution.py:1045
  16.5 38.4 %copy-start.1 = (bf16[8,208,512]{2,1,0:T(8,128)(2,1)}, bf16[8,208,512]{2,1,0:T(8,128)(2,1)S(1)}, u32[]{:S(2)}) copy-start(bf16[8,208,512]{2,1,0:T(8,128)(2,1)S(1)} %pad.27.x_ref) | copy-start | bytes 5111812
  26.6 156.8 %copy-start = (bf16[8,208,512]{2,1,0:T(8,128)(2,1)}, bf16[8,208,512]{2,1,0:T(8,128)(2,1)S(1)}, u32[]{:S(2)}) copy-start(bf16[8,208,512]{2,1,0:T(8,128)(2,1)S(1)} %pad.28.cot_ref) | copy-start | bytes 5111812
  56.6 107.6 %copy-start.8 = (f32[8,512]{1,0:T(8,128)}, f32[8,512]{1,0:T(8,128)S(1)}, u32[]{:S(2)}) copy-start(f32[8,512]{1,0:T(8,128)S(1)} %copy.79.g_ref) | copy-start | bytes 49156
  149.0 33.2 %copy-start.7 = (bf16[512,128]{1,0:T(8,128)(2,1)}, bf16[512,128]{1,0:T(8,128)(2,1)S(1)}, u32[]{:S(2)}) copy-start(bf16[512,128]{1,0:T(8,128)(2,1)S(1)} %slice_select_fusion.wr_ref) | copy-start | bytes 393220
  149.0 34.4 %copy-start.6 = (f32[8,4,1664]{2,1,0:T(4,128)S(1)}, f32[8,4,1664]{2,1,0:T(4,128)}, u32[]{:S(2)}) copy-start(f32[8,4,1664]{2,1,0:T(4,128)} %reshape.161.pos_ref) | copy-start | bytes 638980
  183.3 26.2 %copy-start.5 = (f32[8,208,128]{2,1,0:T(8,128)}, f32[8,208,128]{2,1,0:T(8,128)S(1)}, u32[]{:S(2)}) copy-start(f32[8,208,128]{2,1,0:T(8,128)S(1)} %get-tuple-element.57.prob_ref) | copy-start | bytes 2555908
  244.1 30.5 %all-to-all-start = ((bf16[8,256,512]{2,1,0:T(8,128)(2,1)}), bf16[8,256,512]{2,1,0:T(8,128)(2,1)}, u32[]{:S(2)}, u32[]{:S(2)}) async-start(bf16[8,256,512]{2,1,0:T(8,128)(2,1)} %get-tuple-element.162), calls=%async_computation | async-start | bytes 4194304 | tf_op jit(solution)/shard_map/all_to_all | solution.py:1135
  274.6 41.4 %all-to-all-start.6 = ((bf16[8,256,512]{2,1,0:T(8,128)(2,1)}), bf16[8,256,512]{2,1,0:T(8,128)(2,1)}, u32[]{:S(2)}, u32[]{:S(2)}) async-start(bf16[8,256,512]{2,1,0:T(8,128)(2,1)} %get-tuple-element.67), calls=%async_computation.6 | async-start | bytes 4194304 | tf_op jit(solution)/shard_map/all_to_all | solution.py:1135
  316.0 29.5 %copy-start.14 = (bf16[8,128,1024]{2,1,0:T(8,128)(2,1)S(1)}, bf16[8,128,1024]{2,1,0:T(8,128)(2,1)}, u32[]{:S(2)}) copy-start(bf16[8,128,1024]{2,1,0:T(8,128)(2,1)} %get-tuple-element.64) | copy-start | bytes 6291460
  374.9 29.7 %all-to-all-start.1 = ((bf16[8,128,1024]{2,1,0:T(8,128)(2,1)}), bf16[8,128,1024]{2,1,0:T(8,128)(2,1)S(1)}, u32[]{:S(2)}, u32[]{:S(2)}) async-start(bf16[8,128,1024]{2,1,0:T(8,128)(2,1)} %get-tuple-element.63), calls=%async_computation.1 | async-start | bytes 4194304 | tf_op jit(solution)/shard_map/all_to_all | solution.py:1140
  405.9 30.5 %all-to-all-start.7 = ((bf16[8,128,1024]{2,1,0:T(8,128)(2,1)}), bf16[8,128,1024]{2,1,0:T(8,128)(2,1)}, u32[]{:S(2)}, u32[]{:S(2)}) async-start(bf16[8,128,1024]{2,1,0:T(8,128)(2,1)} %get-tuple-element.68), calls=%async_computation.7 | async-start | bytes 4194304 | tf_op jit(solution)/shard_map/all_to_all | solution.py:1140
  436.3 29.7 %all-to-all-start.5 = ((bf16[8,128,1024]{2,1,0:T(8,128)(2,1)}), bf16[8,128,1024]{2,1,0:T(8,128)(2,1)S(1)}, u32[]{:S(2)}, u32[]{:S(2)}) async-start(bf16[8,128,1024]{2,1,0:T(8,128)(2,1)} %get-tuple-element.66), calls=%async_computation.5 | async-start | bytes 4194304 | tf_op jit(solution)/shard_map/all_to_all | solution.py:1140
  439.9 160.2 %all-reduce.12.cloned.1.call-start = ((), (), s32[]{:S(2)}) async-start(), calls=%async_computation.13 | async-start | bytes 8388608 | tf_op jit(solution)/shard_map/psum | solution.py:1149
  442.9 526.8 %all-reduce.10.cloned.1.call-start = ((), (), s32[]{:S(2)}) async-start(), calls=%async_computation.12 | async-start | bytes 4194304 | tf_op jit(solution)/shard_map/psum | solution.py:1149
  966.3 3.7 copy-start.20
  969.1 11.3 %collective-permute-start = (bf16[4,512,512]{2,1,0:T(8,128)(2,1)}, bf16[4,512,512]{2,1,0:T(8,128)(2,1)}, u32[]{:S(2)}, u32[]{:S(2)}) collective-permute-start(bf16[4,512,512]{2,1,0:T(8,128)(2,1)} %get-tuple-element.157.refs_0_), channel_id=1, source_target_pairs={{0,4},{4,0},{1,5},{5,1},{2,6},{6,2},{3,7},{7,3},{8,12},{12,8},{9,1... | collective-permute-start | bytes 6291464 | tf_op jit(solution)/shard_map/ppermute | solution.py:1150
  969.5 10.8 %collective-permute-start.1 = (bf16[4,512,512]{2,1,0:T(8,128)(2,1)}, bf16[4,512,512]{2,1,0:T(8,128)(2,1)}, u32[]{:S(2)}, u32[]{:S(2)}) collective-permute-start(bf16[4,512,512]{2,1,0:T(8,128)(2,1)} %get-tuple-element.158.refs_1_), channel_id=1, source_target_pairs={{0,4},{4,0},{1,5},{5,1},{2,6},{6,2},{3,7},{7,3},{8,12},{12,8},{9,1... | collective-permute-start | bytes 6291464 | tf_op jit(solution)/shard_map/ppermute | solution.py:1150
  969.6 10.7 %collective-permute-start.2 = (bf16[4,512,512]{2,1,0:T(8,128)(2,1)}, bf16[4,512,512]{2,1,0:T(8,128)(2,1)}, u32[]{:S(2)}, u32[]{:S(2)}) collective-permute-start(bf16[4,512,512]{2,1,0:T(8,128)(2,1)} %all-reduce.10.cloned.1.call-done.refs_2_), channel_id=1, source_target_pairs={{0,4},{4,0},{1,5},{5,1},{2,6},{6,2},{3,7},{7,3},{8,12},{12,8},{9,1... | collective-permute-start | bytes 6291464 | tf_op jit(solution)/shard_map/ppermute | solution.py:1150
  975.9 3.3 copy-start.16
  (11 other events, 18.1 us)
Sparse Core Ops, SparseCore 0:
  13.0 39.0 all-gather.4
  54.0 35.3 all-gather.10
  91.2 35.2 all-gather.8
  128.8 35.3 all-gather.6
  443.5 156.6 all-reduce.11
  602.5 95.7 all-reduce.9

commit v2 on v1

--- a/solution.py
+++ b/solution.py
@@ -394,7 +394,7 @@
             sds((FF // wide, wide, D), NARROW),
         ],
         compiler_params=params(56),
-        cost_estimate=cost(12 * senders * CAP * D * FF, 8 * D * FF),
+        cost_estimate=cost(5e9, 1),
         name="one_expert",
     )(pick, rows, win, wout)
 
@@ -573,7 +573,7 @@
             pltpu.VMEM((D, 4 * D), WIDE),
         ],
         compiler_params=params(56),
-        cost_estimate=cost(60e9, 60e6),
+        cost_estimate=cost(1e6, 1),
         name="expert_block_backward",
     )(gains, w1, wr, mid, second, cot, prob, aux, qkv, mixed, *tables)
 
@@ -674,7 +674,7 @@
             pltpu.VMEM((FF, D), WIDE),
         ],
         compiler_params=params(56),
-        cost_estimate=cost(60e9, 60e6),
+        cost_estimate=cost(1e6, 1),
         name="dense_block_backward",
     )(gains, w0, win, wout, x, first, grad, qkv, mixed)
 
@@ -1039,6 +1039,107 @@
         compiler_params=params(56),
         name="widen",
     )(core, *own, *other, late, late)
+
+
+def gather_kernel(groups, q_ref, k_ref, v_ref, o_ref, small_ref, in_ref, out_ref, *refs):
+    w_all, small_all, in_all, out_all, send, recv, pass_send, pass_recv, copy = refs
+    z, core, f = lax.axis_index("z"), lax.axis_index("core"), lax.axis_index("fsdp")
+    barrier = pltpu.get_barrier_semaphore()
+    for d in range(1, groups):
+        pl.semaphore_signal(
+            barrier, inc=1, device_id=(z, core, lax.rem(f + d, groups)), device_id_type=MESH_ID
+        )
+    pl.semaphore_signal(barrier, inc=1, device_id=(z, 1 - core, f), device_id_type=MESH_ID)
+    pl.semaphore_wait(barrier, groups)
+
+    def rows(count, owner, side):
+        half = count // CORES
+        return pl.ds(pl.multiple_of(owner * count + side * half, 16), half)
+
+    def item(n):
+        if n < 4:
+            ref = (q_ref, k_ref, v_ref, o_ref)[n]
+            count = ref.shape[1]
+            cols = pl.ds(n * D, D)
+            return (
+                lambda side: ref.at[0, rows(count, 0, side), :],
+                lambda owner, side: w_all.at[rows(count, owner, side), cols],
+            )
+        ref, full = ((small_ref, small_all), (in_ref, in_all), (out_ref, out_all))[n - 4]
+        count = ref.shape[0]
+        return (
+            lambda side: ref.at[rows(count, 0, side), :],
+            lambda owner, side: full.at[rows(count, owner, side), :],
+        )
+
+    def fetch(n, d):
+        source, place = item(n)
+        return pltpu.make_async_remote_copy(
+            src_ref=source(core),
+            dst_ref=place(f, core),
+            send_sem=send.at[n, d],
+            recv_sem=recv.at[n, d],
+            device_id=(z, core, lax.rem(f + d, groups)),
+            device_id_type=MESH_ID,
+        )
+
+    def hand_on(n, d):
+        _, place = item(n)
+        there = place(lax.rem(f + groups - d, groups), core)
+        return pltpu.make_async_remote_copy(
+            src_ref=there,
+            dst_ref=there,
+            send_sem=pass_send.at[n, d],
+            recv_sem=pass_recv.at[n, d],
+            device_id=(z, 1 - core, f),
+            device_id_type=MESH_ID,
+        )
+
+    def keep(n, side):
+        source, place = item(n)
+        return pltpu.make_async_copy(source(side), place(f, side), copy.at[n, side])
+
+    count = 7
+    for n in range(count):
+        for d in range(1, groups):
+            fetch(n, d).start()
+    for n in range(count):
+        for side in range(CORES):
+            keep(n, side).start()
+    for n in range(count):
+        for d in range(1, groups):
+            fetch(n, d).wait_recv()
+            hand_on(n, d).start()
+    for n in range(count):
+        for side in range(CORES):
+            keep(n, side).wait()
+        for d in range(1, groups):
+            fetch(n, d).wait_send()
+            hand_on(n, d).wait()
+
+
+def gather_dense(query_w, key_w, value_w, output_w, small, mlp_in, mlp_out, groups):
+    any_space = pl.BlockSpec(memory_space=pl.ANY)
+    dma = pltpu.SemaphoreType.DMA
+    return pl.pallas_call(
+        partial(gather_kernel, groups),
+        in_specs=[any_space] * 7,
+        out_specs=[any_space] * 4,
+        out_shape=[
+            sds((D, 4 * D), NARROW),
+            sds((D, 128), NARROW),
+            sds((D, FF), NARROW),
+            sds((FF, D), NARROW),
+        ],
+        scratch_shapes=[
+            *[dma((7, groups)) for _ in range(4)],
+            dma((7, CORES)),
+        ],
+        compiler_params=pltpu.CompilerParams(
+            vmem_limit_bytes=8 * MIB, collective_id=5, has_side_effects=True
+        ),
+        name="gather_weights",
+    )(query_w, key_w, value_w, output_w, small, mlp_in, mlp_out)
 
 
 def gather(x):
@@ -1085,11 +1186,10 @@
         ],
         1,
     )
-    w0 = gather(jnp.concatenate([query_w[0], key_w[0], value_w[0], output_w[0], small], 1))
-    win = gather(mlp_in)
-    wout = gather(mlp_out)
+    w0, w_small, win, wout = gather_dense(
+        query_w, key_w, value_w, output_w, small, mlp_in, mlp_out, groups
+    )
     w1 = gather(jnp.concatenate([query_w[1], key_w[1], value_w[1], output_w[1]], 1))
-    w_small = w0[:, 4 * D :]
     wr = jnp.where(jnp.arange(128)[None, :] < EXPERTS, w_small, 0)
     gains = jnp.pad(
         jnp.transpose(w_small[:, EXPERTS : EXPERTS + 4]).astype(WIDE), ((0, 4), (0, 0))
@@ -1140,13 +1240,8 @@
             lax.all_to_all(back, ("core", "fsdp"), split_axis=0, concat_axis=0, tiled=True)
         )
         mats += [d_in, d_out]
-    early = len(mats) * 3 // 8
-    mats, ready, others = list(mats), [], []
-    for n in range(0, early, 2):
-        batch = mats[n : min(n + 2, early)]
-        if ready:
-            batch, _ = lax.optimization_barrier((batch, ready))
-        ready += lax.psum(batch, "z")
+    early = len(mats) // 2
+    ready = lax.psum(mats[:early], "z")
     others = [lax.ppermute(mat, "core", [(0, 1), (1, 0)]) for mat in ready]
 
     y, mid_grad, dw1 = moe_bwd(

time: 1020 us -> 867 us (0.85)
  waiting for transfers between devices: 193 us -> 54.6 us
  blocking collectives: 88.3 us -> 61.5 us
    all_gather x4 -> x1, waiting for transfers between devices: 95.2 us -> 0.02 us  [gather(): return lax.all_gather(x, 'fsdp', axis=0, tiled=True)]
    psum x2 -> x1, waiting for transfers between devices: 68.2 us -> 0.02 us  [local(): ready = lax.psum(mats[:early], 'z')]
    pallas_call x0 -> x1, Pallas kernels: none -> 54.3 us  [gather_dense(): pl.pallas_call(partial(gather_kernel, groups), in_specs=[any_space] * 7,...]
    pallas_call x1, Pallas kernels: 299 us -> 251 us  [sum_all(): pl.pallas_call(partial(sum_kernel, nz, groups, len(mats), slices), in_spe...]
    all_to_all x2 -> x1, blocking collectives: 58.9 us -> 30.9 us  [local(): lax.all_to_all(chunk, ('core', 'fsdp'), split_axis=0, concat_axis=0, tile...]
    all_to_all x2 -> x3, waiting for transfers between devices: 2.6 us -> 27.8 us  [local(): lax.all_to_all(chunk, ('core', 'fsdp'), split_axis=0, concat_axis=0, tile...]
    all_to_all x2 -> x3, starting transfers between devices: 19.9 us -> 22 us  [local(): lax.all_to_all(chunk, ('core', 'fsdp'), split_axis=0, concat_axis=0, tile...]
  transfers between devices with their start and end apart: 14 -> 12, of which waited for: 10 -> 7; matrix products, arithmetic and copies ran while one was open for 3% -> 4% of each run, Pallas kernels for 55% -> 66%
where the time goes in v2:
time: 867 us; the launch traced here: 864 us
  Pallas kernels  648 us (75%)
  blocking collectives  61.5 us (7%)
  waiting for transfers between devices  54.6 us (6%)
  local copies, waits for them, and re-layouts  38.7 us (4%)
  starting transfers between devices  34.8 us (4%)
  between operations  14.8 us (2%)
  other arithmetic  11.6 us (1%)
    pallas_call x1, Pallas kernels, sum_all(): pl.pallas_call(partial(sum_kernel, nz, groups, len(mats), slices), in_spe...  251 us
    pallas_call x4, Pallas kernels, expert(): pl.pallas_call(expert_kernel, grid_spec=pltpu.PrefetchScalarGridSpec(num_...  98.7 us
    pallas_call x1, Pallas kernels, dense_bwd(): pl.pallas_call(partial(dense_bwd_kernel, ib), grid=(images // ib,), in_sp...  66.8 us
    pallas_call x1, Pallas kernels, moe_bwd(): pl.pallas_call(partial(moe_bwd_kernel, ib, len(tables)), grid=(images //...  64.6 us
    pallas_call x1, Pallas kernels, gather_dense(): pl.pallas_call(partial(gather_kernel, groups), in_specs=[any_space] * 7,...  54.3 us
    pallas_call x1, Pallas kernels, widen(): pl.pallas_call(partial(widen_kernel, early), grid_spec=pltpu.PrefetchScal...  34.1 us
    all_to_all x1, blocking collectives, local(): lax.all_to_all(chunk, ('core', 'fsdp'), split_axis=0, concat_axis=0, tile...  30.9 us
    all_to_all x1, blocking collectives, local(): lax.all_to_all(back, ('core', 'fsdp'), split_axis=0, concat_axis=0, tiled...  30.6 us
  transfers between devices with their start and end apart: 12, of which 7 were waited for; matrix products, arithmetic and copies ran while one was open for 4% of the time, Pallas kernels for 66%

profile of v2, /device:TPU:0, one launch (start us, length us, event | category | flops | bytes accessed | tf_op | source)
XLA Modules:
  0.0 864.3 jit_solution(8398078254661017082)
XLA Ops:
  11.0 54.3 %gather_weights.1 = (bf16[512,2048]{1,0:T(8,128)(2,1)S(1)}, bf16[512,128]{1,0:T(8,128)(2,1)S(1)}, bf16[512,2048]{1,0:T(8,128)(2,1)S(1)}, bf16[2048,512]{1,0:T(8,128)(2,1)S(1)}) custom-call(bf16[2,128,512]{2,1,0:T(8,128)(2,1)S(1)} %copy-done.14, bf16[2,128,512]{2,1,0:T(8,128)(2,1)S(1)} %copy-done.15, bf16[2,128,512]{2,1,0:T(8,128)(2,1)S(1)} %copy-done.16, ...), custom_call_target="tpu_custom_call" | custom-call | tf_op jit(solution)/shard_map/gather_weights/pallas_call | solution.py:1124
  83.9 14.0 %dense_attention.1 = (f32[8,208,512]{2,1,0:T(8,128)}, bf16[8,208,1536]{2,1,0:T(8,128)(2,1)}, bf16[8,208,512]{2,1,0:T(8,128)(2,1)S(1)}, f32[8,8,128]{2,1,0:T(8,128)S(1)}) custom-call(bf16[8,208,512]{2,1,0:T(8,128)(2,1)S(1)} %pad.27.x_ref, f32[8,512]{1,0:T(8,128)S(1)} %pad_convert_fusion.g_ref, bf16[512,2048]{1,0:T(8,128)(2,1)S(1)} %copy-done.3), custom_call_target="tpu_custom_call" | custom-call | tf_op jit(solution)/shard_map/dense_attention/pallas_call | solution.py:177
  97.9 19.0 %feed_forward.1.x_ref.mid_ref = f32[8,208,512]{2,1,0:T(8,128)} custom-call(f32[8,208,512]{2,1,0:T(8,128)} %get-tuple-element.60.x_ref.first_ref, f32[8,512]{1,0:T(8,128)S(1)} %pad_convert_fusion.g_ref, bf16[512,2048]{1,0:T(8,128)(2,1)S(1)} %copy-done.5, bf16[2048,512]{1,0:T(8,128)(2,1)S(1)} %copy-done.7), custom_call_target="tpu_custom_call" | custom-call | tf_op jit(solution)/shard_map/feed_forward/pallas_call | solution.py:199
  117.0 18.3 %expert_attention.1 = (f32[8,208,512]{2,1,0:T(8,128)}, bf16[8,208,1536]{2,1,0:T(8,128)(2,1)}, bf16[8,208,512]{2,1,0:T(8,128)(2,1)S(1)}, f32[8,8,128]{2,1,0:T(8,1...) custom-call(f32[8,208,512]{2,1,0:T(8,128)} %feed_forward.1.x_ref.mid_ref, ...), custom_call_target="tpu_custom_call" | custom-call | tf_op jit(solution)/shard_map/expert_attention/pallas_call | solution.py:211
  136.5 25.8 %dispatch.1 = bf16[32,256,512]{2,1,0:T(8,128)(2,1)} custom-call(f32[8,4,1664]{2,1,0:T(4,128)S(1)} %copy-done.12, s32[8,4,128]{2,1,0:T(4,128)S(1)} %broadcast_in_dim.40.order_ref, bf16[1664,512]{1,0:T(8,128)(2,1)S(1)} %bitcast.53, bf16[1664,512]{1,0:T(8,128)(2,1)S(1)} %bitcast.51, f32[1664,128]{1,0:T(8,128)S(1)} %bitcast.52), custom_call_target="tpu_custom_call" | custom-call | tf_op jit(solution)/shard_map/dispatch/pallas_call | solution.py:309
  162.4 5.7 fusion.18
  168.1 30.9 %all_to_all.40.rows_ref = bf16[8,256,512]{2,1,0:T(8,128)(2,1)} all-to-all(bf16[8,256,512]{2,1,0:T(8,128)(2,1)S(1)} %get-tuple-element.154), channel_id=1, replica_groups=mesh['z'=4,'core'=2,'fsdp'=4] {'core','fsdp'}, dimensions={0} | all-to-all | bytes 4194304 | tf_op jit(solution)/shard_map/all_to_all | solution.py:1235
  199.0 3.6 all-to-all-start
  202.6 24.7 %one_expert.5 = (bf16[8,128,1024]{2,1,0:T(8,128)(2,1)}, bf16[4,512,512]{2,1,0:T(8,128)(2,1)}, bf16[4,512,512]{2,1,0:T(8,128)(2,1)}) custom-call(s32[1]{0:T(128)} %bitcast.13.pick, bf16[8,256,512]{2,1,0:T(8,128)(2,1)} %all_to_all.40.rows_ref, bf16[8,512,2048]{2,1,0:T(8,128)(2,1)} %win_ref.7, bf16[8,2048,512]{2,1,0:T(8,128)(2,1)} %wout_ref.7), custom_call_target="tpu_custom_call" | custom-call | flops 5000000000 | bytes 1 | tf_op jit(solution)/shard_map/one_expert/pallas_call | solution.py:371
  230.0 14.8 %all-to-all-start.6 = ((bf16[8,256,512]{2,1,0:T(8,128)(2,1)}), bf16[8,256,512]{2,1,0:T(8,128)(2,1)S(1)}, u32[]{:S(2)}, u32[]{:S(2)}) async-start(bf16[8,256,512]{2,1,0:T(8,128)(2,1)} %get-tuple-element.74), calls=%async_computation.6 | async-start | bytes 4194304 | tf_op jit(solution)/shard_map/all_to_all | solution.py:1235
  244.7 24.7 %one_expert.4 = (bf16[8,128,1024]{2,1,0:T(8,128)(2,1)}, bf16[4,512,512]{2,1,0:T(8,128)(2,1)}, bf16[4,512,512]{2,1,0:T(8,128)(2,1)}) custom-call(s32[1]{0:T(128)} %bitcast.9.pick, bf16[8,256,512]{2,1,0:T(8,128)(2,1)} %copy-done.26, bf16[8,512,2048]{2,1,0:T(8,128)(2,1)} %win_ref.7, bf16[8,2048,512]{2,1,0:T(8,128)(2,1)} %wout_ref.7), custom_call_target="tpu_custom_call" | custom-call | flops 5000000000 | bytes 1 | tf_op jit(solution)/shard_map/one_expert/pallas_call | solution.py:371
  271.8 3.6 all-to-all-start.4
  276.2 25.3 %all-to-all-done.4.rows_ref = bf16[8,256,512]{2,1,0:T(8,128)(2,1)S(1)} async-done(((bf16[8,256,512]{2,1,0:T(8,128)(2,1)}), bf16[8,256,512]{2,1,0:T(8,128)(2,1)S(1)}, u32[]{:S(2)}, u32[]{:S(2)}) %all-to-all-start.4) | async-done | bytes 2097184 | tf_op jit(solution)/shard_map/all_to_all | solution.py:1235
  301.5 30.6 %all_to_all.41.rest_1_ = bf16[8,128,1024]{2,1,0:T(8,128)(2,1)} all-to-all(bf16[8,128,1024]{2,1,0:T(8,128)(2,1)} %get-tuple-element.71), channel_id=1, replica_groups=mesh['z'=4,'core'=2,'fsdp'=4] {'core','fsdp'}, dimensions={0} | all-to-all | bytes 4194304 | tf_op jit(solution)/shard_map/all_to_all | solution.py:1240
  332.1 3.6 all-to-all-start.1
  335.7 24.7 %one_expert.7 = (bf16[8,128,1024]{2,1,0:T(8,128)(2,1)}, bf16[4,512,512]{2,1,0:T(8,128)(2,1)}, bf16[4,512,512]{2,1,0:T(8,128)(2,1)}) custom-call(s32[1]{0:T(128)} %bitcast.15.pick, bf16[8,256,512]{2,1,0:T(8,128)(2,1)} %copy-done.24, bf16[8,512,2048]{2,1,0:T(8,128)(2,1)} %win_ref.7, bf16[8,2048,512]{2,1,0:T(8,128)(2,1)} %wout_ref.7), custom_call_target="tpu_custom_call" | custom-call | flops 5000000000 | bytes 1 | tf_op jit(solution)/shard_map/one_expert/pallas_call | solution.py:371
  363.0 4.3 all-to-all-start.7
  367.4 24.7 %one_expert.6 = (bf16[8,128,1024]{2,1,0:T(8,128)(2,1)}, bf16[4,512,512]{2,1,0:T(8,128)(2,1)}, bf16[4,512,512]{2,1,0:T(8,128)(2,1)}) custom-call(s32[1]{0:T(128)} %bitcast.14.pick, bf16[8,256,512]{2,1,0:T(8,128)(2,1)} %copy-done.23, bf16[8,512,2048]{2,1,0:T(8,128)(2,1)} %win_ref.7, bf16[8,2048,512]{2,1,0:T(8,128)(2,1)} %wout_ref.7), custom_call_target="tpu_custom_call" | custom-call | flops 5000000000 | bytes 1 | tf_op jit(solution)/shard_map/one_expert/pallas_call | solution.py:371
  393.5 3.7 all-to-all-start.5
  402.2 21.1 %all-to-all-done.5.rest_2_ = bf16[8,128,1024]{2,1,0:T(8,128)(2,1)S(1)} async-done(((bf16[8,128,1024]{2,1,0:T(8,128)(2,1)}), bf16[8,128,1024]{2,1,0:T(8,128)(2,1)S(1)}, u32[]{:S(2)}, u32[]{:S(2)}) %all-to-all-start.5) | async-done | bytes 2097184 | tf_op jit(solution)/shard_map/all_to_all | solution.py:1240
  424.6 64.6 %expert_block_backward.1 = (f32[1576,512]{1,0:T(8,128)}, f32[8,208,512]{2,1,0:T(8,128)}, bf16[512,2176]{1,0:T(8,128)(2,1)}) custom-call(f32[8,512]{1,0:T(8,128)} %copy-done.13, bf16[512,2048]{1,0:T(8,128)(2,1)} %all-gather.2.cloned.1.call-done.w_ref, bf16[512,128]{1,0:T(8,128)(2,1)} %copy-done.11, f32[8,208,512]{2,1,0:T(8,128)} %feed_forward.1.x_ref.mid_ref, ...), custom_call_target="tpu_custom_call" | custom-call | flops 1000000 | bytes 1 | tf_op jit(solution)/shard_map/expert_block_backward/pallas_call | solution.py:544
  489.2 66.8 %dense_block_backward.1 = (f32[1576,512]{1,0:T(8,128)}, bf16[512,4224]{1,0:T(8,128)(2,1)}, bf16[2048,512]{1,0:T(8,128)(2,1)}) custom-call(f32[8,512]{1,0:T(8,128)} %copy-done.13, bf16[512,2048]{1,0:T(8,128)(2,1)} %copy-done.2, bf16[512,2048]{1,0:T(8,128)(2,1)} %copy-done.4, bf16[2048,512]{1,0:T(8,128)(2,1)} %copy-done.6, bf16[8,208,512]{2,1,0:T(8,128)(2,1)} %copy-done.1, ...), custom_call_target="tpu_custom_call" | custom-call | flops 1000000 | bytes 1 | tf_op jit(solution)/shard_map/dense_block_backward/pallas_call | solution.py:646
  556.0 250.6 %sums.1 = (bf16[16,2,512,512]{3,2,1,0:T(8,128)(2,1)}, bf16[128,2176]{1,0:T(8,128)(2,1)}, bf16[128,4224]{1,0:T(8,128)(2,1)}, bf16[512,512]{1,0:T(8,128)(2,1)}, f32[8,128]{1,0:T(8,128)}) custom-call(bf16[4,512,512]{2,1,0:T(8,128)(2,1)} %get-tuple-element.81.refs_0_, bf16[4,512,512]{2,1,0:T(8,128)(2,1)} %get-tuple-element.82.refs_1_, ...), custom_call_target="tpu_custom_call" | custom-call | tf_op jit(solution)/shard_map/sums/pallas_call | solution.py:962
  823.1 34.1 %widen.1 = (f32[8,512,2048]{2,1,0:T(8,128)}, f32[8,2048,512]{2,1,0:T(8,128)}) custom-call(s32[1]{0:T(128)} %bitcast.25.core_ref, bf16[4,512,512]{2,1,0:T(8,128)(2,1)} %get-tuple-element.148.refs_0_, bf16[4,512,512]{2,1,0:T(8,128)(2,1)} %get-tuple-element.149.refs_1_, bf16[4,512,512]{2,1,0:T(8,128)(2,1)} %get-tuple-element.150.refs_2_, ...), custom_call_target="tpu_custom_call" | custom-call | tf_op jit(solution)/shard_map/widen/pallas_call | solution.py:1027
  (152 shorter events, 55.9 us)
Async XLA Ops:
  7.3 109.7 %all-gather.2.cloned.1.call-start = ((), (), s32[]{:S(2)}) async-start(), calls=%async_computation.8 | async-start | bytes 2621440 | tf_op jit(solution)/shard_map/all_gather | solution.py:1146
  72.7 11.1 %copy-start.1 = (bf16[8,208,512]{2,1,0:T(8,128)(2,1)}, bf16[8,208,512]{2,1,0:T(8,128)(2,1)S(1)}, u32[]{:S(2)}) copy-start(bf16[8,208,512]{2,1,0:T(8,128)(2,1)S(1)} %pad.27.x_ref) | copy-start | bytes 5111812
  72.8 10.1 %copy-start.30 = (s32[8,208,2]{1,0,2:T(8,128)}, s32[8,208,2]{1,0,2:T(8,128)S(1)}, u32[]{:S(2)}) copy-start(s32[8,208,2]{1,0,2:T(8,128)S(1)} %pad.29) | copy-start | bytes 39940
  81.2 16.7 %copy-start.7 = (bf16[2048,512]{1,0:T(8,128)(2,1)S(1)}, bf16[2048,512]{1,0:T(8,128)(2,1)}, u32[]{:S(2)}) copy-start(bf16[2048,512]{1,0:T(8,128)(2,1)} %copy-done.6) | copy-start | bytes 6291460
  82.9 53.6 %copy-start = (bf16[8,208,512]{2,1,0:T(8,128)(2,1)}, bf16[8,208,512]{2,1,0:T(8,128)(2,1)S(1)}, u32[]{:S(2)}) copy-start(bf16[8,208,512]{2,1,0:T(8,128)(2,1)S(1)} %pad.28.cot_ref) | copy-start | bytes 5111812
  82.9 14.9 %copy-start.5 = (bf16[512,2048]{1,0:T(8,128)(2,1)S(1)}, bf16[512,2048]{1,0:T(8,128)(2,1)}, u32[]{:S(2)}) copy-start(bf16[512,2048]{1,0:T(8,128)(2,1)} %copy-done.4) | copy-start | bytes 6291460
  83.8 33.1 %copy-start.13 = (f32[8,512]{1,0:T(8,128)}, f32[8,512]{1,0:T(8,128)S(1)}, u32[]{:S(2)}) copy-start(f32[8,512]{1,0:T(8,128)S(1)} %pad_convert_fusion.g_ref) | copy-start | bytes 49156
  97.8 19.0 %copy-start.9 = (bf16[8,208,512]{2,1,0:T(8,128)(2,1)}, bf16[8,208,512]{2,1,0:T(8,128)(2,1)S(1)}, u32[]{:S(2)}) copy-start(bf16[8,208,512]{2,1,0:T(8,128)(2,1)S(1)} %get-tuple-element.79.mixed_ref) | copy-start | bytes 5111812
  97.8 19.0 %copy-start.20 = (f32[8,8,128]{2,1,0:T(8,128)}, f32[8,8,128]{2,1,0:T(8,128)S(1)}, u32[]{:S(2)}) copy-start(f32[8,8,128]{2,1,0:T(8,128)S(1)} %get-tuple-element.88) | copy-start | bytes 98308
  116.9 18.4 %copy-start.11 = (bf16[512,128]{1,0:T(8,128)(2,1)}, bf16[512,128]{1,0:T(8,128)(2,1)S(1)}, u32[]{:S(2)}) copy-start(bf16[512,128]{1,0:T(8,128)(2,1)S(1)} %broadcast_select_fusion.wr_ref) | copy-start | bytes 393220
  116.9 19.6 %copy-start.12 = (f32[8,4,1664]{2,1,0:T(4,128)S(1)}, f32[8,4,1664]{2,1,0:T(4,128)}, u32[]{:S(2)}) copy-start(f32[8,4,1664]{2,1,0:T(4,128)} %reshape.161.pos_ref) | copy-start | bytes 638980
  136.5 25.9 %copy-start.8 = (f32[8,208,128]{2,1,0:T(8,128)}, f32[8,208,128]{2,1,0:T(8,128)S(1)}, u32[]{:S(2)}) copy-start(f32[8,208,128]{2,1,0:T(8,128)S(1)} %get-tuple-element.64.prob_ref) | copy-start | bytes 2555908
  199.0 29.7 %all-to-all-start = ((bf16[8,256,512]{2,1,0:T(8,128)(2,1)}), bf16[8,256,512]{2,1,0:T(8,128)(2,1)S(1)}, u32[]{:S(2)}, u32[]{:S(2)}) async-start(bf16[8,256,512]{2,1,0:T(8,128)(2,1)} %get-tuple-element.155), calls=%async_computation | async-start | bytes 4194304 | tf_op jit(solution)/shard_map/all_to_all | solution.py:1235
  230.0 40.6 %all-to-all-start.6 = ((bf16[8,256,512]{2,1,0:T(8,128)(2,1)}), bf16[8,256,512]{2,1,0:T(8,128)(2,1)S(1)}, u32[]{:S(2)}, u32[]{:S(2)}) async-start(bf16[8,256,512]{2,1,0:T(8,128)(2,1)} %get-tuple-element.74), calls=%async_computation.6 | async-start | bytes 4194304 | tf_op jit(solution)/shard_map/all_to_all | solution.py:1235
  271.8 29.7 %all-to-all-start.4 = ((bf16[8,256,512]{2,1,0:T(8,128)(2,1)}), bf16[8,256,512]{2,1,0:T(8,128)(2,1)S(1)}, u32[]{:S(2)}, u32[]{:S(2)}) async-start(bf16[8,256,512]{2,1,0:T(8,128)(2,1)} %get-tuple-element.72), calls=%async_computation.4 | async-start | bytes 4194304 | tf_op jit(solution)/shard_map/all_to_all | solution.py:1235
  275.5 534.1 %all-reduce.9.cloned.1.call-start = ((), (), s32[]{:S(2)}) async-start(), calls=%async_computation.9 | async-start | bytes 16777216 | tf_op jit(solution)/shard_map/psum | solution.py:1244
  301.5 30.6 %copy-start.23 = (bf16[8,256,512]{2,1,0:T(8,128)(2,1)}, bf16[8,256,512]{2,1,0:T(8,128)(2,1)S(1)}, u32[]{:S(2)}) copy-start(bf16[8,256,512]{2,1,0:T(8,128)(2,1)S(1)} %all-to-all-done.4.rows_ref) | copy-start | bytes 6291460
  332.1 29.7 %all-to-all-start.1 = ((bf16[8,128,1024]{2,1,0:T(8,128)(2,1)}), bf16[8,128,1024]{2,1,0:T(8,128)(2,1)S(1)}, u32[]{:S(2)}, u32[]{:S(2)}) async-start(bf16[8,128,1024]{2,1,0:T(8,128)(2,1)} %get-tuple-element.70), calls=%async_computation.1 | async-start | bytes 4194304 | tf_op jit(solution)/shard_map/all_to_all | solution.py:1240
  363.0 30.5 %all-to-all-start.7 = ((bf16[8,128,1024]{2,1,0:T(8,128)(2,1)}), bf16[8,128,1024]{2,1,0:T(8,128)(2,1)}, u32[]{:S(2)}, u32[]{:S(2)}) async-start(bf16[8,128,1024]{2,1,0:T(8,128)(2,1)} %get-tuple-element.75), calls=%async_computation.7 | async-start | bytes 4194304 | tf_op jit(solution)/shard_map/all_to_all | solution.py:1240
  393.5 29.8 %all-to-all-start.5 = ((bf16[8,128,1024]{2,1,0:T(8,128)(2,1)}), bf16[8,128,1024]{2,1,0:T(8,128)(2,1)S(1)}, u32[]{:S(2)}, u32[]{:S(2)}) async-start(bf16[8,128,1024]{2,1,0:T(8,128)(2,1)} %get-tuple-element.73), calls=%async_computation.5 | async-start | bytes 4194304 | tf_op jit(solution)/shard_map/all_to_all | solution.py:1240
  809.5 11.4 %collective-permute-start = (bf16[4,512,512]{2,1,0:T(8,128)(2,1)}, bf16[4,512,512]{2,1,0:T(8,128)(2,1)}, u32[]{:S(2)}, u32[]{:S(2)}) collective-permute-start(bf16[4,512,512]{2,1,0:T(8,128)(2,1)} %get-tuple-element.148.refs_0_), channel_id=1, source_target_pairs={{0,4},{4,0},{1,5},{5,1},{2,6},{6,2},{3,7},{7,3},{8,12},{12,8},{9,1... | collective-permute-start | bytes 6291464 | tf_op jit(solution)/shard_map/ppermute | solution.py:1245
  810.0 11.0 %collective-permute-start.1 = (bf16[4,512,512]{2,1,0:T(8,128)(2,1)}, bf16[4,512,512]{2,1,0:T(8,128)(2,1)}, u32[]{:S(2)}, u32[]{:S(2)}) collective-permute-start(bf16[4,512,512]{2,1,0:T(8,128)(2,1)} %get-tuple-element.149.refs_1_), channel_id=1, source_target_pairs={{0,4},{4,0},{1,5},{5,1},{2,6},{6,2},{3,7},{7,3},{8,12},{12,8},{9,1... | collective-permute-start | bytes 6291464 | tf_op jit(solution)/shard_map/ppermute | solution.py:1245
  810.1 10.8 %collective-permute-start.2 = (bf16[4,512,512]{2,1,0:T(8,128)(2,1)}, bf16[4,512,512]{2,1,0:T(8,128)(2,1)}, u32[]{:S(2)}, u32[]{:S(2)}) collective-permute-start(bf16[4,512,512]{2,1,0:T(8,128)(2,1)} %get-tuple-element.150.refs_2_), channel_id=1, source_target_pairs={{0,4},{4,0},{1,5},{5,1},{2,6},{6,2},{3,7},{7,3},{8,12},{12,8},{9,1... | collective-permute-start | bytes 6291464 | tf_op jit(solution)/shard_map/ppermute | solution.py:1245
  810.5 12.6 %collective-permute-start.3 = (bf16[4,512,512]{2,1,0:T(8,128)(2,1)}, bf16[4,512,512]{2,1,0:T(8,128)(2,1)}, u32[]{:S(2)}, u32[]{:S(2)}) collective-permute-start(bf16[4,512,512]{2,1,0:T(8,128)(2,1)} %get-tuple-element.151.refs_3_), channel_id=1, source_target_pairs={{0,4},{4,0},{1,5},{5,1},{2,6},{6,2},{3,7},{7,3},{8,12},{12,8},{9,1... | collective-permute-start | bytes 6291464 | tf_op jit(solution)/shard_map/ppermute | solution.py:1245
  (26 other events, 69.6 us)
Sparse Core Ops, SparseCore 0:
  10.5 56.9 all-gather.1
  279.2 301.9 all-reduce.8

commit v3 on v2

--- a/solution.py
+++ b/solution.py
@@ -324,6 +324,15 @@
     )(pos.reshape(groups, GROUP, tokens), order.reshape(groups, GROUP, 128), moe, cot, prob)
 
 
+def expert_math(slots, grads, win, wout):
+    pre = nn(slots, win)
+    hidden_grad = nt(grads, wout)
+    cdf, bell = normal_parts(pre)
+    hidden = (pre * cdf).astype(NARROW)
+    pre_grad = ((cdf + pre * (bell * INV_ROOT)) * hidden_grad).astype(NARROW)
+    return nn(hidden, wout), nt(pre_grad, win), tn(slots, pre_grad), tn(hidden, grads)
+
+
 def expert_kernel(pick, rows_ref, win_ref, wout_ref, back_ref, din_ref, dout_ref, res, sgr):
     f = pl.program_id(0)
     senders = rows_ref.shape[0]
@@ -335,14 +344,7 @@
         slots = rows_ref[first : first + part, 0:CAP, :].reshape(count, D)
         grads = rows_ref[first : first + part, CAP : 2 * CAP, :].reshape(count, D)
         r = slice(first * CAP, (first + part) * CAP)
-        pre = nn(slots, win)
-        hidden_grad = nt(grads, wout)
-        cdf, bell = normal_parts(pre)
-        hidden = (pre * cdf).astype(NARROW)
-        pre_grad = ((cdf + pre * (bell * INV_ROOT)) * hidden_grad).astype(NARROW)
-        result = nn(hidden, wout)
-        slot_grad = nt(pre_grad, win)
-        in_part, out_part = tn(slots, pre_grad), tn(hidden, grads)
+        result, slot_grad, in_part, out_part = expert_math(slots, grads, win, wout)
         d_in = in_part if d_in is None else d_in + in_part
         d_out = out_part if d_out is None else d_out + out_part
 
@@ -469,7 +471,6 @@
 
 def moe_bwd_kernel(
     ib,
-    tables,
     g_ref,
     w_ref,
     wr_ref,
@@ -480,10 +481,14 @@
     aux_ref,
     qkv_ref,
     mixed_ref,
-    *rest,
+    table_ref,
+    y_ref,
+    grad_ref,
+    dw_out,
+    dr_ref,
+    dg_ref,
+    dw_ref,
 ):
-    table_refs = rest[:tables]
-    y_ref, grad_ref, dw_out, dr_ref, dg_ref, dw_ref = rest[tables:]
     step = pl.program_id(0)
 
     @pl.when(step == 0)
@@ -497,13 +502,12 @@
     prob = prob_ref[...].reshape(ib * SP, 128)
     aux = aux_ref[...].reshape(ib * SP, 128)
     first_pick = second_pick = back = None
-    for j, table in enumerate(table_refs):
-        owners = table.shape[0]
-        count = owners * CAP
+    for j in range(table_ref.shape[0]):
+        count = table_ref.shape[1] * CAP
         slot = lax.broadcasted_iota(jnp.int32, (1, count), 1) + j * count
         hot_one = (aux[:, 0:1] == slot).astype(NARROW)
         hot_two = (aux[:, 1:2] == slot).astype(NARROW)
-        rows = table[...].reshape(count, 2 * D)
+        rows = table_ref[j].reshape(count, 2 * D)
         one = nn(hot_one, rows[:, 0:D])
         two = nn(hot_two, rows[:, 0:D])
         both = nn(hot_one + hot_two, rows[:, D : 2 * D])
@@ -542,7 +546,7 @@
 
 def moe_bwd(gains, w1, wr, mid, second, cot, prob, aux, qkv, mixed, tables, images, ib):
     return pl.pallas_call(
-        partial(moe_bwd_kernel, ib, len(tables)),
+        partial(moe_bwd_kernel, ib),
         grid=(images // ib,),
         in_specs=[
             whole(gains.shape),
@@ -555,7 +559,7 @@
             per_image(ib, SP, 128),
             per_image(ib, SP, 3 * D),
             per_image(ib, SP, D),
-            *[whole(t.shape) for t in tables],
+            whole(tables.shape),
         ],
         out_specs=[
             whole((images * SEQ, D)),
@@ -575,7 +579,7 @@
         compiler_params=params(56),
         cost_estimate=cost(1e6, 1),
         name="expert_block_backward",
-    )(gains, w1, wr, mid, second, cot, prob, aux, qkv, mixed, *tables)
+    )(gains, w1, wr, mid, second, cot, prob, aux, qkv, mixed, tables)
 
 
 def dense_bwd_kernel(
@@ -987,58 +991,397 @@
     )(*mats, *dense, peaks)
 
 
-def widen_kernel(early, core_ref, *refs):
-    own, other, refs = refs[:early], refs[early : 2 * early], refs[2 * early :]
-    late, outs = refs[:-2], refs[-2:]
-    c, j = pl.program_id(0), pl.program_id(1)
-
-    def put(side, block):
-        for f in range(block.shape[0]):
-            s = slice(f * BLOCK, (f + 1) * BLOCK)
-            if side == 0:
-                outs[0][:, s] = block[f].astype(WIDE)
+SUMMED = 12
+BESIDE = 8
+
+
+def exchange_kernel(nz, groups, mine, *refs):
+    (sent_ref, win_hbm, wout_hbm, table_out, sum_out, beside_out, rest_out) = refs[:7]
+    (rows, back, res, sgr, w_in, w_out, own, up, down, made) = refs[7:17]
+    (d_send, d_recv, r_send, r_recv, w_sem, made_sem, up_send, up_recv, down_recv) = refs[17:26]
+    (out_send, sib_send, sib_recv, keep_sem) = refs[26:]
+    s = pl.program_id(0)
+    z, core, f = lax.axis_index("z"), lax.axis_index("core"), lax.axis_index("fsdp")
+    members = CORES * groups
+    me = core * groups + f
+    parts = FF // BLOCK
+    steps = mine * parts
+    last = pl.num_programs(0) - 1
+    left = z < nz // 2
+    inner = jnp.where(left, z + 1, z - 1)
+    has_outer = jnp.logical_and(z > 0, z < nz - 1)
+    edge = jnp.logical_not(has_outer)
+    outer = jnp.where(has_outer, jnp.where(left, z - 1, z + 1), inner)
+
+    def member(d):
+        there = lax.rem(me + d, members)
+        return there, (z, there // groups, lax.rem(there, groups))
+
+    def rows_to(j, d):
+        there, device = member(d)
+        return pltpu.make_async_remote_copy(
+            src_ref=sent_ref.at[j, there],
+            dst_ref=rows.at[j, me],
+            send_sem=d_send.at[j, d],
+            recv_sem=d_recv.at[j, d],
+            device_id=device,
+            device_id_type=MESH_ID,
+        )
+
+    def rows_here(j):
+        return pltpu.make_async_copy(sent_ref.at[j, me], rows.at[j, me], d_recv.at[j, 0])
+
+    def send_rows(j):
+        for d in range(1, members):
+            rows_to(j, d).start()
+        rows_here(j).start()
+
+    def results_to(j, d):
+        there, device = member(d)
+        return pltpu.make_async_remote_copy(
+            src_ref=back.at[j % 2, there],
+            dst_ref=table_out.at[j, me],
+            send_sem=r_send.at[j, d],
+            recv_sem=r_recv.at[j, d],
+            device_id=device,
+            device_id_type=MESH_ID,
+        )
+
+    def results_here(j):
+        return pltpu.make_async_copy(back.at[j % 2, me], table_out.at[j, me], r_recv.at[j, 0])
+
+    def weights(step):
+        e = core * mine + step // parts
+        c = pl.ds(pl.multiple_of(lax.rem(step, parts) * BLOCK, BLOCK), BLOCK)
+        slot = lax.rem(step, 2)
+        return (
+            pltpu.make_async_copy(win_hbm.at[e, :, c], w_in.at[slot], w_sem.at[0, slot]),
+            pltpu.make_async_copy(wout_hbm.at[e, c, :], w_out.at[slot], w_sem.at[1, slot]),
+        )
+
+    @pl.when(s == 0)
+    def _():
+        barrier = pltpu.get_barrier_semaphore()
+        pl.semaphore_signal(barrier, inc=1, device_id=(inner, core, f), device_id_type=MESH_ID)
+
+        @pl.when(has_outer)
+        def _():
+            pl.semaphore_signal(barrier, inc=1, device_id=(outer, core, f), device_id_type=MESH_ID)
+
+        for d in range(1, members):
+            pl.semaphore_signal(barrier, inc=1, device_id=member(d)[1], device_id_type=MESH_ID)
+
+        @pl.when(has_outer)
+        def _():
+            pl.semaphore_wait(barrier, members + 1)
+
+        @pl.when(edge)
+        def _():
+            pl.semaphore_wait(barrier, members)
+
+        send_rows(0)
+        for w in weights(s):
+            w.start()
+
+    for j in range(mine):
+
+        @pl.when(s == j * parts)
+        def _(j=j):
+            for d in range(1, members):
+                rows_to(j, d).wait_recv()
+            rows_here(j).wait()
+            if j == 0:
+                send_rows(1)
+            if j == 1:
+                send_rows(3)
+
+    slot = lax.rem(s, 2)
+
+    def made_to(step, side, near):
+        place = 2 * step + side - SUMMED - (0 if near else BESIDE)
+        there = lax.rem(step, 2)
+        out = beside_out if near else rest_out
+        return pltpu.make_async_copy(
+            made.at[there, side],
+            out.at[jnp.clip(place, 0, out.shape[0] - 1)],
+            made_sem.at[there, side],
+        )
+
+    def each_made(step, act):
+        near = step < (SUMMED + BESIDE) // 2
+
+        @pl.when(near)
+        def _():
+            for side in range(2):
+                act(made_to(step, side, True))
+
+        @pl.when(jnp.logical_not(near))
+        def _():
+            for side in range(2):
+                act(made_to(step, side, False))
+
+    @pl.when(s < steps)
+    def _():
+        for w in weights(s):
+            w.wait()
+
+        @pl.when(s + 1 < steps)
+        def _():
+            for w in weights(s + 1):
+                w.start()
+
+        @pl.when(jnp.logical_and(s >= SUMMED // 2 + 2, s < steps))
+        def _():
+            each_made(s - 2, lambda copy: copy.wait())
+
+        j = s // parts
+        part = lax.rem(s, parts)
+        count = members * CAP
+        slots = rows[j, :, 0:CAP, :].reshape(count, D)
+        grads = rows[j, :, CAP : 2 * CAP, :].reshape(count, D)
+        result, slot_grad, d_in, d_out = expert_math(slots, grads, w_in[slot], w_out[slot])
+
+        @pl.when(part == 0)
+        def _():
+            res[...] = result
+            sgr[...] = slot_grad
+
+        @pl.when(part > 0)
+        def _():
+            res[...] += result
+            sgr[...] += slot_grad
+
+        @pl.when(s < SUMMED // 2)
+        def _():
+            own[2 * s] = d_in.astype(NARROW)
+            own[2 * s + 1] = d_out.astype(NARROW)
+
+        @pl.when(s >= SUMMED // 2)
+        def _():
+            made[slot, 0] = d_in.astype(NARROW)
+            made[slot, 1] = d_out.astype(NARROW)
+
+            each_made(s, lambda copy: copy.start())
+
+    @pl.when(s == 1)
+    def _():
+        send_rows(2)
+
+    for j in range(mine):
+
+        @pl.when(s == (j + 1) * parts - 1)
+        def _(j=j):
+            if j >= 2:
+                for d in range(1, members):
+                    results_to(j - 2, d).wait_send()
+                results_here(j - 2).wait()
+            back[j % 2, :, :, 0:D] = res[...].astype(NARROW).reshape(members, CAP, D)
+            back[j % 2, :, :, D : 2 * D] = sgr[...].astype(NARROW).reshape(members, CAP, D)
+            for d in range(1, members):
+                results_to(j, d).start()
+            results_here(j).start()
+
+    def send_up(t, to_center):
+        return pltpu.make_async_remote_copy(
+            src_ref=own.at[t],
+            dst_ref=(down if to_center else up).at[t],
+            send_sem=up_send.at[t],
+            recv_sem=(down_recv if to_center else up_recv).at[t],
+            device_id=(inner, core, f),
+            device_id_type=MESH_ID,
+        )
+
+    def send_out(t):
+        return pltpu.make_async_remote_copy(
+            src_ref=down.at[t],
+            dst_ref=down.at[t],
+            send_sem=out_send.at[t],
+            recv_sem=down_recv.at[t],
+            device_id=(outer, core, f),
+            device_id_type=MESH_ID,
+        )
+
+    def to_sibling(t):
+        return pltpu.make_async_remote_copy(
+            src_ref=down.at[t],
+            dst_ref=sum_out.at[t, core],
+            send_sem=sib_send.at[t],
+            recv_sem=sib_recv.at[t],
+            device_id=(z, 1 - core, f),
+            device_id_type=MESH_ID,
+        )
+
+    def keep_sum(t):
+        return pltpu.make_async_copy(down.at[t], sum_out.at[t, core], keep_sem.at[t])
+
+    def at(lag, role):
+        t = s - lag
+        return pl.when(jnp.logical_and(role, jnp.logical_and(t >= 0, t < SUMMED)))
+
+    def tick(t):
+        return jnp.clip(t, 0, SUMMED - 1)
+
+    @at(0, edge)
+    def _():
+        send_up(tick(s), False).start()
+
+    @at(2, has_outer)
+    def _():
+        t = tick(s - 2)
+        send_up(t, False).wait_recv()
+        add_rows(own.at[t], own.at[t], up.at[t], BLOCK, 16)
+        send_up(t, True).start()
+
+    @at(4, has_outer)
+    def _():
+        t = tick(s - 4)
+        send_out(t).wait_recv()
+        add_rows(down.at[t], own.at[t], down.at[t], BLOCK, 16)
+        send_out(t).start()
+        keep_sum(t).start()
+        to_sibling(t).start()
+
+    @at(6, edge)
+    def _():
+        t = tick(s - 6)
+        send_out(t).wait_recv()
+        keep_sum(t).start()
+        to_sibling(t).start()
+
+    @pl.when(s == last)
+    def _():
+        for step in (steps - 2, steps - 1):
+            for side in range(2):
+                made_to(step, side, False).wait()
+        for j in range(mine):
+            for d in range(1, members):
+                rows_to(j, d).wait_send()
+                results_to(j, d).wait_recv()
+                if j >= mine - 2:
+                    results_to(j, d).wait_send()
+            if j >= mine - 2:
+                results_here(j).wait()
+
+        for t in range(SUMMED):
+            send_up(t, False).wait_send()
+            keep_sum(t).wait()
+            to_sibling(t).wait()
+
+        @pl.when(has_outer)
+        def _():
+            for t in range(SUMMED):
+                send_out(t).wait_send()
+
+
+def exchange(sent, win, wout, nz, groups):
+    mine, members = sent.shape[0], sent.shape[1]
+    steps = mine * (FF // BLOCK)
+    rest = 2 * steps - SUMMED - BESIDE
+    any_space = pl.BlockSpec(memory_space=pl.ANY)
+    dma = pltpu.SemaphoreType.DMA
+    block = pltpu.VMEM((SUMMED, BLOCK, BLOCK), NARROW)
+    return pl.pallas_call(
+        partial(exchange_kernel, nz, groups, mine),
+        grid=(steps + 2,),
+        in_specs=[any_space] * 3,
+        out_specs=[any_space] * 4,
+        out_shape=[
+            sds((mine, members, CAP, 2 * D), NARROW),
+            sds((SUMMED, CORES, BLOCK, BLOCK), NARROW),
+            sds((BESIDE, BLOCK, BLOCK), NARROW),
+            sds((rest, BLOCK, BLOCK), NARROW),
+        ],
+        scratch_shapes=[
+            pltpu.VMEM((mine, members, 2 * CAP, D), NARROW),
+            pltpu.VMEM((2, members, CAP, 2 * D), NARROW),
+            pltpu.VMEM((members * CAP, D), WIDE),
+            pltpu.VMEM((members * CAP, D), WIDE),
+            pltpu.VMEM((2, D, BLOCK), NARROW),
+            pltpu.VMEM((2, BLOCK, D), NARROW),
+            block,
+            block,
+            block,
+            pltpu.VMEM((2, 2, BLOCK, BLOCK), NARROW),
+            *[dma((mine, members)) for _ in range(4)],
+            dma((2, 2)),
+            dma((2, 2)),
+            *[dma((SUMMED,)) for _ in range(7)],
+        ],
+        compiler_params=pltpu.CompilerParams(
+            vmem_limit_bytes=58 * MIB, collective_id=7, has_side_effects=True
+        ),
+        name="experts",
+    )(sent, win, wout)
+
+
+def widen_kernel(counts, core_ref, *refs):
+    in_ref, out_ref = refs[-2:]
+    c, s = pl.program_id(0), pl.program_id(1)
+
+    def put(ref):
+        in_ref[...] = ref[0].astype(WIDE)
+        out_ref[...] = ref[1].astype(WIDE)
+
+    first, at = 0, 0
+    for kind, count in enumerate(counts):
+        if count:
+            here = jnp.logical_and(s >= first, s < first + count)
+            if kind == 1:
+                for ref, mine in ((refs[at], True), (refs[at + 1], False)):
+                    pl.when(jnp.logical_and(here, (c == core_ref[0]) == mine))(partial(put, ref))
+                at += 2
             else:
-                outs[1][s, :] = block[f].astype(WIDE)
-
-    for side in range(2):
-        for n in range(side, early, 2):
-            for source, here in ((own[n], True), (other[n], False)):
-
-                @pl.when(jnp.logical_and(2 * j + side == n, (c == core_ref[0]) == here))
-                def _(source=source):
-                    put(side, source)
-
-        @pl.when(2 * j + side >= early)
-        def _():
-            put(side, late[side])
-
-
-def widen(core, own, other, late, mine, slices):
-    early = len(own)
-    late = late.reshape(-1, slices, CORES, BLOCK, BLOCK)
-    count = late.shape[0]
-
-    def late_spec(side):
-        def where_from(c, j, _):
-            return (jnp.clip(2 * j + side - early, 0, count - 1), 0, c, 0, 0)
-
-        return pl.BlockSpec((None, slices, None, BLOCK, BLOCK), where_from)
-
+                pl.when(here)(partial(put, refs[at]))
+                at += 1
+        first += count
+
+
+def widen(core, early, own, other, late, mine):
+    block = (None, 2, None, BLOCK, BLOCK)
+    arrays, specs, counts, first = [], [], [], 0
+    for kind, group in enumerate(((early,), (own, other), (late,))):
+        count = 0 if group[0] is None else group[0].shape[0] // 2
+        counts.append(count)
+        if count:
+
+            def pair(s, first=first, count=count):
+                return jnp.clip(s - first, 0, count - 1)
+
+            for a in group:
+                if kind == 1:
+                    arrays.append(a.reshape(count, 2, BLOCK, BLOCK))
+                    specs.append(
+                        pl.BlockSpec(
+                            (None, 2, BLOCK, BLOCK),
+                            lambda c, s, _, pair=pair: (pair(s), 0, 0, 0),
+                        )
+                    )
+                else:
+                    arrays.append(a.reshape(count, 2, CORES, BLOCK, BLOCK))
+                    specs.append(
+                        pl.BlockSpec(block, lambda c, s, _, pair=pair: (pair(s), 0, c, 0, 0))
+                    )
+        first += count
+    parts = FF // BLOCK
     return pl.pallas_call(
-        partial(widen_kernel, early),
+        partial(widen_kernel, counts),
         grid_spec=pltpu.PrefetchScalarGridSpec(
             num_scalar_prefetch=1,
-            grid=(CORES, mine),
-            in_specs=[whole(a.shape) for a in (*own, *other)] + [late_spec(0), late_spec(1)],
+            grid=(CORES, mine * parts),
+            in_specs=specs,
             out_specs=[
-                pl.BlockSpec((None, D, FF), lambda c, j, _: (c * mine + j, 0, 0)),
-                pl.BlockSpec((None, FF, D), lambda c, j, _: (c * mine + j, 0, 0)),
+                pl.BlockSpec(
+                    (None, D, BLOCK), lambda c, s, _: (c * mine + s // parts, 0, s % parts)
+                ),
+                pl.BlockSpec(
+                    (None, BLOCK, D), lambda c, s, _: (c * mine + s // parts, s % parts, 0)
+                ),
             ],
         ),
         out_shape=[sds((CORES * mine, D, FF), WIDE), sds((CORES * mine, FF, D), WIDE)],
         compiler_params=params(56),
         name="widen",
-    )(core, *own, *other, late, late)
+    )(core, *arrays)
 
 
 def gather_kernel(groups, q_ref, k_ref, v_ref, o_ref, small_ref, in_ref, out_ref, *refs):
@@ -1227,22 +1570,25 @@
         pos, order, moe.reshape(-1, D), cot.reshape(-1, D), prob.reshape(-1, 128)
     ).reshape(mine, owners, 2 * CAP, D)
 
-    tables, mats, backs = [], [], []
-    for j in range(mine):
-        chunk = sent[j]
-        if j >= 2:
-            chunk, _ = lax.optimization_barrier((chunk, backs[j - 2]))
-        rows = lax.all_to_all(chunk, ("core", "fsdp"), split_axis=0, concat_axis=0, tiled=True)
-        pick = (core * mine + j).astype(jnp.int32).reshape(1)
-        back, d_in, d_out = expert(pick, rows, expert_in, expert_out)
-        backs.append(back)
-        tables.append(
-            lax.all_to_all(back, ("core", "fsdp"), split_axis=0, concat_axis=0, tiled=True)
-        )
-        mats += [d_in, d_out]
-    early = len(mats) // 2
-    ready = lax.psum(mats[:early], "z")
-    others = [lax.ppermute(mat, "core", [(0, 1), (1, 0)]) for mat in ready]
+    nz = lax.axis_size("z")
+    early = own = other = None
+    if nz == 4 and owners == 8 and mine == 4:
+        tables, early, own, late = exchange(sent, expert_in, expert_out, nz, groups)
+        own = lax.psum(own, "z")
+    else:
+        tables, blocks = [], []
+        for j in range(mine):
+            rows = lax.all_to_all(
+                sent[j], ("core", "fsdp"), split_axis=0, concat_axis=0, tiled=True
+            )
+            pick = (core * mine + j).astype(jnp.int32).reshape(1)
+            back, d_in, d_out = expert(pick, rows, expert_in, expert_out)
+            tables.append(
+                lax.all_to_all(back, ("core", "fsdp"), split_axis=0, concat_axis=0, tiled=True)
+            )
+            blocks.append(jnp.stack([d_in, d_out], 1).reshape(-1, BLOCK, BLOCK))
+        tables = jnp.stack(tables)
+        late = jnp.concatenate(blocks)
 
     y, mid_grad, dw1 = moe_bwd(
         gains, w1, wr, mid, second, cot, prob, aux, qkv1, mixed1, tables, images, ib
@@ -1252,11 +1598,12 @@
     )
     lane = jnp.arange(128)[None, :]
     peaks = jnp.where(lane < 64, jnp.max(peak0, 0), jnp.max(peak1, 0))
-    late, t1, t0, t_wout, maxima = sum_all(
-        mats[early:], [dw1, dw0, d_wout], peaks, lax.axis_size("z"), groups
-    )
+    late, t1, t0, t_wout, maxima = sum_all([late], [dw1, dw0, d_wout], peaks, nz, groups)
+    if own is not None:
+        own, late = lax.optimization_barrier((own, late))
+        other = lax.ppermute(own, "core", [(0, 1), (1, 0)])
     expert_in_grad, expert_out_grad = widen(
-        core.astype(jnp.int32).reshape(1), ready, others, late, mine, mats[0].shape[0]
+        core.astype(jnp.int32).reshape(1), early, own, other, late, mine
     )
 
     t1, t0 = t1.astype(WIDE), t0.astype(WIDE)

time: 867 us -> 788 us (0.909)
  Pallas kernels: 648 us -> 727 us
  blocking collectives: 61.5 us -> 0 us
  waiting for transfers between devices: 54.6 us -> 0.08 us
  starting transfers between devices: 34.8 us -> 0.52 us
  local copies, waits for them, and re-layouts: 38.7 us -> 25.5 us
    pallas_call x6 -> x3, Pallas kernels: 197 us -> 326 us  [the longest x1 208 us: exchange(): pl.pallas_call(partial(exchange_kernel, nz, groups, mine), grid=(steps +...]
    all_to_all x2 -> x0, blocking collectives: 61.5 us -> none  [the longest x1 30.9 us: local(): lax.all_to_all(chunk, ('core', 'fsdp'), split_axis=0, concat_axis=0, tile...]
    all_to_all x6 -> x0, waiting for transfers between devices: 51.7 us -> none  [the longest x3 27.8 us: local(): lax.all_to_all(chunk, ('core', 'fsdp'), split_axis=0, concat_axis=0, tile...]
    pallas_call x1, Pallas kernels: 251 us -> 201 us  [sum_all(): pl.pallas_call(partial(sum_kernel, nz, groups, len(mats), slices), in_spe...]
    all_to_all x6 -> x0, starting transfers between devices: 33.6 us -> none  [the longest x3 22 us: local(): lax.all_to_all(chunk, ('core', 'fsdp'), split_axis=0, concat_axis=0, tile...]
  transfers between devices with their start and end apart: 12 -> 3, of which waited for: 7 -> 0; matrix products, arithmetic and copies ran while one was open for 4% -> 4% of each run, Pallas kernels for 66% -> 55%
where the time goes in v3:
time: 788 us; the launch traced here: 780 us
  Pallas kernels  727 us (92%)
  local copies, waits for them, and re-layouts  25.5 us (3%)
  between operations  15 us (2%)
  other arithmetic  11.6 us (1%)
    pallas_call x1, Pallas kernels, exchange(): pl.pallas_call(partial(exchange_kernel, nz, groups, mine), grid=(steps +...  208 us
    pallas_call x1, Pallas kernels, sum_all(): pl.pallas_call(partial(sum_kernel, nz, groups, len(mats), slices), in_spe...  201 us
    pallas_call x1, Pallas kernels, moe_bwd(): pl.pallas_call(partial(moe_bwd_kernel, ib), grid=(images // ib,), in_spec...  73.8 us
    pallas_call x1, Pallas kernels, dense_bwd(): pl.pallas_call(partial(dense_bwd_kernel, ib), grid=(images // ib,), in_sp...  66.8 us
    pallas_call x1, Pallas kernels, gather_dense(): pl.pallas_call(partial(gather_kernel, groups), in_specs=[any_space] * 7,...  54.4 us
    pallas_call x1, Pallas kernels, widen(): pl.pallas_call(partial(widen_kernel, counts), grid_spec=pltpu.PrefetchSca...  43.8 us
    pallas_call x1, Pallas kernels, dispatch(): pl.pallas_call(dispatch_kernel, grid=(groups,), in_specs=[pl.BlockSpec((N...  25.8 us
    pallas_call x1, Pallas kernels, ffn(): pl.pallas_call(partial(ffn_kernel, ib), grid=(images // ib,), in_specs=[p...  19 us
  transfers between devices with their start and end apart: 3, of which 0 were waited for; matrix products, arithmetic and copies ran while one was open for 4% of the time, Pallas kernels for 55%

profile of v3, /device:TPU:0, one launch (start us, length us, event | category | flops | bytes accessed | tf_op | source)
XLA Modules:
  0.0 779.9 jit_solution(11976352732159832787)
XLA Ops:
  7.3 1.1 slice_bitcast_fusion.8
  11.0 54.4 %gather_weights.1 = (bf16[512,2048]{1,0:T(8,128)(2,1)S(1)}, bf16[512,128]{1,0:T(8,128)(2,1)S(1)}, bf16[512,2048]{1,0:T(8,128)(2,1)S(1)}, bf16[2048,512]{1,0:T(8,128)(2,1)S(1)}) custom-call(bf16[2,128,512]{2,1,0:T(8,128)(2,1)S(1)} %copy-done.14, bf16[2,128,512]{2,1,0:T(8,128)(2,1)S(1)} %copy-done.15, bf16[2,128,512]{2,1,0:T(8,128)(2,1)S(1)} %copy-done.16, ...), custom_call_target="tpu_custom_call" | custom-call | tf_op jit(solution)/shard_map/gather_weights/pallas_call | solution.py:1467
  65.4 1.3 copy-done.2
  66.7 1.3 copy-done.4
  68.0 1.4 copy-done.6
  70.1 1.9 reshape.146
  74.5 1.9 places.1
  76.4 1.7 reshape.151.pos_ref
  78.1 3.1 reshape.147
  81.2 1.7 pad.28.cot_ref
  83.9 13.9 %dense_attention.1 = (f32[8,208,512]{2,1,0:T(8,128)}, bf16[8,208,1536]{2,1,0:T(8,128)(2,1)}, bf16[8,208,512]{2,1,0:T(8,128)(2,1)S(1)}, f32[8,8,128]{2,1,0:T(8,128)S(1)}) custom-call(bf16[8,208,512]{2,1,0:T(8,128)(2,1)S(1)} %pad.27.x_ref, f32[8,512]{1,0:T(8,128)S(1)} %pad_convert_fusion.g_ref, bf16[512,2048]{1,0:T(8,128)(2,1)S(1)} %copy-done.3), custom_call_target="tpu_custom_call" | custom-call | tf_op jit(solution)/shard_map/dense_attention/pallas_call | solution.py:177
  97.8 19.0 %feed_forward.1.x_ref.mid_ref = f32[8,208,512]{2,1,0:T(8,128)} custom-call(f32[8,208,512]{2,1,0:T(8,128)} %get-tuple-element.52.x_ref.first_ref, f32[8,512]{1,0:T(8,128)S(1)} %pad_convert_fusion.g_ref, bf16[512,2048]{1,0:T(8,128)(2,1)S(1)} %copy-done.5, bf16[2048,512]{1,0:T(8,128)(2,1)S(1)} %copy-done.7), custom_call_target="tpu_custom_call" | custom-call | tf_op jit(solution)/shard_map/feed_forward/pallas_call | solution.py:199
  116.9 18.3 %expert_attention.1 = (f32[8,208,512]{2,1,0:T(8,128)}, bf16[8,208,1536]{2,1,0:T(8,128)(2,1)}, bf16[8,208,512]{2,1,0:T(8,128)(2,1)S(1)}, f32[8,8,128]{2,1,0:T(8,1...) custom-call(f32[8,208,512]{2,1,0:T(8,128)} %feed_forward.1.x_ref.mid_ref, ...), custom_call_target="tpu_custom_call" | custom-call | tf_op jit(solution)/shard_map/expert_attention/pallas_call | solution.py:211
  135.1 1.2 copy-done.10
  136.4 25.8 %dispatch.1 = bf16[32,256,512]{2,1,0:T(8,128)(2,1)} custom-call(f32[8,4,1664]{2,1,0:T(4,128)S(1)} %copy-done.12, s32[8,4,128]{2,1,0:T(4,128)S(1)} %broadcast_in_dim.40.order_ref, bf16[1664,512]{1,0:T(8,128)(2,1)S(1)} %bitcast.53, bf16[1664,512]{1,0:T(8,128)(2,1)S(1)} %bitcast.51, f32[1664,128]{1,0:T(8,128)S(1)} %bitcast.52), custom_call_target="tpu_custom_call" | custom-call | tf_op jit(solution)/shard_map/dispatch/pallas_call | solution.py:309
  162.2 208.1 %experts.1 = (bf16[4,8,128,1024]{3,2,1,0:T(8,128)(2,1)}, bf16[12,2,512,512]{3,2,1,0:T(8,128)(2,1)}, bf16[8,512,512]{2,1,0:T(8,128)(2,1)}, bf16[12,512,512]{2,1,0:T(8,128)(2,1)}) custom-call(bf16[4,8,256,512]{3,2,1,0:T(8,128)(2,1)} %bitcast.54, bf16[8,512,2048]{2,1,0:T(8,128)(2,1)} %refs_1_.1, bf16[8,2048,512]{2,1,0:T(8,128)(2,1)} %refs_2_.1), custom_call_target="tpu_custom_call" | custom-call | tf_op jit(solution)/shard_map/experts/pallas_call | solution.py:1283
  372.7 73.8 %expert_block_backward.1 = (f32[1576,512]{1,0:T(8,128)}, f32[8,208,512]{2,1,0:T(8,128)}, bf16[512,2176]{1,0:T(8,128)(2,1)}) custom-call(f32[8,512]{1,0:T(8,128)} %copy-done.13, bf16[512,2048]{1,0:T(8,128)(2,1)} %all-gather.2.cloned.1.call-done.w_ref, bf16[512,128]{1,0:T(8,128)(2,1)} %copy-done.11, f32[8,208,512]{2,1,0:T(8,128)} %feed_forward.1.x_ref.mid_ref, ...), custom_call_target="tpu_custom_call" | custom-call | flops 1000000 | bytes 1 | tf_op jit(solution)/shard_map/expert_block_backward/pallas_call | solution.py:548
  446.5 66.8 %dense_block_backward.1 = (f32[1576,512]{1,0:T(8,128)}, bf16[512,4224]{1,0:T(8,128)(2,1)}, bf16[2048,512]{1,0:T(8,128)(2,1)}) custom-call(f32[8,512]{1,0:T(8,128)} %copy-done.13, bf16[512,2048]{1,0:T(8,128)(2,1)} %copy-done.2, bf16[512,2048]{1,0:T(8,128)(2,1)} %copy-done.4, bf16[2048,512]{1,0:T(8,128)(2,1)} %copy-done.6, bf16[8,208,512]{2,1,0:T(8,128)(2,1)} %copy-done.1, ...), custom_call_target="tpu_custom_call" | custom-call | flops 1000000 | bytes 1 | tf_op jit(solution)/shard_map/dense_block_backward/pallas_call | solution.py:650
  513.9 201.4 %sums.1 = (bf16[12,2,512,512]{3,2,1,0:T(8,128)(2,1)}, bf16[128,2176]{1,0:T(8,128)(2,1)}, bf16[128,4224]{1,0:T(8,128)(2,1)}, bf16[512,512]{1,0:T(8,128)(2,1)}, f32[8,128]{1,0:T(8,128)}) custom-call(bf16[12,512,512]{2,1,0:T(8,128)(2,1)} %get-tuple-element.68.refs_0_, bf16[512,2176]{1,0:T(8,128)(2,1)} %get-tuple-element.69.refs_1_, ...), custom_call_target="tpu_custom_call" | custom-call | tf_op jit(solution)/shard_map/sums/pallas_call | solution.py:966
  715.8 1.4 convert_element_type.30
  718.6 1.1 convert_element_type.29
  721.9 2.1 convert_element_type.31
  727.7 1.1 broadcast_multiply_fusion
  728.8 43.8 %widen.1 = (f32[8,512,2048]{2,1,0:T(8,128)}, f32[8,2048,512]{2,1,0:T(8,128)}) custom-call(s32[1]{0:T(128)} %bitcast.22.core_ref, bf16[6,2,2,512,512]{4,3,2,1,0:T(8,128)(2,1)} %bitcast.55, bf16[4,2,512,512]{3,2,1,0:T(8,128)(2,1)} %bitcast.57, bf16[4,2,512,512]{3,2,1,0:T(8,128)(2,1)} %bitcast.25.refs_2_, bf16[6,2,2,512,512]{4,3,2,1,0:T(8,128)(2,1)} %bitcast.56), custom_call_target="tpu_custom_call" | custom-call | tf_op jit(solution)/shard_map/widen/pallas_call | solution.py:1366
  (118 shorter events, 17.3 us)
Async XLA Ops:
  7.2 3.8 copy-start.16
  7.2 3.8 copy-start.17
  7.2 3.8 copy-start.14
  7.2 3.8 copy-start.15
  7.2 3.3 copy-start.32
  7.2 3.4 copy-start.29
  7.3 3.7 copy-start.18
  7.3 3.7 copy-start.19
  7.3 109.6 %all-gather.2.cloned.1.call-start = ((), (), s32[]{:S(2)}) async-start(), calls=%async_computation | async-start | bytes 2621440 | tf_op jit(solution)/shard_map/all_gather | solution.py:1489
  10.3 705.1 %all-reduce.8.cloned.1.call-start = ((), (), s32[]{:S(2)}) async-start(), calls=%async_computation.1 | async-start | bytes 8388608 | tf_op jit(solution)/shard_map/psum | solution.py:1577
  72.8 11.1 %copy-start.1 = (bf16[8,208,512]{2,1,0:T(8,128)(2,1)}, bf16[8,208,512]{2,1,0:T(8,128)(2,1)S(1)}, u32[]{:S(2)}) copy-start(bf16[8,208,512]{2,1,0:T(8,128)(2,1)S(1)} %pad.27.x_ref) | copy-start | bytes 5111812
  72.9 10.0 %copy-start.25 = (s32[8,208,2]{1,0,2:T(8,128)}, s32[8,208,2]{1,0,2:T(8,128)S(1)}, u32[]{:S(2)}) copy-start(s32[8,208,2]{1,0,2:T(8,128)S(1)} %pad.29) | copy-start | bytes 39940
  81.2 16.6 %copy-start.7 = (bf16[2048,512]{1,0:T(8,128)(2,1)S(1)}, bf16[2048,512]{1,0:T(8,128)(2,1)}, u32[]{:S(2)}) copy-start(bf16[2048,512]{1,0:T(8,128)(2,1)} %copy-done.6) | copy-start | bytes 6291460
  82.9 53.5 %copy-start = (bf16[8,208,512]{2,1,0:T(8,128)(2,1)}, bf16[8,208,512]{2,1,0:T(8,128)(2,1)S(1)}, u32[]{:S(2)}) copy-start(bf16[8,208,512]{2,1,0:T(8,128)(2,1)S(1)} %pad.28.cot_ref) | copy-start | bytes 5111812
  82.9 14.8 %copy-start.5 = (bf16[512,2048]{1,0:T(8,128)(2,1)S(1)}, bf16[512,2048]{1,0:T(8,128)(2,1)}, u32[]{:S(2)}) copy-start(bf16[512,2048]{1,0:T(8,128)(2,1)} %copy-done.4) | copy-start | bytes 6291460
  83.8 33.0 %copy-start.13 = (f32[8,512]{1,0:T(8,128)}, f32[8,512]{1,0:T(8,128)S(1)}, u32[]{:S(2)}) copy-start(f32[8,512]{1,0:T(8,128)S(1)} %pad_convert_fusion.g_ref) | copy-start | bytes 49156
  97.7 19.0 %copy-start.9 = (bf16[8,208,512]{2,1,0:T(8,128)(2,1)}, bf16[8,208,512]{2,1,0:T(8,128)(2,1)S(1)}, u32[]{:S(2)}) copy-start(bf16[8,208,512]{2,1,0:T(8,128)(2,1)S(1)} %get-tuple-element.66.mixed_ref) | copy-start | bytes 5111812
  97.7 19.0 %copy-start.20 = (f32[8,8,128]{2,1,0:T(8,128)}, f32[8,8,128]{2,1,0:T(8,128)S(1)}, u32[]{:S(2)}) copy-start(f32[8,8,128]{2,1,0:T(8,128)S(1)} %get-tuple-element.72) | copy-start | bytes 98308
  116.8 18.3 %copy-start.11 = (bf16[512,128]{1,0:T(8,128)(2,1)}, bf16[512,128]{1,0:T(8,128)(2,1)S(1)}, u32[]{:S(2)}) copy-start(bf16[512,128]{1,0:T(8,128)(2,1)S(1)} %broadcast_select_fusion.wr_ref) | copy-start | bytes 393220
  116.8 19.6 %copy-start.12 = (f32[8,4,1664]{2,1,0:T(4,128)S(1)}, f32[8,4,1664]{2,1,0:T(4,128)}, u32[]{:S(2)}) copy-start(f32[8,4,1664]{2,1,0:T(4,128)} %reshape.151.pos_ref) | copy-start | bytes 638980
  136.3 25.9 %copy-start.8 = (f32[8,208,128]{2,1,0:T(8,128)}, f32[8,208,128]{2,1,0:T(8,128)S(1)}, u32[]{:S(2)}) copy-start(f32[8,208,128]{2,1,0:T(8,128)S(1)} %get-tuple-element.56.prob_ref) | copy-start | bytes 2555908
  715.4 13.4 %collective-permute-start = (bf16[8,512,512]{2,1,0:T(8,128)(2,1)}, bf16[8,512,512]{2,1,0:T(8,128)(2,1)}, u32[]{:S(2)}, u32[]{:S(2)}) collective-permute-start(bf16[8,512,512]{2,1,0:T(8,128)(2,1)} %all-reduce.8.cloned.1.call-done), channel_id=1, source_target_pairs={{0,4},{4,0},{1,5},{5,1},{2,6},{6,2},{3,7},{7,3},{8,12},{12,8},{9,1... | collective-permute-start | bytes 12582920 | tf_op jit(solution)/shard_map/ppermute | solution.py:1604
  724.4 3.3 copy-start.23
  724.4 3.3 copy-start.24
  (12 other events, 21.9 us)
Sparse Core Ops, SparseCore 0:
  10.5 56.9 all-gather.1
  370.5 158.8 all-reduce.7

commit v4 on v3

--- a/solution.py
+++ b/solution.py
@@ -2,6 +2,7 @@
 
 import jax
 import jax.numpy as jnp
+import numpy as np
 from jax import lax
 from jax.experimental import pallas as pl
 from jax.experimental.pallas import tpu as pltpu
@@ -117,40 +118,6 @@
     return x + nn(mixed, w_ref[:, 3 * D : 4 * D])
 
 
-def dense_attn_kernel(ib, x_ref, g_ref, w_ref, y_ref, qkv_ref, mixed_ref, peak_ref):
-    x = x_ref[...].astype(WIDE).reshape(ib * SP, D)
-    y = attn_fwd_body(x, g_ref[0:1, :], w_ref, qkv_ref, mixed_ref, peak_ref, ib)
-    y_ref[...] = y.reshape(ib, SP, D)
-
-
-def ffn_kernel(ib, x_ref, g_ref, win_ref, wout_ref, y_ref):
-    x = x_ref[...].reshape(ib * SP, D)
-    unit, _ = norm_parts(x)
-    normed = (unit * g_ref[2:3, :]).astype(NARROW)
-    acc = x
-    for f in range(FF // 512):
-        c = slice(f * 512, (f + 1) * 512)
-        pre = nn(normed, win_ref[:, c])
-        cdf, _ = normal_parts(pre)
-        acc = acc + nn((pre * cdf).astype(NARROW), wout_ref[c, :])
-    y_ref[...] = acc.reshape(ib, SP, D)
-
-
-def expert_attn_kernel(
-    ib, x_ref, g_ref, w_ref, wr_ref, y_ref, qkv_ref, mixed_ref, peak_ref, moe_ref, prob_ref
-):
-    x = x_ref[...].reshape(ib * SP, D)
-    y = attn_fwd_body(x, g_ref[1:2, :], w_ref, qkv_ref, mixed_ref, peak_ref, ib)
-    y_ref[...] = y.reshape(ib, SP, D)
-    unit, _ = norm_parts(y)
-    moe = (unit * g_ref[3:4, :]).astype(NARROW)
-    moe_ref[...] = moe.reshape(ib, SP, D)
-    lane = lax.broadcasted_iota(jnp.int32, (1, 128), 1)
-    logits = jnp.where(lane < EXPERTS, nn(moe, wr_ref[...]), LOWEST)
-    e = jnp.exp(logits - jnp.max(logits, -1, keepdims=True))
-    prob_ref[...] = (e / jnp.sum(e, -1, keepdims=True)).reshape(ib, SP, 128)
-
-
 def whole(shape):
     return pl.BlockSpec(
         shape, lambda *_: (0,) * len(shape), pipeline_mode=pl.Buffered(buffer_count=1)
@@ -173,67 +140,7 @@
     return pltpu.CompilerParams(vmem_limit_bytes=mib * MIB)
 
 
-def dense_attn(x, gains, w0, images, ib):
-    return pl.pallas_call(
-        partial(dense_attn_kernel, ib),
-        grid=(images // ib,),
-        in_specs=[per_image(ib, SP, D), whole(gains.shape), whole(w0.shape)],
-        out_specs=[
-            per_image(ib, SP, D),
-            per_image(ib, SP, 3 * D),
-            per_image(ib, SP, D),
-            per_image(ib, HEADS, 128),
-        ],
-        out_shape=[
-            sds((images, SP, D), WIDE),
-            sds((images, SP, 3 * D), NARROW),
-            sds((images, SP, D), NARROW),
-            sds((images, HEADS, 128), WIDE),
-        ],
-        compiler_params=params(48),
-        name="dense_attention",
-    )(x, gains, w0)
-
-
-def ffn(x, gains, win, wout, images, ib):
-    return pl.pallas_call(
-        partial(ffn_kernel, ib),
-        grid=(images // ib,),
-        in_specs=[per_image(ib, SP, D), whole(gains.shape), whole(win.shape), whole(wout.shape)],
-        out_specs=per_image(ib, SP, D),
-        out_shape=sds((images, SP, D), WIDE),
-        compiler_params=params(48),
-        name="feed_forward",
-    )(x, gains, win, wout)
-
-
-def expert_attn(x, gains, w1, wr, images, ib):
-    return pl.pallas_call(
-        partial(expert_attn_kernel, ib),
-        grid=(images // ib,),
-        in_specs=[per_image(ib, SP, D), whole(gains.shape), whole(w1.shape), whole(wr.shape)],
-        out_specs=[
-            per_image(ib, SP, D),
-            per_image(ib, SP, 3 * D),
-            per_image(ib, SP, D),
-            per_image(ib, HEADS, 128),
-            per_image(ib, SP, D),
-            per_image(ib, SP, 128),
-        ],
-        out_shape=[
-            sds((images, SP, D), WIDE),
-            sds((images, SP, 3 * D), NARROW),
-            sds((images, SP, D), NARROW),
-            sds((images, HEADS, 128), WIDE),
-            sds((images, SP, D), NARROW),
-            sds((images, SP, 128), WIDE),
-        ],
-        compiler_params=params(48),
-        name="expert_attention",
-    )(x, gains, w1, wr)
-
-
-def places_kernel(order_ref, routes_ref, pos_ref, target_ref):
+def find_places(order_ref, routes_ref, pos_ref, aux_ref, line_ref):
     tokens = routes_ref.shape[1]
     order = order_ref[:, 0:1]
     chunk = 128
@@ -243,9 +150,8 @@
     ).astype(NARROW)
     slot_row = lax.broadcasted_iota(jnp.int32, (EXPERTS, 1), 0).astype(WIDE) * CAP
     base = jnp.zeros((EXPERTS, 1), WIDE)
-    for c in range(tokens // chunk):
-        pos_ref[:, c * chunk : (c + 1) * chunk] = jnp.full((EXPERTS, chunk), -1.0, WIDE)
-    target_ref[...] = jnp.zeros(target_ref.shape, WIDE)
+    pos_ref[...] = jnp.full(pos_ref.shape, -1.0, WIDE)
+    line_ref[...] = jnp.zeros(line_ref.shape, WIDE)
     for k in range(2):
         for c in range(tokens // chunk):
             s = slice(c * chunk, (c + 1) * chunk)
@@ -256,72 +162,73 @@
             slot = jnp.where(place < CAP, slot_row + place, 2.0 * EXPERTS * CAP)
             found = jnp.sum(hit * slot, 0, keepdims=True)
             real = jnp.sum(hit, 0, keepdims=True)
-            target_ref[k : k + 1, s] = jnp.where(real > 0, found, 2.0 * EXPERTS * CAP)
-
-
-def places(order, routes_rows):
-    tokens = routes_rows.shape[1]
-    return pl.pallas_call(
-        places_kernel,
-        in_specs=[pl.BlockSpec(memory_space=pltpu.VMEM)] * 2,
-        out_specs=[pl.BlockSpec(memory_space=pltpu.VMEM)] * 2,
-        out_shape=[sds((EXPERTS, tokens), WIDE), sds((8, tokens), WIDE)],
-        name="places",
-    )(order, routes_rows)
-
-
-GROUP = 4
-
-
-def dispatch_kernel(pos_ref, order_ref, moe_ref, cot_ref, prob_ref, out_ref, parts_ref):
+            line_ref[k : k + 1, s] = jnp.where(real > 0, found, 2.0 * EXPERTS * CAP)
+            line_ref[2 + k : 3 + k, s] = routes_ref[k : k + 1, s].astype(WIDE)
+    for c in range(tokens // chunk):
+        s = slice(c * chunk, (c + 1) * chunk)
+        aux_ref[s, :] = jnp.transpose(line_ref[:, s])
+
+
+def pad_images(ref, wide_ref, out_ref):
+    tokens = ref.shape[0]
+    wide_ref[0:tokens, :] = ref[...].astype(WIDE)
+    rows = lax.broadcasted_iota(jnp.int32, (SP, 1), 0)
+    for i in range(tokens // SEQ):
+        image = wide_ref[i * SEQ : i * SEQ + SP, :]
+        out_ref[i] = jnp.where(rows < SEQ, image, 0.0).astype(NARROW)
+
+
+GROUP = 8
+
+
+def slot_expert(index, groups, held):
+    owners, mine = CORES * groups, held // CORES
+    owner = index % owners
+    return (owner % groups) * held + (owner // groups) * mine + index // owners
+
+
+def dispatch_kernel(groups, held, pos_ref, moe_ref, cot_ref, prob_ref, out_ref, line_ref):
     step = pl.program_id(0)
 
     @pl.when(step == 0)
     def _():
-        prob = prob_ref[...]
-        high = prob.astype(NARROW)
-        rest = prob - high.astype(WIDE)
-        middle = rest.astype(NARROW)
-        parts_ref[:, 0:128] = high
-        parts_ref[:, 128:256] = middle
-        parts_ref[:, 256:384] = (rest - middle.astype(WIDE)).astype(NARROW)
+        for c in range(prob_ref.shape[0] // 128):
+            s = slice(c * 128, (c + 1) * 128)
+            line_ref[:, s] = jnp.transpose(prob_ref[s, :])
 
     slot = lax.broadcasted_iota(jnp.int32, (CAP, 1), 0).astype(WIDE)
-    lane = lax.broadcasted_iota(jnp.int32, (1, 128), 1)
-    hot = jnp.concatenate(
-        [(pos_ref[g : g + 1, :] == slot).astype(NARROW) for g in range(GROUP)], 0
-    )
+    hot, gates = [], []
+    for g in range(GROUP):
+        mine = pos_ref[g : g + 1, :] == slot
+        hot.append(mine.astype(WIDE).astype(NARROW))
+        gate_row = line_ref[pl.ds(slot_expert(step * GROUP + g, groups, held), 1), :]
+        gates.append(jnp.sum(jnp.where(mine, gate_row, 0.0), -1, keepdims=True))
+    hot = jnp.concatenate(hot, 0)
     rows = nn(hot, moe_ref[...]).astype(NARROW)
     grads = nn(hot, cot_ref[...])
-    parts = nn(hot, parts_ref[...])
-    gates = parts[:, 0:128] + parts[:, 128:256] + parts[:, 256:384]
     for g in range(GROUP):
         s = slice(g * CAP, (g + 1) * CAP)
-        expert = order_ref[g : g + 1, 0:1]
-        gate = jnp.sum(jnp.where(lane == expert, gates[s], 0.0), -1, keepdims=True)
         out_ref[g, 0:CAP, :] = rows[s]
-        out_ref[g, CAP : 2 * CAP, :] = (gate * grads[s]).astype(NARROW)
-
-
-def dispatch(pos, order, moe, cot, prob):
+        out_ref[g, CAP : 2 * CAP, :] = (gates[g] * grads[s]).astype(NARROW)
+
+
+def dispatch(pos, moe, cot, prob, groups, held):
     tokens = moe.shape[0]
-    groups = EXPERTS // GROUP
     return pl.pallas_call(
-        dispatch_kernel,
-        grid=(groups,),
+        partial(dispatch_kernel, groups, held),
+        grid=(EXPERTS // GROUP,),
         in_specs=[
-            pl.BlockSpec((None, GROUP, tokens), lambda i: (i, 0, 0)),
-            pl.BlockSpec((None, GROUP, 128), lambda i: (i, 0, 0)),
+            pl.BlockSpec((GROUP, tokens), lambda i: (i, 0)),
             whole(moe.shape),
             whole(cot.shape),
             whole(prob.shape),
         ],
         out_specs=pl.BlockSpec((GROUP, 2 * CAP, D), lambda i: (i, 0, 0)),
         out_shape=sds((EXPERTS, 2 * CAP, D), NARROW),
-        scratch_shapes=[pltpu.VMEM((tokens, 384), NARROW)],
-        compiler_params=params(48),
+        scratch_shapes=[pltpu.VMEM((128, tokens), WIDE)],
+        compiler_params=params(60),
         name="dispatch",
-    )(pos.reshape(groups, GROUP, tokens), order.reshape(groups, GROUP, 128), moe, cot, prob)
+    )(pos, moe, cot, prob)
 
 
 def expert_math(slots, grads, win, wout):
@@ -395,7 +302,7 @@
             sds((FF // wide, D, wide), NARROW),
             sds((FF // wide, wide, D), NARROW),
         ],
-        compiler_params=params(56),
+        compiler_params=params(60),
         cost_estimate=cost(5e9, 1),
         name="one_expert",
     )(pick, rows, win, wout)
@@ -504,9 +411,9 @@
     first_pick = second_pick = back = None
     for j in range(table_ref.shape[0]):
         count = table_ref.shape[1] * CAP
-        slot = lax.broadcasted_iota(jnp.int32, (1, count), 1) + j * count
-        hot_one = (aux[:, 0:1] == slot).astype(NARROW)
-        hot_two = (aux[:, 1:2] == slot).astype(NARROW)
+        slot = lax.broadcasted_iota(jnp.int32, (1, count), 1).astype(WIDE) + float(j * count)
+        hot_one = (aux[:, 0:1] == slot).astype(WIDE).astype(NARROW)
+        hot_two = (aux[:, 1:2] == slot).astype(WIDE).astype(NARROW)
         rows = table_ref[j].reshape(count, 2 * D)
         one = nn(hot_one, rows[:, 0:D])
         two = nn(hot_two, rows[:, 0:D])
@@ -515,8 +422,8 @@
         second_pick = two if second_pick is None else second_pick + two
         back = both if back is None else back + both
     lane = lax.broadcasted_iota(jnp.int32, (1, 128), 1)
-    first_hit = (aux[:, 2:3] == lane).astype(WIDE)
-    second_hit = (aux[:, 3:4] == lane).astype(WIDE)
+    first_hit = (aux[:, 2:3] == lane.astype(WIDE)).astype(WIDE)
+    second_hit = (aux[:, 3:4] == lane.astype(WIDE)).astype(WIDE)
     gate_one = jnp.sum(prob * first_hit, -1, keepdims=True)
     gate_two = jnp.sum(prob * second_hit, -1, keepdims=True)
     put_rows(y_ref, step, ib, second + (gate_one * first_pick + gate_two * second_pick))
@@ -576,7 +483,7 @@
             pltpu.VMEM((8, D), WIDE),
             pltpu.VMEM((D, 4 * D), WIDE),
         ],
-        compiler_params=params(56),
+        compiler_params=params(60),
         cost_estimate=cost(1e6, 1),
         name="expert_block_backward",
     )(gains, w1, wr, mid, second, cot, prob, aux, qkv, mixed, tables)
@@ -677,7 +584,7 @@
             pltpu.VMEM((D, FF), WIDE),
             pltpu.VMEM((FF, D), WIDE),
         ],
-        compiler_params=params(56),
+        compiler_params=params(60),
         cost_estimate=cost(1e6, 1),
         name="dense_block_backward",
     )(gains, w0, win, wout, x, first, grad, qkv, mixed)
@@ -694,10 +601,14 @@
         out[r, :] = (one[r, :].astype(WIDE) + two[r, :].astype(WIDE)).astype(out.dtype)
 
 
-def sum_kernel(nz, groups, mats, slices, *refs):
+def sum_kernel(nz, groups, mats, slices, first, handed, *refs):
     exp_refs, refs = refs[:mats], refs[mats:]
     dense_refs, peak_ref, refs = refs[:3], refs[3], refs[4:]
+    if handed:
+        _, hand_ref, refs = refs[0], refs[1], refs[2:]
     exp_out, dense_outs, peak_out, refs = refs[0], refs[1:4], refs[4], refs[5:]
+    if handed:
+        hand_buf, hand_sem, refs = refs[-2], refs[-1], refs[:-2]
     own, up, down, refs = refs[0], refs[1], refs[2], refs[3:]
     land, refs = refs[:4], refs[4:]
     dense_own, refs = refs[:4], refs[4:]
@@ -765,6 +676,25 @@
             device_id_type=MESH_ID,
         )
 
+    def hand():
+        return pltpu.make_async_remote_copy(
+            src_ref=hand_buf,
+            dst_ref=exp_out.at[pl.ds(first - handed, handed), core],
+            send_sem=hand_sem.at[0],
+            recv_sem=hand_sem.at[1],
+            device_id=sibling,
+            device_id_type=MESH_ID,
+        )
+
+    if handed:
+        arrived = pltpu.make_async_copy(hand_ref, hand_buf, hand_sem.at[2])
+        arrived.start()
+        arrived.wait()
+        handed_here = pltpu.make_async_copy(
+            hand_buf, exp_out.at[pl.ds(first - handed, handed), core], hand_sem.at[2]
+        )
+        handed_here.start()
+        hand().start()
     for n in (3, 1, 0, 2):
         for d in range(1, members):
             scatter(n, d).start()
@@ -860,7 +790,7 @@
 
     def results(t):
         if t < chunks:
-            return exp_out.at[t, core]
+            return exp_out.at[first + t, core]
         n = t - chunks
         if n == 3:
             return peak_out
@@ -941,13 +871,16 @@
     for n in range(4):
         for d in range(1, members):
             scatter(n, d).wait_send()
+    if handed:
+        hand().wait()
+        handed_here.wait()
     for t in range(items):
         keep_result(t).wait()
         if t < items - 1:
             to_sibling(t).wait()
 
 
-def sum_all(mats, dense, peaks, nz, groups):
+def sum_all(mats, dense, peaks, early, handed, nz, groups):
     slices = mats[0].shape[0]
     chunks = len(mats) * slices
     members = CORES * groups
@@ -963,12 +896,15 @@
         ]
 
     dma = pltpu.SemaphoreType.DMA
+    extra = [] if handed is None else [early, handed]
+    count = handed.shape[0] if extra else 0
+    first = early.shape[0] - chunks if extra else 0
     return pl.pallas_call(
-        partial(sum_kernel, nz, groups, len(mats), slices),
-        in_specs=[any_space] * (len(mats) + 3) + [vmem],
+        partial(sum_kernel, nz, groups, len(mats), slices, first, count),
+        in_specs=[any_space] * (len(mats) + 3) + [vmem] + [any_space] * len(extra),
         out_specs=[any_space] * 4 + [vmem],
         out_shape=[
-            sds((chunks, CORES, BLOCK, BLOCK), NARROW),
+            sds((first + chunks, CORES, BLOCK, BLOCK), NARROW),
             *[sds((CORES * r, c), NARROW) for r, c in pieces],
             sds(peaks.shape, WIDE),
         ],
@@ -983,15 +919,18 @@
             *[dma((items,)) for _ in range(8)],
             dma((4, members)),
             dma((4, members)),
+            *([pltpu.VMEM(handed.shape, NARROW), dma((3,))] if extra else []),
         ],
         compiler_params=pltpu.CompilerParams(
             vmem_limit_bytes=58 * MIB, collective_id=3, has_side_effects=True
         ),
+        input_output_aliases={len(mats) + 4: 0} if extra else {},
         name="sums",
-    )(*mats, *dense, peaks)
+    )(*mats, *dense, peaks, *extra)
 
 
 SUMMED = 12
+LAGS = (2, 4, 6)
 BESIDE = 8
 
 
@@ -1225,25 +1164,25 @@
     def _():
         send_up(tick(s), False).start()
 
-    @at(2, has_outer)
-    def _():
-        t = tick(s - 2)
+    @at(LAGS[0], has_outer)
+    def _():
+        t = tick(s - LAGS[0])
         send_up(t, False).wait_recv()
         add_rows(own.at[t], own.at[t], up.at[t], BLOCK, 16)
         send_up(t, True).start()
 
-    @at(4, has_outer)
-    def _():
-        t = tick(s - 4)
+    @at(LAGS[1], has_outer)
+    def _():
+        t = tick(s - LAGS[1])
         send_out(t).wait_recv()
         add_rows(down.at[t], own.at[t], down.at[t], BLOCK, 16)
         send_out(t).start()
         keep_sum(t).start()
         to_sibling(t).start()
 
-    @at(6, edge)
-    def _():
-        t = tick(s - 6)
+    @at(LAGS[2], edge)
+    def _():
+        t = tick(s - LAGS[2])
         send_out(t).wait_recv()
         keep_sum(t).start()
         to_sibling(t).start()
@@ -1282,12 +1221,12 @@
     block = pltpu.VMEM((SUMMED, BLOCK, BLOCK), NARROW)
     return pl.pallas_call(
         partial(exchange_kernel, nz, groups, mine),
-        grid=(steps + 2,),
+        grid=(max(steps, SUMMED + LAGS[2]),),
         in_specs=[any_space] * 3,
         out_specs=[any_space] * 4,
         out_shape=[
             sds((mine, members, CAP, 2 * D), NARROW),
-            sds((SUMMED, CORES, BLOCK, BLOCK), NARROW),
+            sds((2 * steps, CORES, BLOCK, BLOCK), NARROW),
             sds((BESIDE, BLOCK, BLOCK), NARROW),
             sds((rest, BLOCK, BLOCK), NARROW),
         ],
@@ -1314,101 +1253,95 @@
     )(sent, win, wout)
 
 
-def widen_kernel(counts, core_ref, *refs):
-    in_ref, out_ref = refs[-2:]
-    c, s = pl.program_id(0), pl.program_id(1)
-
-    def put(ref):
-        in_ref[...] = ref[0].astype(WIDE)
-        out_ref[...] = ref[1].astype(WIDE)
-
-    first, at = 0, 0
-    for kind, count in enumerate(counts):
-        if count:
-            here = jnp.logical_and(s >= first, s < first + count)
-            if kind == 1:
-                for ref, mine in ((refs[at], True), (refs[at + 1], False)):
-                    pl.when(jnp.logical_and(here, (c == core_ref[0]) == mine))(partial(put, ref))
-                at += 2
-            else:
-                pl.when(here)(partial(put, refs[at]))
-                at += 1
-        first += count
-
-
-def widen(core, early, own, other, late, mine):
-    block = (None, 2, None, BLOCK, BLOCK)
-    arrays, specs, counts, first = [], [], [], 0
-    for kind, group in enumerate(((early,), (own, other), (late,))):
-        count = 0 if group[0] is None else group[0].shape[0] // 2
-        counts.append(count)
-        if count:
-
-            def pair(s, first=first, count=count):
-                return jnp.clip(s - first, 0, count - 1)
-
-            for a in group:
-                if kind == 1:
-                    arrays.append(a.reshape(count, 2, BLOCK, BLOCK))
-                    specs.append(
-                        pl.BlockSpec(
-                            (None, 2, BLOCK, BLOCK),
-                            lambda c, s, _, pair=pair: (pair(s), 0, 0, 0),
-                        )
-                    )
-                else:
-                    arrays.append(a.reshape(count, 2, CORES, BLOCK, BLOCK))
-                    specs.append(
-                        pl.BlockSpec(block, lambda c, s, _, pair=pair: (pair(s), 0, c, 0, 0))
-                    )
-        first += count
+def finish_small(refs):
+    (wide_ref, deep_ref, out_ref, peak_ref, limit_ref, query_ref, key_ref) = refs[:7]
+    (gain_out, q_out, k_out, v_out, o_out, ffn_out, in_out, mlp_out, router_out, cq_out, ck_out) = refs[7:]
+    for n, ref in enumerate((q_out, k_out, v_out, o_out)):
+        c = slice(n * D, (n + 1) * D)
+        ref[0] = wide_ref[:, c].astype(WIDE)
+        ref[1] = deep_ref[:, c].astype(WIDE)
+    in_out[...] = wide_ref[:, 4 * D : 8 * D].astype(WIDE)
+    mlp_out[...] = out_ref[...].astype(WIDE)
+    small = deep_ref[:, 4 * D :].astype(WIDE) + wide_ref[:, 8 * D :].astype(WIDE)
+    router_out[...] = small[:, :EXPERTS]
+    count = small.shape[0]
+    if count < 128:
+        small = jnp.concatenate([small, jnp.zeros((128 - count, 128), WIDE)], 0)
+    turned = jnp.transpose(small)
+    gain_out[...] = turned[EXPERTS : EXPERTS + 2, :count]
+    ffn_out[...] = turned[EXPERTS + 2 : EXPERTS + 4, :count]
+    head = lax.broadcasted_iota(jnp.int32, (HEADS, D), 0)
+    feature = lax.broadcasted_iota(jnp.int32, (HEADS, D), 1)
+    owns = jnp.logical_and(feature >= head * HEAD, feature < (head + 1) * HEAD)
+    for layer in range(2):
+        limit = limit_ref[:, layer : layer + 1]
+        top = peak_ref[:, layer * 64 : layer * 64 + 1]
+        scale = jnp.sqrt(limit / jnp.maximum(top, limit))
+        row = jnp.sum(jnp.where(owns, scale, 0.0), 0, keepdims=True)
+        cq_out[layer] = query_ref[layer] * row
+        ck_out[layer] = key_ref[layer] * row
+
+
+def finish_kernel(blocks_ref, *refs):
+    small, (in_ref, out_ref) = refs[:-2], refs[-2:]
+
+    @pl.when(jnp.logical_and(pl.program_id(0) == 0, pl.program_id(1) == 0))
+    def _():
+        finish_small(small)
+
+    for n in range(FF // BLOCK):
+        r = slice(n * BLOCK, (n + 1) * BLOCK)
+        in_ref[:, r] = blocks_ref[n, 0].astype(WIDE)
+        out_ref[r, :] = blocks_ref[n, 1].astype(WIDE)
+
+
+def finish(blocks, mine, small, outs):
     parts = FF // BLOCK
     return pl.pallas_call(
-        partial(widen_kernel, counts),
-        grid_spec=pltpu.PrefetchScalarGridSpec(
-            num_scalar_prefetch=1,
-            grid=(CORES, mine * parts),
-            in_specs=specs,
-            out_specs=[
-                pl.BlockSpec(
-                    (None, D, BLOCK), lambda c, s, _: (c * mine + s // parts, 0, s % parts)
-                ),
-                pl.BlockSpec(
-                    (None, BLOCK, D), lambda c, s, _: (c * mine + s // parts, s % parts, 0)
-                ),
-            ],
-        ),
-        out_shape=[sds((CORES * mine, D, FF), WIDE), sds((CORES * mine, FF, D), WIDE)],
-        compiler_params=params(56),
-        name="widen",
-    )(core, *arrays)
-
-
-def gather_kernel(groups, q_ref, k_ref, v_ref, o_ref, small_ref, in_ref, out_ref, *refs):
-    w_all, small_all, in_all, out_all, send, recv, pass_send, pass_recv, copy = refs
+        finish_kernel,
+        grid=(CORES, mine),
+        in_specs=[
+            pl.BlockSpec((parts, 2, None, BLOCK, BLOCK), lambda c, j: (j, 0, c, 0, 0)),
+            *[whole(a.shape) for a in small],
+        ],
+        out_specs=[whole(o.shape) for o in outs]
+        + [
+            pl.BlockSpec((None, D, FF), lambda c, j: (c * mine + j, 0, 0)),
+            pl.BlockSpec((None, FF, D), lambda c, j: (c * mine + j, 0, 0)),
+        ],
+        out_shape=[*outs, sds((CORES * mine, D, FF), WIDE), sds((CORES * mine, FF, D), WIDE)],
+        compiler_params=params(60),
+        name="finish",
+    )(blocks.reshape(mine * parts, 2, CORES, BLOCK, BLOCK), *small)
+
+
+def forward_kernel(groups, ib, *refs):
+    q_ref, k_ref, v_ref, o_ref, small_ref, in_ref, out_ref, refs = *refs[:7], refs[7:]
+    token_ref, cot_ref, order_ref, routes_ref, refs = *refs[:4], refs[4:]
+    kept, refs = refs[:4], refs[4:]
+    gain_ref, router_ref, x_out, cot_out, pos_ref, aux_ref, refs = *refs[:6], refs[6:]
+    first_ref, qkv0_ref, mixed0_ref, peak0_ref, mid_ref, refs = *refs[:5], refs[5:]
+    second_ref, qkv1_ref, mixed1_ref, peak1_ref, moe_ref, prob_ref, refs = *refs[:6], refs[6:]
+    w0, win, wout, w1, small_all, state, wide_ref, line_ref, rows_ref, refs = *refs[:9], refs[9:]
+    send, recv, pass_send, pass_recv, copy, rows_sem, kept_sem = refs
+    phase, i = pl.program_id(0), pl.program_id(1)
     z, core, f = lax.axis_index("z"), lax.axis_index("core"), lax.axis_index("fsdp")
-    barrier = pltpu.get_barrier_semaphore()
-    for d in range(1, groups):
-        pl.semaphore_signal(
-            barrier, inc=1, device_id=(z, core, lax.rem(f + d, groups)), device_id_type=MESH_ID
-        )
-    pl.semaphore_signal(barrier, inc=1, device_id=(z, 1 - core, f), device_id_type=MESH_ID)
-    pl.semaphore_wait(barrier, groups)
 
     def rows(count, owner, side):
         half = count // CORES
         return pl.ds(pl.multiple_of(owner * count + side * half, 16), half)
 
     def item(n):
-        if n < 4:
-            ref = (q_ref, k_ref, v_ref, o_ref)[n]
+        if n < 4 or n >= 7:
+            ref = (q_ref, k_ref, v_ref, o_ref)[n % 7]
+            full, layer = (w0, 0) if n < 4 else (w1, 1)
             count = ref.shape[1]
-            cols = pl.ds(n * D, D)
+            cols = pl.ds(n % 7 * D, D)
             return (
-                lambda side: ref.at[0, rows(count, 0, side), :],
-                lambda owner, side: w_all.at[rows(count, owner, side), cols],
+                lambda side: ref.at[layer, rows(count, 0, side), :],
+                lambda owner, side: full.at[rows(count, owner, side), cols],
             )
-        ref, full = ((small_ref, small_all), (in_ref, in_all), (out_ref, out_all))[n - 4]
+        ref, full = ((small_ref, small_all), (in_ref, win), (out_ref, wout))[n - 4]
         count = ref.shape[0]
         return (
             lambda side: ref.at[rows(count, 0, side), :],
@@ -1442,55 +1375,184 @@
         source, place = item(n)
         return pltpu.make_async_copy(source(side), place(f, side), copy.at[n, side])
 
-    count = 7
-    for n in range(count):
+    sets = ((0, 1, 2, 3, 4), (5, 6), (7, 8, 9, 10))
+
+    def begin(stage):
+        for n in sets[stage]:
+            for d in range(1, groups):
+                fetch(n, d).start()
+            for side in range(CORES):
+                keep(n, side).start()
+
+    def arrive(stage):
+        for n in sets[stage]:
+            for d in range(1, groups):
+                fetch(n, d).wait_recv()
+                hand_on(n, d).start()
+
+    def complete(stage):
+        for n in sets[stage]:
+            for side in range(CORES):
+                keep(n, side).wait()
+            for d in range(1, groups):
+                fetch(n, d).wait_send()
+                hand_on(n, d).wait()
+
+    def keepers():
+        return [
+            pltpu.make_async_copy(ref, out, kept_sem.at[n])
+            for n, (ref, out) in enumerate(zip((w0, win, wout, w1), kept))
+        ]
+
+    start = i == 0
+
+    @pl.when(jnp.logical_and(phase == 0, start))
+    def _():
+        barrier = pltpu.get_barrier_semaphore()
         for d in range(1, groups):
-            fetch(n, d).start()
-    for n in range(count):
-        for side in range(CORES):
-            keep(n, side).start()
-    for n in range(count):
-        for d in range(1, groups):
-            fetch(n, d).wait_recv()
-            hand_on(n, d).start()
-    for n in range(count):
-        for side in range(CORES):
-            keep(n, side).wait()
-        for d in range(1, groups):
-            fetch(n, d).wait_send()
-            hand_on(n, d).wait()
-
-
-def gather_dense(query_w, key_w, value_w, output_w, small, mlp_in, mlp_out, groups):
+            there = (z, core, lax.rem(f + d, groups))
+            pl.semaphore_signal(barrier, inc=1, device_id=there, device_id_type=MESH_ID)
+        pl.semaphore_signal(barrier, inc=1, device_id=(z, 1 - core, f), device_id_type=MESH_ID)
+        pl.semaphore_wait(barrier, groups)
+        begin(0)
+        loads = [
+            pltpu.make_async_copy(ref, rows_ref.at[n], rows_sem.at[n])
+            for n, ref in enumerate((token_ref, cot_ref))
+        ]
+        for load in loads:
+            load.start()
+        for n, out in enumerate((x_out, cot_out)):
+            loads[n].wait()
+            pad_images(rows_ref.at[n], wide_ref, out)
+        arrive(0)
+        begin(1)
+        find_places(order_ref, routes_ref, pos_ref, aux_ref, line_ref)
+        complete(0)
+        lane = lax.broadcasted_iota(jnp.int32, (1, 128), 1)
+        small = small_all[...].astype(WIDE)
+        router_ref[...] = jnp.where(lane < EXPERTS, small, 0.0).astype(NARROW)
+        gain_ref[...] = jnp.transpose(small)[EXPERTS : EXPERTS + 8, :]
+
+    @pl.when(jnp.logical_and(phase == 1, start))
+    def _():
+        arrive(1)
+        begin(2)
+        complete(1)
+
+    @pl.when(jnp.logical_and(phase == 2, start))
+    def _():
+        arrive(2)
+        complete(2)
+        for k in keepers():
+            k.start()
+
+    images = pl.ds(i * ib, ib)
+
+    @pl.when(phase == 0)
+    def _():
+        x = x_out[images].astype(WIDE).reshape(ib * SP, D)
+        y = attn_fwd_body(x, gain_ref[0:1, :], w0, qkv0_ref, mixed0_ref, peak0_ref, ib)
+        y = y.reshape(ib, SP, D)
+        first_ref[...] = y
+        state[images] = y
+
+    @pl.when(phase == 1)
+    def _():
+        x = state[images].reshape(ib * SP, D)
+        unit, _ = norm_parts(x)
+        normed = (unit * gain_ref[2:3, :]).astype(NARROW)
+        acc = x
+        for n in range(FF // 512):
+            c = slice(n * 512, (n + 1) * 512)
+            pre = nn(normed, win[:, c])
+            cdf, _ = normal_parts(pre)
+            acc = acc + nn((pre * cdf).astype(NARROW), wout[c, :])
+        y = acc.reshape(ib, SP, D)
+        mid_ref[...] = y
+        state[images] = y
+
+    @pl.when(phase == 2)
+    def _():
+        x = state[images].reshape(ib * SP, D)
+        y = attn_fwd_body(x, gain_ref[1:2, :], w1, qkv1_ref, mixed1_ref, peak1_ref, ib)
+        second_ref[...] = y.reshape(ib, SP, D)
+        unit, _ = norm_parts(y)
+        moe = (unit * gain_ref[3:4, :]).astype(NARROW)
+        moe_ref[...] = moe.reshape(ib, SP, D)
+        lane = lax.broadcasted_iota(jnp.int32, (1, 128), 1)
+        logits = jnp.where(lane < EXPERTS, nn(moe, router_ref[...]), LOWEST)
+        e = jnp.exp(logits - jnp.max(logits, -1, keepdims=True))
+        prob_ref[...] = (e / jnp.sum(e, -1, keepdims=True)).reshape(ib, SP, 128)
+
+    @pl.when(jnp.logical_and(phase == 2, i == pl.num_programs(1) - 1))
+    def _():
+        for k in keepers():
+            k.wait()
+
+
+def forward(weights, tokens, cotangent, routes_rows, groups, held, ib):
     any_space = pl.BlockSpec(memory_space=pl.ANY)
+    vmem = pl.BlockSpec(memory_space=pltpu.VMEM)
     dma = pltpu.SemaphoreType.DMA
+    images = tokens.shape[0] // SEQ
+    padded, pairs = images * SP, images // ib
+    slots = np.arange(EXPERTS, dtype=np.int32)[:, None]
+    order = np.broadcast_to(slot_expert(slots, groups, held), (EXPERTS, 128)).astype(np.int32)
+
+    def of_phase(n, *tail):
+        def place(phase, i):
+            return (jnp.where(phase == n, i, jnp.where(phase < n, 0, pairs - 1)), *[0] * len(tail))
+
+        return pl.BlockSpec((ib, *tail), place)
+
+    tails = (
+        (0, WIDE, SP, D),
+        (0, NARROW, SP, 3 * D),
+        (0, NARROW, SP, D),
+        (0, WIDE, HEADS, 128),
+        (1, WIDE, SP, D),
+        (2, WIDE, SP, D),
+        (2, NARROW, SP, 3 * D),
+        (2, NARROW, SP, D),
+        (2, WIDE, HEADS, 128),
+        (2, NARROW, SP, D),
+        (2, WIDE, SP, 128),
+    )
+    matrices = [(D, 4 * D), (D, FF), (FF, D), (D, 4 * D)]
     return pl.pallas_call(
-        partial(gather_kernel, groups),
-        in_specs=[any_space] * 7,
-        out_specs=[any_space] * 4,
+        partial(forward_kernel, groups, ib),
+        grid=(3, pairs),
+        in_specs=[any_space] * 9 + [vmem] * 2,
+        out_specs=[any_space] * 4
+        + [vmem] * 6
+        + [of_phase(n, *tail) for n, _, *tail in tails],
         out_shape=[
-            sds((D, 4 * D), NARROW),
+            *[sds(m, NARROW) for m in matrices],
+            sds((8, D), WIDE),
             sds((D, 128), NARROW),
-            sds((D, FF), NARROW),
-            sds((FF, D), NARROW),
+            sds((images, SP, D), NARROW),
+            sds((images, SP, D), NARROW),
+            sds((EXPERTS, padded), WIDE),
+            sds((padded, 128), WIDE),
+            *[sds((images, *tail), dtype) for _, dtype, *tail in tails],
         ],
         scratch_shapes=[
-            *[dma((7, groups)) for _ in range(4)],
-            dma((7, CORES)),
+            *[pltpu.VMEM(m, NARROW) for m in matrices],
+            pltpu.VMEM((D, 128), NARROW),
+            pltpu.VMEM((images, SP, D), WIDE),
+            pltpu.VMEM((-(-(tokens.shape[0] + SP) // 16) * 16, D), WIDE),
+            pltpu.VMEM((128, padded), WIDE),
+            pltpu.VMEM((2, *tokens.shape), NARROW),
+            *[dma((11, groups)) for _ in range(4)],
+            dma((11, CORES)),
+            dma((2,)),
+            dma((4,)),
         ],
         compiler_params=pltpu.CompilerParams(
-            vmem_limit_bytes=8 * MIB, collective_id=5, has_side_effects=True
+            vmem_limit_bytes=60 * MIB, collective_id=5, has_side_effects=True
         ),
-        name="gather_weights",
-    )(query_w, key_w, value_w, output_w, small, mlp_in, mlp_out)
-
-
-def gather(x):
-    return lax.all_gather(x, "fsdp", axis=0, tiled=True)
-
-
-def images_of(x, images):
-    return jnp.pad(x.reshape(images, SEQ, x.shape[-1]), ((0, 0), (0, SP - SEQ), (0, 0)))
+        name="forward",
+    )(*weights, tokens, cotangent, jnp.asarray(order), routes_rows)
 
 
 def local(
@@ -1529,49 +1591,29 @@
         ],
         1,
     )
-    w0, w_small, win, wout = gather_dense(
-        query_w, key_w, value_w, output_w, small, mlp_in, mlp_out, groups
+    routes_rows = jnp.pad(
+        jnp.transpose(routes).reshape(2, images, SEQ),
+        ((0, 6), (0, 0), (0, SP - SEQ)),
+        constant_values=-1,
+    ).reshape(8, -1)
+    w0, win, wout, w1, gains, wr, x, cot, pos, aux, *states = forward(
+        (query_w, key_w, value_w, output_w, small, mlp_in, mlp_out),
+        tokens,
+        cotangent,
+        routes_rows,
+        groups,
+        held,
+        ib,
     )
-    w1 = gather(jnp.concatenate([query_w[1], key_w[1], value_w[1], output_w[1]], 1))
-    wr = jnp.where(jnp.arange(128)[None, :] < EXPERTS, w_small, 0)
-    gains = jnp.pad(
-        jnp.transpose(w_small[:, EXPERTS : EXPERTS + 4]).astype(WIDE), ((0, 4), (0, 0))
-    )
-
-    x = images_of(tokens, images)
-    cot = images_of(cotangent, images)
-    routes_image = jnp.pad(
-        routes.reshape(images, SEQ, 2), ((0, 0), (0, SP - SEQ), (0, 0)), constant_values=-1
-    )
-    routes_rows = jnp.pad(
-        jnp.transpose(routes_image.reshape(-1, 2)), ((0, 6), (0, 0)), constant_values=-1
-    )
-    slot = jnp.arange(EXPERTS, dtype=jnp.int32)
-    place_there, owner = slot // owners, slot % owners
-    order = (owner % groups) * held + (owner // groups) * mine + place_there
-    order = jnp.broadcast_to(order[:, None], (EXPERTS, 128))
-    pos, target = places(order, routes_rows)
-    aux = jnp.pad(
-        jnp.concatenate(
-            [
-                jnp.transpose(target[0:2]).astype(jnp.int32).reshape(images, SP, 2),
-                routes_image,
-            ],
-            -1,
-        ),
-        ((0, 0), (0, 0), (0, 124)),
-        constant_values=-1,
-    )
-
-    first, qkv0, mixed0, peak0 = dense_attn(x, gains, w0, images, ib)
-    mid = ffn(first, gains, win, wout, images, ib)
-    second, qkv1, mixed1, peak1, moe, prob = expert_attn(mid, gains, w1, wr, images, ib)
+    first, qkv0, mixed0, peak0, mid, second, qkv1, mixed1, peak1, moe, prob = states
+    aux = aux.reshape(images, SP, 128)
+
     sent = dispatch(
-        pos, order, moe.reshape(-1, D), cot.reshape(-1, D), prob.reshape(-1, 128)
+        pos, moe.reshape(-1, D), cot.reshape(-1, D), prob.reshape(-1, 128), groups, held
     ).reshape(mine, owners, 2 * CAP, D)
 
     nz = lax.axis_size("z")
-    early = own = other = None
+    early = own = None
     if nz == 4 and owners == 8 and mine == 4:
         tables, early, own, late = exchange(sent, expert_in, expert_out, nz, groups)
         own = lax.psum(own, "z")
@@ -1598,41 +1640,26 @@
     )
     lane = jnp.arange(128)[None, :]
     peaks = jnp.where(lane < 64, jnp.max(peak0, 0), jnp.max(peak1, 0))
-    late, t1, t0, t_wout, maxima = sum_all([late], [dw1, dw0, d_wout], peaks, nz, groups)
-    if own is not None:
-        own, late = lax.optimization_barrier((own, late))
-        other = lax.ppermute(own, "core", [(0, 1), (1, 0)])
-    expert_in_grad, expert_out_grad = widen(
-        core.astype(jnp.int32).reshape(1), early, own, other, late, mine
+    blocks, t1, t0, t_wout, maxima = sum_all(
+        [late], [dw1, dw0, d_wout], peaks, early, own, nz, groups
     )
-
-    t1, t0 = t1.astype(WIDE), t0.astype(WIDE)
-    t_small = t1[:, 4 * D :] + t0[:, 8 * D :]
-    norm_rows = jnp.transpose(t_small[:, EXPERTS : EXPERTS + 4])
-    maxima = jnp.stack([maxima[:, 0], maxima[:, 64]])
-    factor = clip_threshold / jnp.maximum(maxima, clip_threshold)
-    column_scale = jnp.repeat(jnp.sqrt(factor), HEAD, axis=1)
-
-    def both(n):
-        return jnp.stack([t0[:, n * D : (n + 1) * D], t1[:, n * D : (n + 1) * D]])
-
-    return (
-        y,
-        x_grad,
-        norm_rows[0:2],
-        both(0),
-        both(1),
-        both(2),
-        both(3),
-        norm_rows[2:4],
-        t0[:, 4 * D : 8 * D],
-        t_wout.astype(WIDE),
-        t_small[:, :EXPERTS],
-        expert_in_grad,
-        expert_out_grad,
-        updated_query * column_scale[:, None, :],
-        updated_key * column_scale[:, None, :],
+    small_outs = [
+        sds(attn_norm.shape, WIDE),
+        *[sds(query_w.shape, WIDE)] * 4,
+        sds(ffn_norm.shape, WIDE),
+        sds(mlp_in.shape, WIDE),
+        sds(mlp_out.shape, WIDE),
+        sds(router_w.shape, WIDE),
+        sds(updated_query.shape, WIDE),
+        sds(updated_key.shape, WIDE),
+    ]
+    *grads, clipped_query, clipped_key, expert_in_grad, expert_out_grad = finish(
+        blocks,
+        mine,
+        [t0, t1, t_wout, maxima, jnp.transpose(clip_threshold), updated_query, updated_key],
+        small_outs,
     )
+    return (y, x_grad, *grads, expert_in_grad, expert_out_grad, clipped_query, clipped_key)
 
 
 def solution(mesh):

time: 788 us -> 732 us (0.929)
  Pallas kernels: 727 us -> 687 us
  local copies, waits for them, and re-layouts: 25.5 us -> 6.81 us
  waiting for transfers between devices: 0.08 us -> 12.3 us
  other arithmetic: 11.6 us -> 1.33 us
    pallas_call x9 -> x5, Pallas kernels: 587 us -> 545 us  [the longest x1 207 us: exchange(): pl.pallas_call(partial(exchange_kernel, nz, groups, mine), grid=(max(step...]
    psum x1, waiting for transfers between devices: 0.02 us -> 12.3 us  [local(): own = lax.psum(own, 'z')]
  transfers between devices with their start and end apart: 3 -> 1, of which waited for: 0 -> 1; matrix products, arithmetic and copies ran while one was open for 4% -> 0% of each run, Pallas kernels for 55% -> 20%
where the time goes in v4:
time: 732 us; the launch traced here: 722 us
  Pallas kernels  687 us (94%)
  between operations  14.6 us (2%)
  waiting for transfers between devices  12.3 us (2%)
    pallas_call x1, Pallas kernels, exchange(): pl.pallas_call(partial(exchange_kernel, nz, groups, mine), grid=(max(step...  207 us
    pallas_call x1, Pallas kernels, sum_all(): pl.pallas_call(partial(sum_kernel, nz, groups, len(mats), slices, first,...  198 us
    pallas_call x1, Pallas kernels, forward(): pl.pallas_call(partial(forward_kernel, groups, ib), grid=(3, pairs), in_s...  85 us
    pallas_call x1, Pallas kernels, moe_bwd(): pl.pallas_call(partial(moe_bwd_kernel, ib), grid=(images // ib,), in_spec...  75.1 us
    pallas_call x1, Pallas kernels, dense_bwd(): pl.pallas_call(partial(dense_bwd_kernel, ib), grid=(images // ib,), in_sp...  66.8 us
    pallas_call x1, Pallas kernels, finish(): pl.pallas_call(finish_kernel, grid=(CORES, mine), in_specs=[pl.BlockSpec(...  34.8 us
    pallas_call x1, Pallas kernels, dispatch(): pl.pallas_call(partial(dispatch_kernel, groups, held), grid=(EXPERTS // G...  19.9 us
  transfers between devices with their start and end apart: 1, of which 1 were waited for; matrix products, arithmetic and copies ran while one was open for 0% of the time, Pallas kernels for 20%

profile of v4, /device:TPU:0, one launch (start us, length us, event | category | flops | bytes accessed | tf_op | source)
XLA Modules:
  0.0 722.0 jit_solution(16780288290978237199)
XLA Ops:
  7.2 0.0 all-reduce.3.cloned.1.call-start
  7.2 0.8 reshape.59
  8.0 0.8 copy.34
  8.8 0.8 copy.35
  9.6 0.8 copy.36
  10.4 0.7 reshape.60.refs_10_
  11.1 0.1 pad.8.clone
  11.2 0.7 maximum_maximum_fusion.refs_4_
  11.9 85.0 %forward.1 = (bf16[512,2048]{1,0:T(8,128)(2,1)}, bf16[512,2048]{1,0:T(8,128)(2,1)}, bf16[2048,512]{1,0:T(8,128)(2,1)}, bf16[512,2048]{1,0:T(8,128)(2,1)}, f32[8,...) custom-call(bf16[2,128,512]{2,1,0:T(8,128)(2,1)} %refs_0_.1, ...), custom_call_target="tpu_custom_call" | custom-call | tf_op jit(solution)/shard_map/forward/pallas_call | solution.py:1522
  97.0 19.9 %dispatch.1 = bf16[32,256,512]{2,1,0:T(8,128)(2,1)} custom-call(f32[32,1664]{1,0:T(8,128)} %get-tuple-element.74.pos_ref, bf16[1664,512]{1,0:T(8,128)(2,1)} %bitcast.14, bf16[1664,512]{1,0:T(8,128)(2,1)} %bitcast.12, f32[1664,128]{1,0:T(8,128)} %bitcast.13), custom_call_target="tpu_custom_call" | custom-call | tf_op jit(solution)/shard_map/dispatch/pallas_call | solution.py:217
  116.9 206.9 %experts.1 = (bf16[4,8,128,1024]{3,2,1,0:T(8,128)(2,1)}, bf16[32,2,512,512]{3,2,1,0:T(8,128)(2,1)}, bf16[8,512,512]{2,1,0:T(8,128)(2,1)}, bf16[12,512,512]{2,1,0:T(8,128)(2,1)}) custom-call(bf16[4,8,256,512]{3,2,1,0:T(8,128)(2,1)} %bitcast.11, bf16[8,512,2048]{2,1,0:T(8,128)(2,1)} %refs_1_.3, bf16[8,2048,512]{2,1,0:T(8,128)(2,1)} %refs_2_.3), custom_call_target="tpu_custom_call" | custom-call | tf_op jit(solution)/shard_map/experts/pallas_call | solution.py:1222
  323.8 0.0 copy-start.2
  323.8 0.0 copy-start.1
  323.8 0.0 copy-start
  323.8 0.0 all-reduce.3.cloned.1.call-update
  323.9 0.6 copy-done.2
  324.5 0.7 copy.37
  325.2 75.1 %expert_block_backward.1 = (f32[1576,512]{1,0:T(8,128)}, f32[8,208,512]{2,1,0:T(8,128)}, bf16[512,2176]{1,0:T(8,128)(2,1)}) custom-call(f32[8,512]{1,0:T(8,128)} %get-tuple-element.64.g_ref, bf16[512,2048]{1,0:T(8,128)(2,1)} %get-tuple-element.65.w_ref, bf16[512,128]{1,0:T(8,128)(2,1)} %get-tuple-element.66.wr_ref, ...), custom_call_target="tpu_custom_call" | custom-call | flops 1000000 | bytes 1 | tf_op jit(solution)/shard_map/expert_block_backward/pallas_call | solution.py:455
  400.3 66.8 %dense_block_backward.1 = (f32[1576,512]{1,0:T(8,128)}, bf16[512,4224]{1,0:T(8,128)(2,1)}, bf16[2048,512]{1,0:T(8,128)(2,1)}) custom-call(f32[8,512]{1,0:T(8,128)} %get-tuple-element.64.g_ref, bf16[512,2048]{1,0:T(8,128)(2,1)} %get-tuple-element.78.w_ref, bf16[512,2048]{1,0:T(8,128)(2,1)} %get-tuple-element.79.win_ref, ...), custom_call_target="tpu_custom_call" | custom-call | flops 1000000 | bytes 1 | tf_op jit(solution)/shard_map/dense_block_backward/pallas_call | solution.py:557
  467.1 0.6 broadcast_select_fusion.refs_4_
  467.7 12.3 %all-reduce.3.cloned.1.call-done.refs_6_ = bf16[8,512,512]{2,1,0:T(8,128)(2,1)} async-done(((bf16[8,512,512]{2,1,0:T(8,128)(2,1)}), bf16[8,512,512]{2,1,0:T(8,128)(2,1)}) %all-reduce.3.cloned.1.call-update) | async-done | bytes 4194320 | tf_op jit(solution)/shard_map/psum | solution.py:1619
  480.0 198.4 %sums.1 = (bf16[32,2,512,512]{3,2,1,0:T(8,128)(2,1)}, bf16[128,2176]{1,0:T(8,128)(2,1)}, bf16[128,4224]{1,0:T(8,128)(2,1)}, bf16[512,512]{1,0:T(8,128)(2,1)}, f32[8,128]{1,0:T(8,128)}) custom-call(bf16[12,512,512]{2,1,0:T(8,128)(2,1)} %get-tuple-element.87.refs_0_, bf16[512,2176]{1,0:T(8,128)(2,1)} %get-tuple-element.88.refs_1_, ...), custom_call_target="tpu_custom_call", output_to_operand_aliasing={{0}: (5, {})} | custom-call | tf_op jit(solution)/shard_map/sums/pallas_call | solution.py:902
  678.4 34.8 %finish.1 = (f32[2,128]{1,0:T(2,128)}, f32[2,128,512]{2,1,0:T(8,128)}, f32[2,128,512]{2,1,0:T(8,128)}, f32[2,128,512]{2,1,0:T(8,128)}, f32[2,128,512]{2,1,0:T(8,...) custom-call(bf16[16,2,2,512,512]{4,3,2,1,0:T(8,128)(2,1)} %bitcast.1, ...), custom_call_target="tpu_custom_call" | custom-call | tf_op jit(solution)/shard_map/finish/pallas_call | solution.py:1300
  713.2 1.5 copy.38
  (7 shorter events, 0.0 us)
Async XLA Ops:
  7.2 472.8 %all-reduce.3.cloned.1.call-start = ((), (), s32[]{:S(2)}) async-start(), calls=%async_computation | async-start | bytes 8388608 | tf_op jit(solution)/shard_map/psum | solution.py:1619
  323.8 0.7 copy-start.2
  323.8 1.3 copy-start.1
  323.8 1.3 copy-start
Sparse Core Ops, SparseCore 0:
  324.0 155.9 all-reduce.2

commit v5 on v4

--- a/solution.py
+++ b/solution.py
@@ -591,6 +591,8 @@
 
 
 BLOCK = 512
+CUTS = 2
+AHEAD = 3
 MESH_ID = pl.DeviceIdType.MESH
 
 
@@ -654,8 +656,11 @@
     def _():
         pl.semaphore_wait(barrier, members)
 
-    chunks = mats * slices
+    chunks = mats * slices * CUTS
     items = chunks + 4
+
+    def cut_rows(t):
+        return pl.ds(t % CUTS * (BLOCK // CUTS), BLOCK // CUTS)
 
     def piece(n, ref, there):
         if n == 3:
@@ -707,8 +712,13 @@
     for k in keep:
         k.start()
 
+    def source_at_edge(t):
+        if t >= chunks:
+            return dense_own[t - chunks]
+        return exp_refs[t // CUTS // slices].at[t // CUTS % slices, cut_rows(t), :]
+
     def load(t):
-        return pltpu.make_async_copy(exp_refs[t // slices].at[t % slices], own.at[t], own_sem.at[t])
+        return pltpu.make_async_copy(source_at_edge(t), own.at[t], own_sem.at[t])
 
     @pl.when(has_outer)
     def _():
@@ -731,9 +741,6 @@
             device_id=(inner, core, f),
             device_id_type=MESH_ID,
         )
-
-    def source_at_edge(t):
-        return exp_refs[t // slices].at[t % slices] if t < chunks else bufs(t)[0]
 
     def join(t, out, one, two):
         if t == items - 1:
@@ -790,7 +797,7 @@
 
     def results(t):
         if t < chunks:
-            return exp_out.at[first + t, core]
+            return exp_out.at[first + t // CUTS, core, cut_rows(t), :]
         n = t - chunks
         if n == 3:
             return peak_out
@@ -839,7 +846,7 @@
         if t < items - 1:
             to_sibling(t).start()
 
-    early = min(8, chunks)
+    early = min(11 * CUTS, chunks)
     sequence = [*range(early), *range(items - 1, chunks - 1, -1), *range(early, chunks)]
 
     def run(up, at_edge, lag):
@@ -852,11 +859,11 @@
     @pl.when(edge)
     def _():
         run(
-            lambda i: up_from_edge(sequence[i], sequence[i - 2] if i >= 2 else None),
+            lambda i: up_from_edge(sequence[i], sequence[i - AHEAD] if i >= AHEAD else None),
             True,
-            min(7, items),
-        )
-        for t in sequence[-2:]:
+            min(7 * CUTS, items),
+        )
+        for t in sequence[-AHEAD:]:
             send_up(t, source_at_edge(t), half == 1).wait_send()
 
     if half > 1:
@@ -882,13 +889,14 @@
 
 def sum_all(mats, dense, peaks, early, handed, nz, groups):
     slices = mats[0].shape[0]
-    chunks = len(mats) * slices
+    blocks = len(mats) * slices
+    chunks = blocks * CUTS
     members = CORES * groups
     items = chunks + 4
     any_space = pl.BlockSpec(memory_space=pl.ANY)
     vmem = pl.BlockSpec(memory_space=pltpu.VMEM)
     pieces = [(a.shape[0] // members, a.shape[1]) for a in dense]
-    block = pltpu.VMEM((chunks, BLOCK, BLOCK), NARROW)
+    block = pltpu.VMEM((chunks, BLOCK // CUTS, BLOCK), NARROW)
 
     def four(lead=()):
         return [pltpu.VMEM((*lead, *p), NARROW) for p in pieces] + [
@@ -898,13 +906,13 @@
     dma = pltpu.SemaphoreType.DMA
     extra = [] if handed is None else [early, handed]
     count = handed.shape[0] if extra else 0
-    first = early.shape[0] - chunks if extra else 0
+    first = early.shape[0] - blocks if extra else 0
     return pl.pallas_call(
         partial(sum_kernel, nz, groups, len(mats), slices, first, count),
         in_specs=[any_space] * (len(mats) + 3) + [vmem] + [any_space] * len(extra),
         out_specs=[any_space] * 4 + [vmem],
         out_shape=[
-            sds((first + chunks, CORES, BLOCK, BLOCK), NARROW),
+            sds((first + blocks, CORES, BLOCK, BLOCK), NARROW),
             *[sds((CORES * r, c), NARROW) for r, c in pieces],
             sds(peaks.shape, WIDE),
         ],
@@ -1282,37 +1290,77 @@
         ck_out[layer] = key_ref[layer] * row
 
 
-def finish_kernel(blocks_ref, *refs):
-    small, (in_ref, out_ref) = refs[:-2], refs[-2:]
-
-    @pl.when(jnp.logical_and(pl.program_id(0) == 0, pl.program_id(1) == 0))
-    def _():
-        finish_small(small)
-
-    for n in range(FF // BLOCK):
+PAIRS = 2
+
+
+def widen_blocks(blocks_ref, in_ref, out_ref):
+    for n in range(PAIRS):
         r = slice(n * BLOCK, (n + 1) * BLOCK)
         in_ref[:, r] = blocks_ref[n, 0].astype(WIDE)
         out_ref[r, :] = blocks_ref[n, 1].astype(WIDE)
 
 
-def finish(blocks, mine, small, outs):
-    parts = FF // BLOCK
+def block_specs(mine, first):
+    parts = FF // BLOCK // PAIRS
+    wide = PAIRS * BLOCK
+
+    def place(c, s):
+        return c * mine + (s + first) // parts, (s + first) % parts
+
+    return (
+        pl.BlockSpec((PAIRS, 2, None, BLOCK, BLOCK), lambda c, s: (s + first, 0, c, 0, 0)),
+        [
+            pl.BlockSpec((None, D, wide), lambda c, s: (place(c, s)[0], 0, place(c, s)[1])),
+            pl.BlockSpec((None, wide, D), lambda c, s: (*place(c, s), 0)),
+        ],
+    )
+
+
+def gradient_shapes(mine):
+    return [sds((CORES * mine, D, FF), WIDE), sds((CORES * mine, FF, D), WIDE)]
+
+
+def widen_early(blocks, count, mine):
+    source, places = block_specs(mine, 0)
     return pl.pallas_call(
-        finish_kernel,
-        grid=(CORES, mine),
+        widen_blocks,
+        grid=(CORES, count // 2 // PAIRS),
+        in_specs=[source],
+        out_specs=places,
+        out_shape=gradient_shapes(mine),
+        compiler_params=params(60),
+        name="widen_early",
+    )(blocks.reshape(-1, 2, CORES, BLOCK, BLOCK))
+
+
+def finish_kernel(given, blocks_ref, *refs):
+    small, (in_ref, out_ref) = refs[given:-2], refs[-2:]
+
+    @pl.when(jnp.logical_and(pl.program_id(0) == 0, pl.program_id(1) == 0))
+    def _():
+        finish_small(small)
+
+    widen_blocks(blocks_ref, in_ref, out_ref)
+
+
+def finish(blocks, done, given, mine, small, outs):
+    first = done // 2 // PAIRS
+    source, places = block_specs(mine, first)
+    steps = blocks.shape[0] // 2 // PAIRS - first
+    return pl.pallas_call(
+        partial(finish_kernel, len(given)),
+        grid=(CORES, steps),
         in_specs=[
-            pl.BlockSpec((parts, 2, None, BLOCK, BLOCK), lambda c, j: (j, 0, c, 0, 0)),
+            source,
+            *[pl.BlockSpec(memory_space=pl.ANY)] * len(given),
             *[whole(a.shape) for a in small],
         ],
-        out_specs=[whole(o.shape) for o in outs]
-        + [
-            pl.BlockSpec((None, D, FF), lambda c, j: (c * mine + j, 0, 0)),
-            pl.BlockSpec((None, FF, D), lambda c, j: (c * mine + j, 0, 0)),
-        ],
-        out_shape=[*outs, sds((CORES * mine, D, FF), WIDE), sds((CORES * mine, FF, D), WIDE)],
+        out_specs=[whole(o.shape) for o in outs] + places,
+        out_shape=[*outs, *gradient_shapes(mine)],
+        input_output_aliases={1 + n: len(outs) + n for n in range(len(given))},
         compiler_params=params(60),
         name="finish",
-    )(blocks.reshape(mine * parts, 2, CORES, BLOCK, BLOCK), *small)
+    )(blocks.reshape(-1, 2, CORES, BLOCK, BLOCK), *given, *small)
 
 
 def forward_kernel(groups, ib, *refs):
@@ -1415,6 +1463,7 @@
         pl.semaphore_signal(barrier, inc=1, device_id=(z, 1 - core, f), device_id_type=MESH_ID)
         pl.semaphore_wait(barrier, groups)
         begin(0)
+        begin(1)
         loads = [
             pltpu.make_async_copy(ref, rows_ref.at[n], rows_sem.at[n])
             for n, ref in enumerate((token_ref, cot_ref))
@@ -1425,7 +1474,6 @@
             loads[n].wait()
             pad_images(rows_ref.at[n], wide_ref, out)
         arrive(0)
-        begin(1)
         find_places(order_ref, routes_ref, pos_ref, aux_ref, line_ref)
         complete(0)
         lane = lax.broadcasted_iota(jnp.int32, (1, 128), 1)
@@ -1640,6 +1688,11 @@
     )
     lane = jnp.arange(128)[None, :]
     peaks = jnp.where(lane < 64, jnp.max(peak0, 0), jnp.max(peak1, 0))
+    given = []
+    if early is not None:
+        (early, _, _) = lax.optimization_barrier((early, dw0, d_wout))
+        given = widen_early(early, SUMMED, mine)
+        (late, *given) = lax.optimization_barrier((late, *given))
     blocks, t1, t0, t_wout, maxima = sum_all(
         [late], [dw1, dw0, d_wout], peaks, early, own, nz, groups
     )
@@ -1655,6 +1708,8 @@
     ]
     *grads, clipped_query, clipped_key, expert_in_grad, expert_out_grad = finish(
         blocks,
+        SUMMED if given else 0,
+        given,
         mine,
         [t0, t1, t_wout, maxima, jnp.transpose(clip_threshold), updated_query, updated_key],
         small_outs,

time: 732 us -> 721 us (0.985)
  waiting for transfers between devices: 12.3 us -> 0.02 us
    psum x1, waiting for transfers between devices: 12.3 us -> 0.01 us  [local(): own = lax.psum(own, 'z')]
    pallas_call x1 -> x2, Pallas kernels: 34.8 us -> 39.5 us  [the longest x1 25.6 us: finish(): pl.pallas_call(partial(finish_kernel, len(given)), grid=(CORES, steps), i...]
  transfers between devices with their start and end apart: 1 -> 1, of which waited for: 1 -> 0; matrix products, arithmetic and copies ran while one was open for 0% -> 0% of each run, Pallas kernels for 20% -> 22%
where the time goes in v5:
time: 721 us; the launch traced here: 712 us
  Pallas kernels  689 us (96%)
  between operations  14.6 us (2%)
    pallas_call x1, Pallas kernels, exchange(): pl.pallas_call(partial(exchange_kernel, nz, groups, mine), grid=(max(step...  207 us
    pallas_call x1, Pallas kernels, sum_all(): pl.pallas_call(partial(sum_kernel, nz, groups, len(mats), slices, first,...  198 us
    pallas_call x1, Pallas kernels, forward(): pl.pallas_call(partial(forward_kernel, groups, ib), grid=(3, pairs), in_s...  83 us
    pallas_call x1, Pallas kernels, moe_bwd(): pl.pallas_call(partial(moe_bwd_kernel, ib), grid=(images // ib,), in_spec...  75 us
    pallas_call x1, Pallas kernels, dense_bwd(): pl.pallas_call(partial(dense_bwd_kernel, ib), grid=(images // ib,), in_sp...  66.8 us
    pallas_call x1, Pallas kernels, finish(): pl.pallas_call(partial(finish_kernel, len(given)), grid=(CORES, steps), i...  25.6 us
    pallas_call x1, Pallas kernels, dispatch(): pl.pallas_call(partial(dispatch_kernel, groups, held), grid=(EXPERTS // G...  19.9 us
  transfers between devices with their start and end apart: 1, of which 0 were waited for; matrix products, arithmetic and copies ran while one was open for 0% of the time, Pallas kernels for 22%

profile of v5, /device:TPU:0, one launch (start us, length us, event | category | flops | bytes accessed | tf_op | source)
XLA Modules:
  0.0 711.7 jit_solution(14910617019326148339)
XLA Ops:
  7.2 0.0 all-reduce.3.cloned.1.call-start
  7.2 0.8 reshape.62
  8.0 0.8 copy.36
  8.8 0.8 copy.37
  9.6 0.8 copy.38
  10.4 0.7 reshape.63.refs_10_
  11.1 0.1 pad.8.clone
  11.2 0.7 maximum_maximum_fusion.refs_4_
  11.9 83.0 %forward.1 = (bf16[512,2048]{1,0:T(8,128)(2,1)}, bf16[512,2048]{1,0:T(8,128)(2,1)}, bf16[2048,512]{1,0:T(8,128)(2,1)}, bf16[512,2048]{1,0:T(8,128)(2,1)}, f32[8,...) custom-call(bf16[2,128,512]{2,1,0:T(8,128)(2,1)} %refs_0_.1, ...), custom_call_target="tpu_custom_call" | custom-call | tf_op jit(solution)/shard_map/forward/pallas_call | solution.py:1570
  95.0 19.9 %dispatch.1 = bf16[32,256,512]{2,1,0:T(8,128)(2,1)} custom-call(f32[32,1664]{1,0:T(8,128)} %get-tuple-element.80.pos_ref, bf16[1664,512]{1,0:T(8,128)(2,1)} %bitcast.16, bf16[1664,512]{1,0:T(8,128)(2,1)} %bitcast.14, f32[1664,128]{1,0:T(8,128)} %bitcast.15), custom_call_target="tpu_custom_call" | custom-call | tf_op jit(solution)/shard_map/dispatch/pallas_call | solution.py:217
  114.9 206.9 %experts.1 = (bf16[4,8,128,1024]{3,2,1,0:T(8,128)(2,1)}, bf16[32,2,512,512]{3,2,1,0:T(8,128)(2,1)}, bf16[8,512,512]{2,1,0:T(8,128)(2,1)}, bf16[12,512,512]{2,1,0:T(8,128)(2,1)}) custom-call(bf16[4,8,256,512]{3,2,1,0:T(8,128)(2,1)} %bitcast.13, bf16[8,512,2048]{2,1,0:T(8,128)(2,1)} %refs_1_.3, bf16[8,2048,512]{2,1,0:T(8,128)(2,1)} %refs_2_.3), custom_call_target="tpu_custom_call" | custom-call | tf_op jit(solution)/shard_map/experts/pallas_call | solution.py:1230
  321.7 0.0 copy-start.2
  321.7 0.0 copy-start.1
  321.8 0.0 copy-start
  321.8 0.0 all-reduce.3.cloned.1.call-update
  321.8 0.6 copy-done.2
  322.4 0.7 copy.39
  323.1 75.0 %expert_block_backward.1 = (f32[1576,512]{1,0:T(8,128)}, f32[8,208,512]{2,1,0:T(8,128)}, bf16[512,2176]{1,0:T(8,128)(2,1)}) custom-call(f32[8,512]{1,0:T(8,128)} %get-tuple-element.70.g_ref, bf16[512,2048]{1,0:T(8,128)(2,1)} %get-tuple-element.71.w_ref, bf16[512,128]{1,0:T(8,128)(2,1)} %get-tuple-element.72.wr_ref, ...), custom_call_target="tpu_custom_call" | custom-call | flops 1000000 | bytes 1 | tf_op jit(solution)/shard_map/expert_block_backward/pallas_call | solution.py:455
  398.2 66.8 %dense_block_backward.1 = (f32[1576,512]{1,0:T(8,128)}, bf16[512,4224]{1,0:T(8,128)(2,1)}, bf16[2048,512]{1,0:T(8,128)(2,1)}) custom-call(f32[8,512]{1,0:T(8,128)} %get-tuple-element.70.g_ref, bf16[512,2048]{1,0:T(8,128)(2,1)} %get-tuple-element.84.w_ref, bf16[512,2048]{1,0:T(8,128)(2,1)} %get-tuple-element.85.win_ref, ...), custom_call_target="tpu_custom_call" | custom-call | flops 1000000 | bytes 1 | tf_op jit(solution)/shard_map/dense_block_backward/pallas_call | solution.py:557
  465.0 13.9 %widen_early.1 = (f32[8,512,2048]{2,1,0:T(8,128)}, f32[8,2048,512]{2,1,0:T(8,128)}) custom-call(bf16[16,2,2,512,512]{4,3,2,1,0:T(8,128)(2,1)} %bitcast.11), custom_call_target="tpu_custom_call" | custom-call | tf_op jit(solution)/shard_map/widen_early/pallas_call | solution.py:1325
  478.8 0.6 broadcast_select_fusion.refs_4_
  479.4 197.8 %sums.1 = (bf16[32,2,512,512]{3,2,1,0:T(8,128)(2,1)}, bf16[128,2176]{1,0:T(8,128)(2,1)}, bf16[128,4224]{1,0:T(8,128)(2,1)}, bf16[512,512]{1,0:T(8,128)(2,1)}, f32[8,128]{1,0:T(8,128)}) custom-call(bf16[12,512,512]{2,1,0:T(8,128)(2,1)} %get-tuple-element.100.refs_0_, bf16[512,2176]{1,0:T(8,128)(2,1)} %get-tuple-element.101.refs_1_, ...), custom_call_target="tpu_custom_call", output_to_operand_aliasing={{0}: (5, {})} | custom-call | tf_op jit(solution)/shard_map/sums/pallas_call | solution.py:910
  677.2 25.6 %finish.1 = (f32[2,128]{1,0:T(2,128)}, f32[2,128,512]{2,1,0:T(8,128)}, f32[2,128,512]{2,1,0:T(8,128)}, f32[2,128,512]{2,1,0:T(8,128)}, f32[2,128,512]{2,1,0:T(8,...) custom-call(bf16[16,2,2,512,512]{4,3,2,1,0:T(8,128)(2,1)} %bitcast.1, ...), custom_call_target="tpu_custom_call", output_to_operand_aliasing={{11}: (1, {}), {12}: (2, {})} | custom-call | tf_op jit(solution)/shard_map/finish/pallas_call | solution.py:1350
  702.9 1.5 copy.40
  (8 shorter events, 0.0 us)
Async XLA Ops:
  7.2 472.3 %all-reduce.3.cloned.1.call-start = ((), (), s32[]{:S(2)}) async-start(), calls=%async_computation | async-start | bytes 8388608 | tf_op jit(solution)/shard_map/psum | solution.py:1667
  321.7 0.7 copy-start.2
  321.7 1.3 copy-start.1
  321.8 1.3 copy-start
Sparse Core Ops, SparseCore 0:
  321.9 156.9 all-reduce.2

commit v6 on v5

--- a/solution.py
+++ b/solution.py
@@ -187,29 +187,44 @@
     return (owner % groups) * held + (owner // groups) * mine + index // owners
 
 
+def turn_probs(prob_ref, line_ref):
+    for c in range(prob_ref.shape[0] // 128):
+        s = slice(c * 128, (c + 1) * 128)
+        line_ref[:, s] = jnp.transpose(prob_ref[s, :])
+
+
+def make_rows(experts, places, moe, cot, line_ref, outs):
+    slot = lax.broadcasted_iota(jnp.int32, (CAP, 1), 0).astype(WIDE)
+    hot, gates = [], []
+    for expert, place in zip(experts, places):
+        mine = place == slot
+        hot.append(mine.astype(WIDE).astype(NARROW))
+        gate_row = line_ref[pl.ds(expert, 1), :]
+        gates.append(jnp.sum(jnp.where(mine, gate_row, 0.0), -1, keepdims=True))
+    hot = jnp.concatenate(hot, 0)
+    rows = nn(hot, moe).astype(NARROW)
+    grads = nn(hot, cot)
+    for g, (gate, out) in enumerate(zip(gates, outs)):
+        s = slice(g * CAP, (g + 1) * CAP)
+        out[0:CAP, :] = rows[s]
+        out[CAP : 2 * CAP, :] = (gate * grads[s]).astype(NARROW)
+
+
 def dispatch_kernel(groups, held, pos_ref, moe_ref, cot_ref, prob_ref, out_ref, line_ref):
     step = pl.program_id(0)
 
     @pl.when(step == 0)
     def _():
-        for c in range(prob_ref.shape[0] // 128):
-            s = slice(c * 128, (c + 1) * 128)
-            line_ref[:, s] = jnp.transpose(prob_ref[s, :])
-
-    slot = lax.broadcasted_iota(jnp.int32, (CAP, 1), 0).astype(WIDE)
-    hot, gates = [], []
-    for g in range(GROUP):
-        mine = pos_ref[g : g + 1, :] == slot
-        hot.append(mine.astype(WIDE).astype(NARROW))
-        gate_row = line_ref[pl.ds(slot_expert(step * GROUP + g, groups, held), 1), :]
-        gates.append(jnp.sum(jnp.where(mine, gate_row, 0.0), -1, keepdims=True))
-    hot = jnp.concatenate(hot, 0)
-    rows = nn(hot, moe_ref[...]).astype(NARROW)
-    grads = nn(hot, cot_ref[...])
-    for g in range(GROUP):
-        s = slice(g * CAP, (g + 1) * CAP)
-        out_ref[g, 0:CAP, :] = rows[s]
-        out_ref[g, CAP : 2 * CAP, :] = (gates[g] * grads[s]).astype(NARROW)
+        turn_probs(prob_ref, line_ref)
+
+    make_rows(
+        [slot_expert(step * GROUP + g, groups, held) for g in range(GROUP)],
+        [pos_ref[g : g + 1, :] for g in range(GROUP)],
+        moe_ref[...],
+        cot_ref[...],
+        line_ref,
+        [out_ref.at[g] for g in range(GROUP)],
+    )
 
 
 def dispatch(pos, moe, cot, prob, groups, held):
@@ -943,10 +958,12 @@
 
 
 def exchange_kernel(nz, groups, mine, *refs):
-    (sent_ref, win_hbm, wout_hbm, table_out, sum_out, beside_out, rest_out) = refs[:7]
-    (rows, back, res, sgr, w_in, w_out, own, up, down, made) = refs[7:17]
-    (d_send, d_recv, r_send, r_recv, w_sem, made_sem, up_send, up_recv, down_recv) = refs[17:26]
-    (out_send, sib_send, sib_recv, keep_sem) = refs[26:]
+    pos_ref, moe_ref, cot_ref, prob_ref, win_hbm, wout_hbm, refs = *refs[:6], refs[6:]
+    table_out, sum_out, beside_out, rest_out, refs = *refs[:4], refs[4:]
+    sent, line_ref, refs = *refs[:2], refs[2:]
+    (rows, back, res, sgr, w_in, w_out, own, up, down, made) = refs[:10]
+    (d_send, d_recv, r_send, r_recv, w_sem, made_sem, up_send, up_recv, down_recv) = refs[10:19]
+    (out_send, sib_send, sib_recv, keep_sem) = refs[19:]
     s = pl.program_id(0)
     z, core, f = lax.axis_index("z"), lax.axis_index("core"), lax.axis_index("fsdp")
     members = CORES * groups
@@ -967,7 +984,7 @@
     def rows_to(j, d):
         there, device = member(d)
         return pltpu.make_async_remote_copy(
-            src_ref=sent_ref.at[j, there],
+            src_ref=sent.at[j, there],
             dst_ref=rows.at[j, me],
             send_sem=d_send.at[j, d],
             recv_sem=d_recv.at[j, d],
@@ -976,7 +993,18 @@
         )
 
     def rows_here(j):
-        return pltpu.make_async_copy(sent_ref.at[j, me], rows.at[j, me], d_recv.at[j, 0])
+        return pltpu.make_async_copy(sent.at[j, me], rows.at[j, me], d_recv.at[j, 0])
+
+    def prepare(j, others):
+        theirs = [member(d)[0] for d in others]
+        make_rows(
+            [slot_expert(j * members + there, groups, CORES * mine) for there in theirs],
+            [pos_ref[pl.ds(j * members + there, 1), :] for there in theirs],
+            moe_ref[...],
+            cot_ref[...],
+            line_ref,
+            [sent.at[j, there] for there in theirs],
+        )
 
     def send_rows(j):
         for d in range(1, members):
@@ -1026,9 +1054,18 @@
         def _():
             pl.semaphore_wait(barrier, members)
 
-        send_rows(0)
         for w in weights(s):
             w.start()
+        turn_probs(prob_ref, line_ref)
+        for d in range(1, members, 2):
+            others = [d, (d + 1) % members]
+            prepare(0, others)
+            for there in others:
+                if there:
+                    rows_to(0, there).start()
+        rows_here(0).start()
+        for j in range(1, mine):
+            prepare(j, range(members))
 
     for j in range(mine):
 
@@ -1084,9 +1121,15 @@
         j = s // parts
         part = lax.rem(s, parts)
         count = members * CAP
-        slots = rows[j, :, 0:CAP, :].reshape(count, D)
-        grads = rows[j, :, CAP : 2 * CAP, :].reshape(count, D)
-        result, slot_grad, d_in, d_out = expert_math(slots, grads, w_in[slot], w_out[slot])
+        half = members // 2
+        halves = []
+        for h in range(2):
+            side = slice(h * half, (h + 1) * half)
+            slots = rows[j, side, 0:CAP, :].reshape(count // 2, D)
+            grads = rows[j, side, CAP : 2 * CAP, :].reshape(count // 2, D)
+            halves.append(expert_math(slots, grads, w_in[slot], w_out[slot]))
+        result, slot_grad = (jnp.concatenate([halves[0][n], halves[1][n]], 0) for n in range(2))
+        d_in, d_out = (halves[0][n] + halves[1][n] for n in range(2, 4))
 
         @pl.when(part == 0)
         def _():
@@ -1220,8 +1263,9 @@
                 send_out(t).wait_send()
 
 
-def exchange(sent, win, wout, nz, groups):
-    mine, members = sent.shape[0], sent.shape[1]
+def exchange(pos, moe, cot, prob, win, wout, nz, groups):
+    members = CORES * groups
+    mine = win.shape[0] // CORES
     steps = mine * (FF // BLOCK)
     rest = 2 * steps - SUMMED - BESIDE
     any_space = pl.BlockSpec(memory_space=pl.ANY)
@@ -1230,7 +1274,7 @@
     return pl.pallas_call(
         partial(exchange_kernel, nz, groups, mine),
         grid=(max(steps, SUMMED + LAGS[2]),),
-        in_specs=[any_space] * 3,
+        in_specs=[*[whole(a.shape) for a in (pos, moe, cot, prob)], any_space, any_space],
         out_specs=[any_space] * 4,
         out_shape=[
             sds((mine, members, CAP, 2 * D), NARROW),
@@ -1239,6 +1283,8 @@
             sds((rest, BLOCK, BLOCK), NARROW),
         ],
         scratch_shapes=[
+            pltpu.VMEM((mine, members, 2 * CAP, D), NARROW),
+            pltpu.VMEM((128, moe.shape[0]), WIDE),
             pltpu.VMEM((mine, members, 2 * CAP, D), NARROW),
             pltpu.VMEM((2, members, CAP, 2 * D), NARROW),
             pltpu.VMEM((members * CAP, D), WIDE),
@@ -1255,10 +1301,10 @@
             *[dma((SUMMED,)) for _ in range(7)],
         ],
         compiler_params=pltpu.CompilerParams(
-            vmem_limit_bytes=58 * MIB, collective_id=7, has_side_effects=True
+            vmem_limit_bytes=62 * MIB, collective_id=7, has_side_effects=True
         ),
         name="experts",
-    )(sent, win, wout)
+    )(pos, moe, cot, prob, win, wout)
 
 
 def finish_small(refs):
@@ -1656,16 +1702,14 @@
     first, qkv0, mixed0, peak0, mid, second, qkv1, mixed1, peak1, moe, prob = states
     aux = aux.reshape(images, SP, 128)
 
-    sent = dispatch(
-        pos, moe.reshape(-1, D), cot.reshape(-1, D), prob.reshape(-1, 128), groups, held
-    ).reshape(mine, owners, 2 * CAP, D)
-
+    routed = (pos, moe.reshape(-1, D), cot.reshape(-1, D), prob.reshape(-1, 128))
     nz = lax.axis_size("z")
     early = own = None
     if nz == 4 and owners == 8 and mine == 4:
-        tables, early, own, late = exchange(sent, expert_in, expert_out, nz, groups)
+        tables, early, own, late = exchange(*routed, expert_in, expert_out, nz, groups)
         own = lax.psum(own, "z")
     else:
+        sent = dispatch(*routed, groups, held).reshape(mine, owners, 2 * CAP, D)
         tables, blocks = [], []
         for j in range(mine):
             rows = lax.all_to_all(

time: 721 us -> 711 us (0.986)
  Pallas kernels: 689 us -> 669 us
  waiting for transfers between devices: 0.02 us -> 9.34 us
    pallas_call x1 -> x0, Pallas kernels: 19.9 us -> none  [dispatch(): pl.pallas_call(partial(dispatch_kernel, groups, held), grid=(EXPERTS // G...]
    pallas_call x1, Pallas kernels: 207 us -> 220 us  [exchange(): pl.pallas_call(partial(exchange_kernel, nz, groups, mine), grid=(max(step...]
    pallas_call x1, Pallas kernels: 75 us -> 65.1 us  [moe_bwd(): pl.pallas_call(partial(moe_bwd_kernel, ib), grid=(images // ib,), in_spec...]
    psum x1, waiting for transfers between devices: 0.01 us -> 9.32 us  [local(): own = lax.psum(own, 'z')]
  transfers between devices with their start and end apart: 1 -> 1, of which waited for: 0 -> 1; matrix products, arithmetic and copies ran while one was open for 0% -> 0% of each run, Pallas kernels for 22% -> 21%
where the time goes in v6:
time: 711 us; the launch traced here: 701 us
  Pallas kernels  669 us (94%)
  between operations  14.6 us (2%)
  waiting for transfers between devices  9.34 us (1%)
    pallas_call x1, Pallas kernels, exchange(): pl.pallas_call(partial(exchange_kernel, nz, groups, mine), grid=(max(step...  220 us
    pallas_call x1, Pallas kernels, sum_all(): pl.pallas_call(partial(sum_kernel, nz, groups, len(mats), slices, first,...  195 us
    pallas_call x1, Pallas kernels, forward(): pl.pallas_call(partial(forward_kernel, groups, ib), grid=(3, pairs), in_s...  82.8 us
    pallas_call x1, Pallas kernels, dense_bwd(): pl.pallas_call(partial(dense_bwd_kernel, ib), grid=(images // ib,), in_sp...  66.8 us
    pallas_call x1, Pallas kernels, moe_bwd(): pl.pallas_call(partial(moe_bwd_kernel, ib), grid=(images // ib,), in_spec...  65.1 us
    pallas_call x1, Pallas kernels, finish(): pl.pallas_call(partial(finish_kernel, len(given)), grid=(CORES, steps), i...  25.6 us
  transfers between devices with their start and end apart: 1, of which 1 were waited for; matrix products, arithmetic and copies ran while one was open for 0% of the time, Pallas kernels for 21%

profile of v6, /device:TPU:0, one launch (start us, length us, event | category | flops | bytes accessed | tf_op | source)
XLA Modules:
  0.0 701.5 jit_solution(5035040491294908406)
XLA Ops:
  7.2 0.0 all-reduce.3.cloned.1.call-start
  7.2 0.8 reshape.59
  8.0 0.8 copy.36
  8.8 0.8 copy.37
  9.6 0.8 copy.38
  10.4 0.7 reshape.60.refs_10_
  11.1 0.1 pad.8.clone
  11.2 0.7 maximum_maximum_fusion.refs_4_
  11.9 82.8 %forward.1 = (bf16[512,2048]{1,0:T(8,128)(2,1)}, bf16[512,2048]{1,0:T(8,128)(2,1)}, bf16[2048,512]{1,0:T(8,128)(2,1)}, bf16[512,2048]{1,0:T(8,128)(2,1)}, f32[8,...) custom-call(bf16[2,128,512]{2,1,0:T(8,128)(2,1)} %refs_0_.1, ...), custom_call_target="tpu_custom_call" | custom-call | tf_op jit(solution)/shard_map/forward/pallas_call | solution.py:1616
  94.8 220.5 %experts.1 = (bf16[4,8,128,1024]{3,2,1,0:T(8,128)(2,1)}, bf16[32,2,512,512]{3,2,1,0:T(8,128)(2,1)}, bf16[8,512,512]{2,1,0:T(8,128)(2,1)}, bf16[12,512,512]{2,1,0:T(8,128)(2,1)}) custom-call(f32[32,1664]{1,0:T(8,128)} %get-tuple-element.80.refs_0_, bf16[1664,512]{1,0:T(8,128)(2,1)} %bitcast.14, bf16[1664,512]{1,0:T(8,128)(2,1)} %bitcast.12, ...), custom_call_target="tpu_custom_call" | custom-call | tf_op jit(solution)/shard_map/experts/pallas_call | solution.py:1274
  315.2 0.0 copy-start.2
  315.2 0.0 copy-start.1
  315.2 0.0 copy-start
  315.3 0.0 all-reduce.3.cloned.1.call-update
  315.3 0.6 copy-done.2
  315.9 0.7 copy.39
  316.6 65.1 %expert_block_backward.1 = (f32[1576,512]{1,0:T(8,128)}, f32[8,208,512]{2,1,0:T(8,128)}, bf16[512,2176]{1,0:T(8,128)(2,1)}) custom-call(f32[8,512]{1,0:T(8,128)} %get-tuple-element.70.g_ref, bf16[512,2048]{1,0:T(8,128)(2,1)} %get-tuple-element.71.w_ref, bf16[512,128]{1,0:T(8,128)(2,1)} %get-tuple-element.72.wr_ref, ...), custom_call_target="tpu_custom_call" | custom-call | flops 1000000 | bytes 1 | tf_op jit(solution)/shard_map/expert_block_backward/pallas_call | solution.py:470
  381.7 66.8 %dense_block_backward.1 = (f32[1576,512]{1,0:T(8,128)}, bf16[512,4224]{1,0:T(8,128)(2,1)}, bf16[2048,512]{1,0:T(8,128)(2,1)}) custom-call(f32[8,512]{1,0:T(8,128)} %get-tuple-element.70.g_ref, bf16[512,2048]{1,0:T(8,128)(2,1)} %get-tuple-element.84.w_ref, bf16[512,2048]{1,0:T(8,128)(2,1)} %get-tuple-element.85.win_ref, ...), custom_call_target="tpu_custom_call" | custom-call | flops 1000000 | bytes 1 | tf_op jit(solution)/shard_map/dense_block_backward/pallas_call | solution.py:572
  448.5 13.9 %widen_early.1 = (f32[8,512,2048]{2,1,0:T(8,128)}, f32[8,2048,512]{2,1,0:T(8,128)}) custom-call(bf16[16,2,2,512,512]{4,3,2,1,0:T(8,128)(2,1)} %bitcast.10), custom_call_target="tpu_custom_call" | custom-call | tf_op jit(solution)/shard_map/widen_early/pallas_call | solution.py:1371
  462.4 0.6 broadcast_select_fusion.refs_4_
  463.0 9.3 %all-reduce.3.cloned.1.call-done.refs_6_ = bf16[8,512,512]{2,1,0:T(8,128)(2,1)} async-done(((bf16[8,512,512]{2,1,0:T(8,128)(2,1)}), bf16[8,512,512]{2,1,0:T(8,128)(2,1)}) %all-reduce.3.cloned.1.call-update) | async-done | bytes 4194320 | tf_op jit(solution)/shard_map/psum | solution.py:1710
  472.3 194.7 %sums.1 = (bf16[32,2,512,512]{3,2,1,0:T(8,128)(2,1)}, bf16[128,2176]{1,0:T(8,128)(2,1)}, bf16[128,4224]{1,0:T(8,128)(2,1)}, bf16[512,512]{1,0:T(8,128)(2,1)}, f32[8,128]{1,0:T(8,128)}) custom-call(bf16[12,512,512]{2,1,0:T(8,128)(2,1)} %get-tuple-element.100.refs_0_, bf16[512,2176]{1,0:T(8,128)(2,1)} %get-tuple-element.101.refs_1_, ...), custom_call_target="tpu_custom_call", output_to_operand_aliasing={{0}: (5, {})} | custom-call | tf_op jit(solution)/shard_map/sums/pallas_call | solution.py:925
  667.0 25.6 %finish.1 = (f32[2,128]{1,0:T(2,128)}, f32[2,128,512]{2,1,0:T(8,128)}, f32[2,128,512]{2,1,0:T(8,128)}, f32[2,128,512]{2,1,0:T(8,128)}, f32[2,128,512]{2,1,0:T(8,...) custom-call(bf16[16,2,2,512,512]{4,3,2,1,0:T(8,128)(2,1)} %bitcast.1, ...), custom_call_target="tpu_custom_call", output_to_operand_aliasing={{11}: (1, {}), {12}: (2, {})} | custom-call | tf_op jit(solution)/shard_map/finish/pallas_call | solution.py:1396
  692.7 1.5 copy.40
  (7 shorter events, 0.0 us)
Async XLA Ops:
  7.2 465.2 %all-reduce.3.cloned.1.call-start = ((), (), s32[]{:S(2)}) async-start(), calls=%async_computation | async-start | bytes 8388608 | tf_op jit(solution)/shard_map/psum | solution.py:1710
  315.2 0.7 copy-start.2
  315.2 1.3 copy-start.1
  315.2 1.3 copy-start
Sparse Core Ops, SparseCore 0:
  315.4 156.9 all-reduce.2

commit v7 on v6

--- a/solution.py
+++ b/solution.py
@@ -663,6 +663,10 @@
             device_id_type=MESH_ID,
         )
 
+    if handed:
+        arrived = pltpu.make_async_copy(hand_ref, hand_buf, hand_sem.at[2])
+        arrived.start()
+
     @pl.when(has_outer)
     def _():
         pl.semaphore_wait(barrier, members + 1)
@@ -707,8 +711,6 @@
         )
 
     if handed:
-        arrived = pltpu.make_async_copy(hand_ref, hand_buf, hand_sem.at[2])
-        arrived.start()
         arrived.wait()
         handed_here = pltpu.make_async_copy(
             hand_buf, exp_out.at[pl.ds(first - handed, handed), core], hand_sem.at[2]
@@ -1046,6 +1048,11 @@
         for d in range(1, members):
             pl.semaphore_signal(barrier, inc=1, device_id=member(d)[1], device_id_type=MESH_ID)
 
+        for w in weights(s):
+            w.start()
+        turn_probs(prob_ref, line_ref)
+        prepare(0, [1, 2])
+
         @pl.when(has_outer)
         def _():
             pl.semaphore_wait(barrier, members + 1)
@@ -1054,12 +1061,10 @@
         def _():
             pl.semaphore_wait(barrier, members)
 
-        for w in weights(s):
-            w.start()
-        turn_probs(prob_ref, line_ref)
         for d in range(1, members, 2):
             others = [d, (d + 1) % members]
-            prepare(0, others)
+            if d > 1:
+                prepare(0, others)
             for there in others:
                 if there:
                     rows_to(0, there).start()

time: 711 us -> 708 us (level)
  no operation moved by 1% of the time
where the time goes in v7:
time: 708 us; the launch traced here: 698 us
  Pallas kernels  666 us (94%)
  between operations  14.6 us (2%)
  waiting for transfers between devices  9.33 us (1%)
    pallas_call x1, Pallas kernels, exchange(): pl.pallas_call(partial(exchange_kernel, nz, groups, mine), grid=(max(step...  219 us
    pallas_call x1, Pallas kernels, sum_all(): pl.pallas_call(partial(sum_kernel, nz, groups, len(mats), slices, first,...  192 us
    pallas_call x1, Pallas kernels, forward(): pl.pallas_call(partial(forward_kernel, groups, ib), grid=(3, pairs), in_s...  82.8 us
    pallas_call x1, Pallas kernels, dense_bwd(): pl.pallas_call(partial(dense_bwd_kernel, ib), grid=(images // ib,), in_sp...  66.8 us
    pallas_call x1, Pallas kernels, moe_bwd(): pl.pallas_call(partial(moe_bwd_kernel, ib), grid=(images // ib,), in_spec...  65.1 us
    pallas_call x1, Pallas kernels, finish(): pl.pallas_call(partial(finish_kernel, len(given)), grid=(CORES, steps), i...  25.6 us
  transfers between devices with their start and end apart: 1, of which 1 were waited for; matrix products, arithmetic and copies ran while one was open for 0% of the time, Pallas kernels for 21%

profile of v7, /device:TPU:0, one launch (start us, length us, event | category | flops | bytes accessed | tf_op | source)
XLA Modules:
  0.0 698.0 jit_solution(6360990451954970706)
XLA Ops:
  7.2 0.0 all-reduce.3.cloned.1.call-start
  7.2 0.8 reshape.59
  8.0 0.8 copy.36
  8.8 0.8 copy.37
  9.6 0.8 copy.38
  10.4 0.7 reshape.60.refs_10_
  11.1 0.1 pad.8.clone
  11.2 0.7 maximum_maximum_fusion.refs_4_
  11.9 82.8 %forward.1 = (bf16[512,2048]{1,0:T(8,128)(2,1)}, bf16[512,2048]{1,0:T(8,128)(2,1)}, bf16[2048,512]{1,0:T(8,128)(2,1)}, bf16[512,2048]{1,0:T(8,128)(2,1)}, f32[8,...) custom-call(bf16[2,128,512]{2,1,0:T(8,128)(2,1)} %refs_0_.1, ...), custom_call_target="tpu_custom_call" | custom-call | tf_op jit(solution)/shard_map/forward/pallas_call | solution.py:1621
  94.8 219.3 %experts.1 = (bf16[4,8,128,1024]{3,2,1,0:T(8,128)(2,1)}, bf16[32,2,512,512]{3,2,1,0:T(8,128)(2,1)}, bf16[8,512,512]{2,1,0:T(8,128)(2,1)}, bf16[12,512,512]{2,1,0:T(8,128)(2,1)}) custom-call(f32[32,1664]{1,0:T(8,128)} %get-tuple-element.80.refs_0_, bf16[1664,512]{1,0:T(8,128)(2,1)} %bitcast.14, bf16[1664,512]{1,0:T(8,128)(2,1)} %bitcast.12, ...), custom_call_target="tpu_custom_call" | custom-call | tf_op jit(solution)/shard_map/experts/pallas_call | solution.py:1279
  314.0 0.0 copy-start.2
  314.0 0.0 copy-start.1
  314.0 0.0 copy-start
  314.0 0.0 all-reduce.3.cloned.1.call-update
  314.1 0.6 copy-done.2
  314.7 0.7 copy.39
  315.4 65.1 %expert_block_backward.1 = (f32[1576,512]{1,0:T(8,128)}, f32[8,208,512]{2,1,0:T(8,128)}, bf16[512,2176]{1,0:T(8,128)(2,1)}) custom-call(f32[8,512]{1,0:T(8,128)} %get-tuple-element.70.g_ref, bf16[512,2048]{1,0:T(8,128)(2,1)} %get-tuple-element.71.w_ref, bf16[512,128]{1,0:T(8,128)(2,1)} %get-tuple-element.72.wr_ref, ...), custom_call_target="tpu_custom_call" | custom-call | flops 1000000 | bytes 1 | tf_op jit(solution)/shard_map/expert_block_backward/pallas_call | solution.py:470
  380.5 66.8 %dense_block_backward.1 = (f32[1576,512]{1,0:T(8,128)}, bf16[512,4224]{1,0:T(8,128)(2,1)}, bf16[2048,512]{1,0:T(8,128)(2,1)}) custom-call(f32[8,512]{1,0:T(8,128)} %get-tuple-element.70.g_ref, bf16[512,2048]{1,0:T(8,128)(2,1)} %get-tuple-element.84.w_ref, bf16[512,2048]{1,0:T(8,128)(2,1)} %get-tuple-element.85.win_ref, ...), custom_call_target="tpu_custom_call" | custom-call | flops 1000000 | bytes 1 | tf_op jit(solution)/shard_map/dense_block_backward/pallas_call | solution.py:572
  447.3 13.9 %widen_early.1 = (f32[8,512,2048]{2,1,0:T(8,128)}, f32[8,2048,512]{2,1,0:T(8,128)}) custom-call(bf16[16,2,2,512,512]{4,3,2,1,0:T(8,128)(2,1)} %bitcast.10), custom_call_target="tpu_custom_call" | custom-call | tf_op jit(solution)/shard_map/widen_early/pallas_call | solution.py:1376
  461.2 0.6 broadcast_select_fusion.refs_4_
  461.8 9.3 %all-reduce.3.cloned.1.call-done.refs_6_ = bf16[8,512,512]{2,1,0:T(8,128)(2,1)} async-done(((bf16[8,512,512]{2,1,0:T(8,128)(2,1)}), bf16[8,512,512]{2,1,0:T(8,128)(2,1)}) %all-reduce.3.cloned.1.call-update) | async-done | bytes 4194320 | tf_op jit(solution)/shard_map/psum | solution.py:1715
  471.1 192.5 %sums.1 = (bf16[32,2,512,512]{3,2,1,0:T(8,128)(2,1)}, bf16[128,2176]{1,0:T(8,128)(2,1)}, bf16[128,4224]{1,0:T(8,128)(2,1)}, bf16[512,512]{1,0:T(8,128)(2,1)}, f32[8,128]{1,0:T(8,128)}) custom-call(bf16[12,512,512]{2,1,0:T(8,128)(2,1)} %get-tuple-element.100.refs_0_, bf16[512,2176]{1,0:T(8,128)(2,1)} %get-tuple-element.101.refs_1_, ...), custom_call_target="tpu_custom_call", output_to_operand_aliasing={{0}: (5, {})} | custom-call | tf_op jit(solution)/shard_map/sums/pallas_call | solution.py:927
  663.6 25.6 %finish.1 = (f32[2,128]{1,0:T(2,128)}, f32[2,128,512]{2,1,0:T(8,128)}, f32[2,128,512]{2,1,0:T(8,128)}, f32[2,128,512]{2,1,0:T(8,128)}, f32[2,128,512]{2,1,0:T(8,...) custom-call(bf16[16,2,2,512,512]{4,3,2,1,0:T(8,128)(2,1)} %bitcast.1, ...), custom_call_target="tpu_custom_call", output_to_operand_aliasing={{11}: (1, {}), {12}: (2, {})} | custom-call | tf_op jit(solution)/shard_map/finish/pallas_call | solution.py:1401
  689.2 1.5 copy.40
  (7 shorter events, 0.0 us)
Async XLA Ops:
  7.2 463.9 %all-reduce.3.cloned.1.call-start = ((), (), s32[]{:S(2)}) async-start(), calls=%async_computation | async-start | bytes 8388608 | tf_op jit(solution)/shard_map/psum | solution.py:1715
  314.0 0.7 copy-start.2
  314.0 1.3 copy-start.1
  314.0 1.3 copy-start
Sparse Core Ops, SparseCore 0:
  314.2 156.8 all-reduce.2
